TPU v7x, 128 devices: a whole 4x4x4 slice. The times are simulated.
128 devices in a mesh: tm: 16 (over x, y), panel: 8 (over z, core).
Axes of the slice: x: 4, y: 4, z: 4, core: 2. Of those that a mesh axis runs over, the one named last changes fastest.
Arguments:
- transitions: float32 [64, 512, 512], P('tm', 'panel'), may hold values from -1 to 1.1, as said below
- offsets: float32 [64, 512], P('tm', 'panel'), may hold values from -1.2 to 1.2
- noise_cov: float32 [64, 512, 512], P('tm', 'panel'), may hold values from -0.05 to 0.2, as said below
Outputs:
- smoothed_means: float32 [64, 512], P('tm', 'panel')
- smoothed_covs: float32 [64, 512, 512], P('tm', 'panel')
Inputs may be any that keep to these rules, and one draw needn't show every extreme that they name: `transitions`: each row is a rate times a row of a near-identity matrix. `noise_cov`: symmetric.
All inputs are finite; a program needn't handle non-finite values.
Results may differ from a plain program's by a relative error of at most 0.00027.
Values sent between devices are 32-bit elements; how exact they have to be, the bound alone decides.
No kernel may reach another device: no remote copies, remote signals or barrier semaphores. Data moves between devices by JAX's collectives and lax.ppermute only.
A program may use at most 128 MiB of HBM per device.

v0:
```python
import jax
import jax.numpy as jnp
from jax import lax
from jax.sharding import PartitionSpec as P


def prefix(array, axis, combine, identity):
    peers, index = (lax.axis_size(axis), lax.axis_index(axis))
    everything = jax.tree.map(lambda part: lax.all_gather(part, axis), array)
    start = jax.tree.map(
        lambda part, zero: jnp.broadcast_to(jnp.asarray(zero, part.dtype), part.shape),
        array,
        identity,
    )

    def step(k, before):
        at = peers - 1 - k
        reached = at > index
        new = combine(before, jax.tree.map(lambda part: part[at], everything))
        return jax.tree.map(lambda a, b: jnp.where(reached, a, b), new, before)

    return lax.fori_loop(0, peers, step, start)


def product(left, right):
    return jnp.dot(left, right, precision=lax.Precision.HIGHEST, preferred_element_type=jnp.float32)


def pick(stack, index):
    return lax.dynamic_index_in_dim(stack, index, 0, keepdims=False)


def place(stack, value, index):
    return lax.dynamic_update_index_in_dim(stack, value, index, 0)


def per_device(transitions, offsets, noise_cov):
    steps = transitions.shape[0]
    entire_transition_matrix = lax.all_gather(transitions, "panel", axis=1, tiled=True)

    def reduce_step(count, state):
        acc_gain, acc_offset, acc_cov = (state[0], state[1], state[2])
        index = steps - 2 - count
        whole_gain, whole_offset, complete_covariance = (
            lax.all_gather(acc_gain, "panel", axis=0, tiled=True),
            lax.all_gather(acc_offset, "panel", axis=0, tiled=True),
            lax.all_gather(acc_cov, "panel", axis=0, tiled=True),
        )
        rows_gain = pick(transitions, index)
        new_gain = product(rows_gain, whole_gain)
        new_offset = product(rows_gain, whole_offset) + pick(offsets, index)
        new_cov = product(
            product(rows_gain, complete_covariance), pick(entire_transition_matrix, index).T
        ) + pick(noise_cov, index)
        return (new_gain, new_offset, new_cov)

    start = (transitions[steps - 1], offsets[steps - 1], noise_cov[steps - 1])
    reduced = lax.fori_loop(0, steps - 1, reduce_step, start)
    total = (reduced[0], reduced[1], reduced[2])
    whole = (
        lax.all_gather(total[0], "panel", axis=0, tiled=True),
        lax.all_gather(total[1], "panel", axis=0, tiled=True),
        lax.all_gather(total[2], "panel", axis=0, tiled=True),
    )
    width = whole[0].shape[0]
    identity = (
        jnp.eye(width, dtype=jnp.float32),
        jnp.zeros((width,), jnp.float32),
        jnp.zeros((width, width), jnp.float32),
    )

    def join(earlier, later):
        gain_a, offset_a, cov_a = earlier
        gain_b, offset_b, cov_b = later
        return (
            product(gain_b, gain_a),
            product(gain_b, offset_a) + offset_b,
            product(product(gain_b, cov_a), gain_b.T) + cov_b,
        )

    carry = prefix((whole[0], whole[1], whole[2]), "tm", join, identity)
    next_mean, successor_spread_matrix = (carry[1], carry[2])

    def smooth(index, whole_mean, complete_covariance):
        rows_gain = pick(transitions, index)
        mean_rows = product(rows_gain, whole_mean) + pick(offsets, index)
        cov_rows = product(
            product(rows_gain, complete_covariance), pick(entire_transition_matrix, index).T
        ) + pick(noise_cov, index)
        return (mean_rows, cov_rows)

    last_mean, last_cov = smooth(steps - 1, next_mean, successor_spread_matrix)
    means = jnp.zeros(offsets.shape, jnp.float32)
    covs = jnp.zeros(noise_cov.shape, jnp.float32)
    means = place(means, last_mean, steps - 1)
    covs = place(covs, last_cov, steps - 1)

    def back_step(count, state):
        means_now, present_covariances, mean_rows, cov_rows = state
        index = steps - 2 - count
        whole_mean, complete_covariance = (
            lax.all_gather(mean_rows, "panel", axis=0, tiled=True),
            lax.all_gather(cov_rows, "panel", axis=0, tiled=True),
        )
        new_mean, new_cov = smooth(index, whole_mean, complete_covariance)
        means_now = place(means_now, new_mean, index)
        present_covariances = place(present_covariances, new_cov, index)
        return (means_now, present_covariances, new_mean, new_cov)

    result = lax.fori_loop(0, steps - 1, back_step, (means, covs, last_mean, last_cov))
    return (result[0], result[1])


def solution(mesh):
    placed = (P("tm", "panel", None), P("tm", "panel"), P("tm", "panel", None))
    return jax.shard_map(
        per_device,
        mesh=mesh,
        in_specs=placed,
        out_specs=(P("tm", "panel"), P("tm", "panel", None)),
        check_vma=False,
    )
```

profile of v0, /device:TPU:1, one launch (start us, length us, event | category | flops | bytes accessed | tf_op | source)
XLA Modules:
  0.0 736.8 jit_solution(12844740934708944956)
XLA Ops:
  9.6 36.1 %all-gather.13.cloned.1.call-done = f32[4,512,512]{2,1,0:T(8,128)} async-done(((f32[4,64,512]{2,1,0:T(8,128)}), f32[4,512,512]{2,1,0:T(8,128)}) %all-gather.13.cloned.1.call-update) | async-done | bytes 4194320 | tf_op jit(solution)/shard_map/all_gather | solution.py:39
  45.7 161.3 %while.58 = (s32[]{:T(128)}, f32[64,512]{1,0:T(8,128)S(1)}, f32[64]{0:T(128)S(1)}, f32[64,512]{1,0:T(8,128)S(1)}, f32[4,64,512]{2,1,0:T(8,128)}, /*index=5*/f32[...) while((s32[]{:T(128)}, f32[64,512]{1,0:T(8,128)S(1)}, ...), condition=%wide.region_1.2_spmd, body=%wide.region_0.1_spmd.sunk | while | flops 604406336 | bytes 12332683 | solution.py:58
  49.3 12.0 %all-reduce.7 = f32[512]{0:T(512)S(1)} all-reduce(f32[512]{0:T(512)S(1)} %dynamic-update-slice.5), channel_id=1, replica_groups=mesh['tm'=16,'panel'=8] {'panel'}, use_global_device_ids=true, to_apply=%add.2 | all-reduce | flops 512 | bytes 4096 | tf_op jit(solution)/shard_map/while
  62.4 9.4 %all-gather.25.cloned.1.call-done = f32[512,512]{1,0:T(8,128)} async-done(((f32[64,512]{1,0:T(8,128)}), f32[512,512]{1,0:T(8,128)}) %all-gather.25.cloned.1.call-update) | async-done | bytes 1048592 | tf_op jit(solution)/shard_map/while/body/eval_jaxpr/all_gather | solution.py:47
  73.8 2.3 convolution_add_fusion.5
  76.1 21.4 %all-gather.23.cloned.1.call-done = f32[512,512]{1,0:T(8,128)} async-done(((f32[64,512]{1,0:T(8,128)}), f32[512,512]{1,0:T(8,128)}) %all-gather.23.cloned.1.call-update) | async-done | bytes 1048592 | tf_op jit(solution)/shard_map/while/body/eval_jaxpr/all_gather | solution.py:45
  102.9 12.0 %all-reduce.7 = f32[512]{0:T(512)S(1)} all-reduce(f32[512]{0:T(512)S(1)} %dynamic-update-slice.5), channel_id=1, replica_groups=mesh['tm'=16,'panel'=8] {'panel'}, use_global_device_ids=true, to_apply=%add.2 | all-reduce | flops 512 | bytes 4096 | tf_op jit(solution)/shard_map/while
  116.0 9.4 %all-gather.25.cloned.1.call-done = f32[512,512]{1,0:T(8,128)} async-done(((f32[64,512]{1,0:T(8,128)}), f32[512,512]{1,0:T(8,128)}) %all-gather.25.cloned.1.call-update) | async-done | bytes 1048592 | tf_op jit(solution)/shard_map/while/body/eval_jaxpr/all_gather | solution.py:47
  127.4 2.3 convolution_add_fusion.5
  129.8 21.3 %all-gather.23.cloned.1.call-done = f32[512,512]{1,0:T(8,128)} async-done(((f32[64,512]{1,0:T(8,128)}), f32[512,512]{1,0:T(8,128)}) %all-gather.23.cloned.1.call-update) | async-done | bytes 1048592 | tf_op jit(solution)/shard_map/while/body/eval_jaxpr/all_gather | solution.py:45
  156.7 12.0 %all-reduce.7 = f32[512]{0:T(512)S(1)} all-reduce(f32[512]{0:T(512)S(1)} %dynamic-update-slice.5), channel_id=1, replica_groups=mesh['tm'=16,'panel'=8] {'panel'}, use_global_device_ids=true, to_apply=%add.2 | all-reduce | flops 512 | bytes 4096 | tf_op jit(solution)/shard_map/while
  169.7 9.2 %all-gather.25.cloned.1.call-done = f32[512,512]{1,0:T(8,128)} async-done(((f32[64,512]{1,0:T(8,128)}), f32[512,512]{1,0:T(8,128)}) %all-gather.25.cloned.1.call-update) | async-done | bytes 1048592 | tf_op jit(solution)/shard_map/while/body/eval_jaxpr/all_gather | solution.py:47
  181.0 2.3 convolution_add_fusion.5
  183.3 21.6 %all-gather.23.cloned.1.call-done = f32[512,512]{1,0:T(8,128)} async-done(((f32[64,512]{1,0:T(8,128)}), f32[512,512]{1,0:T(8,128)}) %all-gather.23.cloned.1.call-update) | async-done | bytes 1048592 | tf_op jit(solution)/shard_map/while/body/eval_jaxpr/all_gather | solution.py:45
  208.5 25.1 %all-gather.15.cloned.1.call-done = f32[512,512]{1,0:T(8,128)} async-done(((f32[64,512]{1,0:T(8,128)}), f32[512,512]{1,0:T(8,128)}) %all-gather.15.cloned.1.call-update) | async-done | bytes 1048592 | tf_op jit(solution)/shard_map/all_gather | solution.py:61
  233.7 25.1 %all-gather.17.cloned.1.call-done = f32[512,512]{1,0:T(8,128)} async-done(((f32[64,512]{1,0:T(8,128)}), f32[512,512]{1,0:T(8,128)}) %all-gather.17.cloned.1.call-update) | async-done | bytes 1048592 | tf_op jit(solution)/shard_map/all_gather | solution.py:63
  260.4 12.0 %all-reduce.4 = f32[512]{0:T(512)S(1)} all-reduce(f32[512]{0:T(512)S(1)} %dynamic-update-slice.2), channel_id=1, replica_groups=mesh['tm'=16,'panel'=8] {'panel'}, use_global_device_ids=true, to_apply=%add.4 | all-reduce | flops 512 | bytes 4096
  272.4 20.2 %all-gather.3 = f32[16,1,512]{2,1,0:T(1,128)S(1)} all-gather(f32[1,1,512]{2,1,0:T(1,128)S(1)} %bitcast.180), channel_id=3, replica_groups=mesh['tm'=16,'panel'=8] {'tm'}, dimensions={0}, use_global_device_ids=true | all-gather | bytes 34816 | tf_op jit(solution)/shard_map/all_gather | solution.py:9
  292.6 79.1 %all-gather.19.cloned.1.call-done = f32[8192,512]{1,0:T(8,128)} async-done(((f32[512,512]{1,0:T(8,128)}), f32[8192,512]{1,0:T(8,128)}) %all-gather.19.cloned.1.call-update) | async-done | bytes 16777232 | tf_op jit(solution)/shard_map/all_gather | solution.py:9
  371.6 113.1 %all-gather.21.cloned.1.call-done = f32[8192,512]{1,0:T(8,128)} async-done(((f32[512,512]{1,0:T(8,128)}), f32[8192,512]{1,0:T(8,128)}) %all-gather.21.cloned.1.call-update) | async-done | bytes 16777232 | tf_op jit(solution)/shard_map/all_gather | solution.py:9
  484.7 147.7 %while.60 = (s32[]{:T(128)}, f32[512]{0:T(512)S(1)}, f32[512,512]{1,0:T(8,128)S(1)}, s32[]{:T(128)}, f32[16,512,512]{2,1,0:T(8,128)}, /*index=5*/f32[16,512]{1,0...) while((s32[]{:T(128)}, f32[512]{0:T(512)S(1)}, ...), condition=%wide.region_3.4_spmd.clone, body=%wide.region_2.3_spmd.clone.sunk | while | flops 3225421824 | bytes 9459901 | solution.py:22
  484.7 3.2 fusion.110
  487.9 3.8 fusion.111
  494.0 3.1 fusion.110
  497.1 3.8 fusion.111
  503.3 3.1 fusion.110
  506.4 3.8 fusion.111
  512.5 3.1 fusion.110
  515.6 3.8 fusion.111
  521.7 3.1 fusion.110
  524.8 3.8 fusion.111
  530.9 3.1 fusion.110
  534.0 3.8 fusion.111
  540.1 3.1 fusion.110
  543.2 3.8 fusion.111
  549.4 3.1 fusion.110
  552.5 3.8 fusion.111
  558.6 3.1 fusion.110
  561.7 3.9 fusion.111
  567.9 3.1 fusion.110
  571.0 3.8 fusion.111
  577.1 3.1 fusion.110
  580.2 3.8 fusion.111
  586.3 3.1 fusion.110
  589.4 3.8 fusion.111
  595.5 3.1 fusion.110
  598.6 3.8 fusion.111
  604.8 3.1 fusion.110
  607.8 3.8 fusion.111
  614.0 3.1 fusion.110
  617.1 3.8 fusion.111
  623.2 3.1 fusion.110
  626.3 3.8 fusion.111
  634.2 2.4 convolution_add_fusion.3
  636.9 92.5 %while.59 = (s32[]{:T(128)}, f32[4,64]{1,0:T(4,128)S(1)}, f32[4,64,512]{2,1,0:T(8,128)S(1)}, f32[64]{0:T(128)S(1)}, f32[64,512]{1,0:T(8,128)S(1)}, /*index=5*/f3...) while((s32[]{:T(128)}, f32[4,64]{1,0:T(4,128)S(1)}, ...), condition=%wide.region_5.6_spmd, body=%wide.region_4.5_spmd.sunk | while | flops 403079744 | bytes 7090255 | solution.py:110
  639.2 12.6 %all-reduce.8 = f32[512]{0:T(512)S(1)} all-reduce(f32[512]{0:T(512)S(1)} %dynamic-update-slice.6), channel_id=1, replica_groups=mesh['tm'=16,'panel'=8] {'panel'}, use_global_device_ids=true, to_apply=%add.3 | all-reduce | flops 512 | bytes 4096 | tf_op jit(solution)/shard_map/while
  652.0 11.6 %all-gather.27.cloned.1.call-done = f32[512,512]{1,0:T(8,128)} async-done(((f32[64,512]{1,0:T(8,128)}), f32[512,512]{1,0:T(8,128)}) %all-gather.27.cloned.1.call-update) | async-done | bytes 1048592 | tf_op jit(solution)/shard_map/while/body/eval_jaxpr/all_gather | solution.py:103
  665.6 2.3 bitcast_dynamic-update-slice_fusion.2
  670.2 12.0 %all-reduce.8 = f32[512]{0:T(512)S(1)} all-reduce(f32[512]{0:T(512)S(1)} %dynamic-update-slice.6), channel_id=1, replica_groups=mesh['tm'=16,'panel'=8] {'panel'}, use_global_device_ids=true, to_apply=%add.3 | all-reduce | flops 512 | bytes 4096 | tf_op jit(solution)/shard_map/while
  682.5 12.0 %all-gather.27.cloned.1.call-done = f32[512,512]{1,0:T(8,128)} async-done(((f32[64,512]{1,0:T(8,128)}), f32[512,512]{1,0:T(8,128)}) %all-gather.27.cloned.1.call-update) | async-done | bytes 1048592 | tf_op jit(solution)/shard_map/while/body/eval_jaxpr/all_gather | solution.py:103
  696.5 2.3 bitcast_dynamic-update-slice_fusion.2
  701.1 12.0 %all-reduce.8 = f32[512]{0:T(512)S(1)} all-reduce(f32[512]{0:T(512)S(1)} %dynamic-update-slice.6), channel_id=1, replica_groups=mesh['tm'=16,'panel'=8] {'panel'}, use_global_device_ids=true, to_apply=%add.3 | all-reduce | flops 512 | bytes 4096 | tf_op jit(solution)/shard_map/while
  713.3 11.8 %all-gather.27.cloned.1.call-done = f32[512,512]{1,0:T(8,128)} async-done(((f32[64,512]{1,0:T(8,128)}), f32[512,512]{1,0:T(8,128)}) %all-gather.27.cloned.1.call-update) | async-done | bytes 1048592 | tf_op jit(solution)/shard_map/while/body/eval_jaxpr/all_gather | solution.py:103
  727.1 2.3 bitcast_dynamic-update-slice_fusion.2
  (176 shorter events, 79.0 us)
Async XLA Ops:
  7.2 251.7 %copy-start.11 = (u32[128]{0:T(128)S(1)}, u32[128]{0:T(128)}, u32[]{:S(2)}) copy-start(u32[128]{0:T(128)} %constant.208) | copy-start | bytes 1540
  7.2 38.5 %all-gather.13.cloned.1.call-start = ((), (), s32[]{:S(2)}) async-start(), calls=%async_computation | async-start | bytes 4718592 | tf_op jit(solution)/shard_map/all_gather | solution.py:39
  45.7 0.6 copy-start.2
  45.7 0.8 copy-start.4
  45.7 26.0 %all-gather.25.cloned.1.call-start = ((), (), s32[]{:S(2)}) async-start(), calls=%async_computation.6 | async-start | bytes 1179648 | tf_op jit(solution)/shard_map/while/body/eval_jaxpr/all_gather | solution.py:47
  46.4 51.1 %all-gather.23.cloned.1.call-start = ((), (), s32[]{:S(2)}) async-start(), calls=%async_computation.5 | async-start | bytes 1179648 | tf_op jit(solution)/shard_map/while/body/eval_jaxpr/all_gather | solution.py:45
  99.6 0.6 copy-start.2
  99.6 0.7 copy-start.4
  99.6 25.8 %all-gather.25.cloned.1.call-start = ((), (), s32[]{:S(2)}) async-start(), calls=%async_computation.6 | async-start | bytes 1179648 | tf_op jit(solution)/shard_map/while/body/eval_jaxpr/all_gather | solution.py:47
  100.2 50.8 %all-gather.23.cloned.1.call-start = ((), (), s32[]{:S(2)}) async-start(), calls=%async_computation.5 | async-start | bytes 1179648 | tf_op jit(solution)/shard_map/while/body/eval_jaxpr/all_gather | solution.py:45
  153.1 0.6 copy-start.2
  153.2 0.7 copy-start.4
  153.2 25.8 %all-gather.25.cloned.1.call-start = ((), (), s32[]{:S(2)}) async-start(), calls=%async_computation.6 | async-start | bytes 1179648 | tf_op jit(solution)/shard_map/while/body/eval_jaxpr/all_gather | solution.py:47
  153.8 51.1 %all-gather.23.cloned.1.call-start = ((), (), s32[]{:S(2)}) async-start(), calls=%async_computation.5 | async-start | bytes 1179648 | tf_op jit(solution)/shard_map/while/body/eval_jaxpr/all_gather | solution.py:45
  207.0 0.7 copy-start.5
  207.0 0.8 copy-start.3
  207.0 26.6 %all-gather.15.cloned.1.call-start = ((), (), s32[]{:S(2)}) async-start(), calls=%async_computation.1 | async-start | bytes 1179648 | tf_op jit(solution)/shard_map/all_gather | solution.py:61
  207.7 51.1 %all-gather.17.cloned.1.call-start = ((), (), s32[]{:S(2)}) async-start(), calls=%async_computation.2 | async-start | bytes 1179648 | tf_op jit(solution)/shard_map/all_gather | solution.py:63
  208.5 163.1 %all-gather.19.cloned.1.call-start = ((), (), s32[]{:S(2)}) async-start(), calls=%async_computation.3 | async-start | bytes 17825792 | tf_op jit(solution)/shard_map/all_gather | solution.py:9
  233.6 251.1 %all-gather.21.cloned.1.call-start = ((), (), s32[]{:S(2)}) async-start(), calls=%async_computation.4 | async-start | bytes 17825792 | tf_op jit(solution)/shard_map/all_gather | solution.py:9
  484.7 147.7 %copy-start = (f32[4,64,512]{2,1,0:T(8,128)S(1)}, f32[4,64,512]{2,1,0:T(8,128)}, u32[]{:S(2)}) copy-start(f32[4,64,512]{2,1,0:T(8,128)} %get-tuple-element.976) | copy-start | bytes 1572868
  484.7 149.5 %copy-start.6 = (f32[4,64,512]{2,1,0:T(8,128)S(1)}, f32[4,64,512]{2,1,0:T(8,128)}, u32[]{:S(2)}) copy-start(f32[4,64,512]{2,1,0:T(8,128)} %get-tuple-element.993) | copy-start | bytes 1572868
  484.7 151.9 %copy-start.8 = (f32[4,64]{1,0:T(4,128)S(1)}, f32[4,64]{1,0:T(4,128)}, u32[]{:S(2)}) copy-start(f32[4,64]{1,0:T(4,128)} %get-tuple-element.1001) | copy-start | bytes 3076
  484.7 152.2 %copy-start.10 = (u32[128]{0:T(128)S(1)}, u32[128]{0:T(128)}, u32[]{:S(2)}) copy-start(u32[128]{0:T(128)} %constant.258) | copy-start | bytes 1540
  636.9 0.7 copy-start.1
  636.9 26.7 %all-gather.27.cloned.1.call-start = ((), (), s32[]{:S(2)}) async-start(), calls=%async_computation.7 | async-start | bytes 1179648 | tf_op jit(solution)/shard_map/while/body/eval_jaxpr/all_gather | solution.py:103
  667.9 0.7 copy-start.1
  667.9 26.6 %all-gather.27.cloned.1.call-start = ((), (), s32[]{:S(2)}) async-start(), calls=%async_computation.7 | async-start | bytes 1179648 | tf_op jit(solution)/shard_map/while/body/eval_jaxpr/all_gather | solution.py:103
  698.8 0.7 copy-start.1
  698.8 26.3 %all-gather.27.cloned.1.call-start = ((), (), s32[]{:S(2)}) async-start(), calls=%async_computation.7 | async-start | bytes 1179648 | tf_op jit(solution)/shard_map/while/body/eval_jaxpr/all_gather | solution.py:103
  729.5 0.8 copy-start.7
  729.5 0.8 copy-start.9
Sparse Core Ops, SparseCore 0:
  9.7 35.9 all-gather.12
  48.2 23.4 all-gather.24
  74.0 23.4 all-gather.22
  101.8 23.4 all-gather.24
  127.5 23.5 all-gather.22
  155.4 23.4 all-gather.24
  181.2 23.6 all-gather.22
  210.1 23.4 all-gather.14
  235.3 23.4 all-gather.16
  260.8 110.7 all-gather.18
  373.8 110.8 all-gather.20
  639.8 23.7 all-gather.26
  671.1 23.4 all-gather.26
  701.7 23.4 all-gather.26
where the time goes:
time: 739 us; the launch traced here: 737 us
  waiting for transfers between devices  410 us (55%)
  matrix products  186 us (25%)
  blocking collectives  105 us (14%)
  local copies, waits for them, and re-layouts  15.3 us (2%)
  between operations  14.6 us (2%)
    all_gather x2, waiting for transfers between devices, prefix(): everything = jax.tree.map(lambda part: lax.all_gather(part, axis), array)  192 us
    dot_general x72, matrix products, product(): jnp.dot(left, right, precision=lax.Precision.HIGHEST, preferred_element_t...  186 us
    while x6, blocking collectives  72.6 us
    all_gather x3, waiting for transfers between devices, reduce_step(): lax.all_gather(acc_gain, 'panel', axis=0, tiled=True)  64.3 us
    all_gather x1, waiting for transfers between devices, per_device(): lax.all_gather(transitions, 'panel', axis=1, tiled=True)  36.1 us
    all_gather x3, waiting for transfers between devices, back_step(): lax.all_gather(cov_rows, 'panel', axis=0, tiled=True)  35.4 us
    all_gather x3, waiting for transfers between devices, reduce_step(): lax.all_gather(acc_cov, 'panel', axis=0, tiled=True)  27.9 us
    all_gather x1, waiting for transfers between devices, per_device(): lax.all_gather(total[2], 'panel', axis=0, tiled=True)  25.1 us
  transfers between devices with their start and end apart: 14, of which 14 were waited for; matrix products, arithmetic and copies ran while one was open for 4% of the time, Pallas kernels for 0%

commit v1 on v0

v1 whole, which is shorter than its diff:
```python
import functools

import jax
import jax.numpy as jnp
from jax import lax
from jax.experimental import pallas as pl
from jax.experimental.pallas import tpu as pltpu
from jax.sharding import PartitionSpec as P

D = 512
ROWS = 64
HALF = 256
AUG = D + 8
NN = (((1,), (0,)), ((), ()))
NT = (((1,), (1,)), ((), ()))
VMEM = pl.BlockSpec(memory_space=pltpu.VMEM)
SMEM = pl.BlockSpec(memory_space=pltpu.SMEM)
ANY = pl.BlockSpec(memory_space=pl.ANY)


def shape(*dims, dtype=jnp.float32):
    return jax.ShapeDtypeStruct(dims, dtype)


def split(a):
    high = a.astype(jnp.bfloat16)
    return high, (a - high.astype(jnp.float32)).astype(jnp.bfloat16)


def dot(a, b, dims):
    return lax.dot_general(a, b, dims, preferred_element_type=jnp.float32)


def dot3(a, b, dims):
    return dot(a[0], b[0], dims) + (dot(a[0], b[1], dims) + dot(a[1], b[0], dims))


def call(kernel, name, outs, ins, scratch=(), products=4, aliases=None):
    return pl.pallas_call(
        kernel,
        out_shape=outs,
        in_specs=ins,
        out_specs=[VMEM if spec is None else spec for spec in [None] * len(outs)],
        scratch_shapes=list(scratch),
        compiler_params=pltpu.CompilerParams(vmem_limit_bytes=56 << 20),
        cost_estimate=pl.CostEstimate(
            flops=products * 6 * D**3, bytes_accessed=8 << 20, transcendentals=0
        ),
        name=name,
    )


def block_kernel(place, *refs):
    pieces, (e_hi, e_lo, s_hi, s_lo, total, half) = refs[:8], refs[8:]
    z, c = place[0], place[1]
    for core in range(2):
        for shift in range(4):
            panel = 2 * ((z - shift + 4) % 4) + (c if core == 0 else 1 - c)
            rows = pl.ds(pl.multiple_of(panel * ROWS, ROWS), ROWS)
            for k in range(4):
                high, low = split(pieces[core * 4 + shift][k * ROWS : (k + 1) * ROWS, :])
                e_hi[k, rows, :] = high
                e_lo[k, rows, :] = low
    tail = (e_hi[3], e_lo[3])
    for k in (2, 1, 0):
        product = dot3((e_hi[k], e_lo[k]), tail, NN)
        tail = split(product)
        s_hi[k] = tail[0]
        s_lo[k] = tail[1]
    total[...] = product
    half[...] = total[pl.ds(pl.multiple_of(c * HALF, HALF), HALF), :]


def congruence(gain, cov, scratch):
    scratch[:D, :] = dot3(gain, split(cov[:D, :]), NN)
    scratch[D:, :] = cov[D:, :]
    return dot3(split(scratch[...]), gain, NT)


def noise_kernel(place, e_hi, e_lo, *refs):
    pieces, (rows_out, means_out, whole, half, scratch) = refs[:8], refs[8:]
    z, c = place[0], place[1]
    mine = 2 * z + c
    offsets = sum(piece[256:264, :] for piece in pieces)
    row = lax.broadcasted_iota(jnp.int32, (8, D), 0)
    means_out[...] = jnp.zeros((8, D), jnp.float32)
    for k in (3, 2, 1, 0):
        if k == 3:
            whole[...] = jnp.zeros((AUG, D), jnp.float32)
        else:
            whole[...] = congruence((e_hi[k], e_lo[k]), whole[...], scratch)
        for core in range(2):
            for shift in range(4):
                panel = 2 * ((z - shift + 4) % 4) + (c if core == 0 else 1 - c)
                rows = pl.ds(pl.multiple_of(panel * ROWS, ROWS), ROWS)
                whole[rows, :] += pieces[core * 4 + shift][k * ROWS : (k + 1) * ROWS, :]
        offset = jnp.sum(jnp.where(row == k, offsets, 0.0), axis=0, keepdims=True)
        whole[D:, :] += jnp.where(row == 0, offset, 0.0)
        rows_out[k] = whole[pl.ds(pl.multiple_of(mine * ROWS, ROWS), ROWS), :]
        means_out[k : k + 1, :] = whole[D : D + 1, :]
    half[:HALF, :] = whole[pl.ds(pl.multiple_of(c * HALF, HALF), HALF), :]
    half[HALF:, :] = whole[D:, :]


def gains_kernel(place, own, *refs):
    pieces, (a_hi, a_lo, p_hi, p_lo, half, scratch) = refs[:6], refs[6:]
    c, y = place[1], place[2]
    high, low = split(own[...])
    a_hi[y] = high
    a_lo[y] = low
    for core in range(2):
        for shift in (1, 2, 3):
            block = (y - shift + 4) % 4
            rows = pl.ds(pl.multiple_of((c if core == 0 else 1 - c) * HALF, HALF), HALF)
            high, low = split(pieces[core * 3 + shift - 1][...])
            a_hi[block, rows, :] = high
            a_lo[block, rows, :] = low

    @pl.when(y == 3)
    def _():
        same = lax.broadcasted_iota(jnp.int32, (D, D), 0) == lax.broadcasted_iota(jnp.int32, (D, D), 1)
        p_hi[...] = jnp.where(same, 1.0, 0.0).astype(jnp.bfloat16)
        p_lo[...] = jnp.zeros((D, D), jnp.bfloat16)

    tail = (a_hi[3], a_lo[3])
    for block in (2, 1, 0):

        @pl.when(y == block)
        def _():
            p_hi[...] = tail[0]
            p_lo[...] = tail[1]

        product = dot3((a_hi[block], a_lo[block]), tail, NN)
        tail = split(product)
    scratch[...] = product
    half[...] = scratch[pl.ds(pl.multiple_of(c * HALF, HALF), HALF), :]


def covs_kernel(place, a_hi, a_lo, own, *refs):
    pieces, (later, half, covs, scratch, now) = refs[:6], refs[6:]
    c, y = place[1], place[2]
    covs[y] = own[...]
    for core in range(2):
        for shift in (1, 2, 3):
            block = (y - shift + 4) % 4
            rows = pl.ds(pl.multiple_of((c if core == 0 else 1 - c) * HALF, HALF), HALF)
            covs[block, rows, :] = pieces[core * 3 + shift - 1][:HALF, :]
            if core == 0:
                covs[block, D:, :] = pieces[core * 3 + shift - 1][HALF:, :]

    @pl.when(y == 3)
    def _():
        later[...] = jnp.zeros((AUG, D), jnp.float32)

    now[...] = covs[3]
    for block in (2, 1, 0):

        @pl.when(y == block)
        def _():
            later[...] = now[...]

        now[...] = congruence((a_hi[block], a_lo[block]), now[...], scratch) + covs[block]
    half[:HALF, :] = now[pl.ds(pl.multiple_of(c * HALF, HALF), HALF), :]
    half[HALF:, :] = now[D:, :]


def final_kernel(place, e_hi, e_lo, s_hi, s_lo, p_hi, p_lo, later, rows_in, means_in, *refs):
    gains, covs, (out, means, now, scratch, short) = refs[:4], refs[4:10], refs[10:]
    z, c = place[0], place[1]
    mine = pl.ds(pl.multiple_of((2 * z + c) * ROWS, ROWS), ROWS)

    def whole(pair):
        rows = [pl.ds(pl.multiple_of((c if core == 0 else 1 - c) * HALF, HALF), HALF) for core in range(2)]
        return rows

    def load(pair, target):
        for core in range(2):
            rows = pl.ds(pl.multiple_of((c if core == 0 else 1 - c) * HALF, HALF), HALF)
            target[rows, :] = pair[core][:HALF, :]

    def add(pair):
        for core in range(2):
            rows = pl.ds(pl.multiple_of((c if core == 0 else 1 - c) * HALF, HALF), HALF)
            now[rows, :] += pair[core][:HALF, :]
        now[D:, :] += pair[0][HALF:, :]

    now[...] = jnp.zeros((AUG, D), jnp.float32)
    add(covs[4:6])
    for index in (1, 0):
        load(gains[2 * index : 2 * index + 2], scratch)
        now[...] = congruence(split(scratch[:D, :]), now[...], scratch)
        add(covs[2 * index : 2 * index + 2])
    now[...] = congruence((p_hi[...], p_lo[...]), now[...], scratch) + later[...]
    inner = split(now[:D, :])
    means[...] = jnp.zeros((8, D), jnp.float32)
    for k in range(4):
        hi, lo = (s_hi, s_lo) if k < 3 else (e_hi, e_lo)
        short[:ROWS, :] = dot3((hi[k, mine, :], lo[k, mine, :]), inner, NN)
        short[ROWS:, :] = now[D:, :]
        result = dot3(split(short[...]), (hi[k], lo[k]), NT)
        out[k] = result[:ROWS, :] + rows_in[k]
        means[k : k + 1, :] = result[ROWS : ROWS + 1, :] + means_in[k : k + 1, :]


def per_device(transitions, offsets, noise_cov):
    panel, block = lax.axis_index("panel"), lax.axis_index("tm")
    place = jnp.stack([panel // 2, panel % 2, block % 4, block // 4]).astype(jnp.int32)

    def along_z(value, step):
        return lax.ppermute(
            value, "panel", [(2 * z + c, 2 * ((z + step) % 4) + c) for z in range(4) for c in range(2)]
        )

    def other_core(value):
        return lax.ppermute(value, "panel", [(2 * z + c, 2 * z + 1 - c) for z in range(4) for c in range(2)])

    def along_y(value, step):
        return lax.ppermute(
            value, "tm", [(4 * x + y, 4 * x + (y + step) % 4) for x in range(4) for y in range(4)]
        )

    def back_x(value, step):
        return lax.ppermute(
            value, "tm", [(4 * x + y, 4 * (x - step) + y) for x in range(step, 4) for y in range(4)]
        )

    bf = jnp.bfloat16
    gains_own = transitions.reshape(HALF, D)
    got = [gains_own] + [along_z(gains_own, step) for step in (1, 2, 3)]
    got = got + [other_core(piece) for piece in got]
    e_hi, e_lo, s_hi, s_lo, total, total_half = call(
        block_kernel,
        "block",
        [
            shape(4, D, D, dtype=bf),
            shape(4, D, D, dtype=bf),
            shape(3, D, D, dtype=bf),
            shape(3, D, D, dtype=bf),
            shape(D, D),
            shape(HALF, D),
        ],
        [SMEM] + [VMEM] * 8,
        products=3,
    )(place, *got)

    packed = lax.dynamic_update_slice(jnp.zeros((8, D), jnp.float32), offsets, (0, panel * ROWS))
    noise = jnp.concatenate([noise_cov.reshape(HALF, D), packed], axis=0)
    noise, total_half = lax.optimization_barrier((noise, total_half))
    got = [noise] + [along_z(noise, step) for step in (1, 2, 3)]
    got = got + [other_core(piece) for piece in got]
    rows, means, cov, cov_half = call(
        noise_kernel,
        "noise",
        [shape(4, ROWS, D), shape(8, D), shape(AUG, D), shape(HALF + 8, D)],
        [SMEM] + [VMEM] * 10,
        [pltpu.VMEM((AUG, D), jnp.float32)],
        products=6,
    )(place, e_hi, e_lo, *got)

    got = [along_y(total_half, step) for step in (1, 2, 3)]
    got = got + [other_core(piece) for piece in got]
    a_hi, a_lo, p_hi, p_lo, gain_half = call(
        gains_kernel,
        "gains",
        [
            shape(4, D, D, dtype=bf),
            shape(4, D, D, dtype=bf),
            shape(D, D, dtype=bf),
            shape(D, D, dtype=bf),
            shape(HALF, D),
        ],
        [SMEM] + [VMEM] * 7,
        [pltpu.VMEM((D, D), jnp.float32)],
        products=3,
    )(place, total, *got)

    got = [along_y(cov_half, step) for step in (1, 2, 3)]
    got = got + [other_core(piece) for piece in got]
    later, cov_half = call(
        covs_kernel,
        "covs",
        [shape(AUG, D), shape(HALF + 8, D)],
        [SMEM] + [VMEM] * 9,
        [
            pltpu.VMEM((4, AUG, D), jnp.float32),
            pltpu.VMEM((AUG, D), jnp.float32),
            pltpu.VMEM((AUG, D), jnp.float32),
        ],
        products=6,
    )(place, a_hi, a_lo, cov, *got)

    far = []
    for value, steps in ((gain_half, (1, 2)), (cov_half, (1, 2, 3))):
        for step in steps:
            piece = back_x(value, step)
            far += [piece, other_core(piece)]
    out, means = call(
        final_kernel,
        "final",
        [shape(4, ROWS, D), shape(8, D)],
        [SMEM] + [VMEM] * 19,
        [
            pltpu.VMEM((AUG, D), jnp.float32),
            pltpu.VMEM((AUG, D), jnp.float32),
            pltpu.VMEM((ROWS + 8, D), jnp.float32),
        ],
        products=7,
    )(place, e_hi, e_lo, s_hi, s_lo, p_hi, p_lo, later, rows, means, *far)
    return lax.dynamic_slice(means, (0, panel * ROWS), (4, ROWS)), out


def solution(mesh):
    placed = (P("tm", "panel", None), P("tm", "panel"), P("tm", "panel", None))
    return jax.shard_map(
        per_device,
        mesh=mesh,
        in_specs=placed,
        out_specs=(P("tm", "panel"), P("tm", "panel", None)),
        check_vma=False,
    )
```

time: 739 us -> 213 us (0.29)
  the two profiles are of different devices: /device:TPU:1 before, /device:TPU:3 now
where the time goes in v1:
time: 213 us
  waiting for transfers between devices  109 us (51%)
  Pallas kernels  51.8 us (24%)
  starting transfers between devices  41.4 us (19%)
  local copies, waits for them, and re-layouts  8.61 us (4%)
    ppermute x5, waiting for transfers between devices, back_x(): lax.ppermute(value, 'tm', [(4 * x + y, 4 * (x - step) + y) for x in range...  39.9 us
    ppermute x6, waiting for transfers between devices, along_z(): lax.ppermute(value, 'panel', [(2 * z + c, 2 * ((z + step) % 4) + c) for z...  39.1 us
    ppermute x6, waiting for transfers between devices, along_y(): lax.ppermute(value, 'tm', [(4 * x + y, 4 * x + (y + step) % 4) for x in r...  27.9 us
    ppermute x19, starting transfers between devices, other_core(): lax.ppermute(value, 'panel', [(2 * z + c, 2 * z + 1 - c) for z in range(4...  16 us
    pallas_call x1, Pallas kernels, per_device(): call(final_kernel, 'final', [shape(4, ROWS, D), shape(8, D)], [SMEM] + [V...  15.5 us
    pallas_call x1, Pallas kernels, per_device(): call(noise_kernel, 'noise', [shape(4, ROWS, D), shape(8, D), shape(AUG, D...  10.8 us
    pallas_call x1, Pallas kernels, per_device(): call(covs_kernel, 'covs', [shape(AUG, D), shape(HALF + 8, D)], [SMEM] + [...  10.4 us
    ppermute x6, starting transfers between devices, along_z(): lax.ppermute(value, 'panel', [(2 * z + c, 2 * ((z + step) % 4) + c) for z...  9.61 us
  transfers between devices with their start and end apart: 36, of which 12 were waited for; matrix products, arithmetic and copies ran while one was open for 2% of the time, Pallas kernels for 9%

profile of v1, /device:TPU:3, one launch (start us, length us, event | category | flops | bytes accessed | tf_op | source)
XLA Modules:
  0.0 213.1 jit_solution(11529491967061699208)
XLA Ops:
  0.6 1.7 collective-permute-start
  2.3 3.3 %collective-permute-start.1 = (f32[256,512]{1,0:T(8,128)}, f32[256,512]{1,0:T(8,128)S(1)}, u32[]{:S(2)}, u32[]{:S(2)}) collective-permute-start(f32[256,512]{1,0:T(8,128)} %bitcast.8), channel_id=1, source_target_pairs={{0,4},{1,5},{2,6},{3,7},{4,0},{5,1},{6,2},{7,3},{8,12},{9,13},{10,... | collective-permute-start | bytes 1572872 | tf_op jit(solution)/shard_map/ppermute | solution.py:210
  5.6 0.7 collective-permute-start.2
  6.4 1.5 collective-permute-start.3
  7.9 8.4 %collective-permute-done.refs_1_ = f32[256,512]{1,0:T(8,128)S(1)} collective-permute-done((f32[256,512]{1,0:T(8,128)}, f32[256,512]{1,0:T(8,128)S(1)}, u32[]{:S(2)}, u32[]{:S(2)}) %collective-permute-start) | collective-permute-done | bytes 524320 | tf_op jit(solution)/shard_map/ppermute | solution.py:210
  16.3 1.2 collective-permute-start.4
  17.5 10.9 %collective-permute-done.1.refs_2_ = f32[256,512]{1,0:T(8,128)S(1)} collective-permute-done((f32[256,512]{1,0:T(8,128)}, f32[256,512]{1,0:T(8,128)S(1)}, u32[]{:S(2)}, u32[]{:S(2)}) %collective-permute-start.1) | collective-permute-done | bytes 524320 | tf_op jit(solution)/shard_map/ppermute | solution.py:210
  28.4 1.5 collective-permute-start.5
  30.1 1.7 dynamic_update_slice.3
  31.8 0.6 pad_add_fusion.place
  32.4 1.1 pad_maximum_fusion.refs_0_
  33.6 0.7 copy-done.23
  34.3 0.2 copy-done.24
  34.6 0.2 copy-done.25
  34.8 7.8 %block.1 = (bf16[4,512,512]{2,1,0:T(8,128)(2,1)}, bf16[4,512,512]{2,1,0:T(8,128)(2,1)}, bf16[3,512,512]{2,1,0:T(8,128)(2,1)}, bf16[3,512,512]{2,1,0:T(8,128)(2,1...) custom-call(s32[4]{0:T(128)} %pad_add_fusion.place, f32[256,512]{1,0:T(8,128)} %bitcast.11, f32[256,512]{1,0:T(8,128)} %copy-done.20, ...), custom_call_target="tpu_custom_call" | custom-call | flops 2415919104 | bytes 8388608 | tf_op jit(solution)/shard_map/block/pallas_call | solution.py:231
  42.5 0.8 collective-permute-start.13
  43.3 2.1 collective-permute-start.14
  45.4 1.0 collective-permute-start.15
  46.4 1.3 collective-permute-start.7
  47.7 1.0 collective-permute-start.16
  48.7 8.8 %collective-permute-done.13.refs_1_ = f32[264,512]{1,0:T(8,128)S(1)} collective-permute-done((f32[264,512]{1,0:T(8,128)S(1)}, f32[264,512]{1,0:T(8,128)S(1)}, u32[]{:S(2)}, u32[]{:S(2)}) %collective-permute-start.13) | collective-permute-done | bytes 540704 | tf_op jit(solution)/shard_map/ppermute | solution.py:210
  57.5 1.0 collective-permute-start.17
  58.5 11.1 %collective-permute-done.14.refs_2_ = f32[264,512]{1,0:T(8,128)S(1)} collective-permute-done((f32[264,512]{1,0:T(8,128)S(1)}, f32[264,512]{1,0:T(8,128)S(1)}, u32[]{:S(2)}, u32[]{:S(2)}) %collective-permute-start.14) | collective-permute-done | bytes 540704 | tf_op jit(solution)/shard_map/ppermute | solution.py:210
  69.6 0.7 collective-permute-start.18
  70.2 0.4 collective-permute-start.19
  70.6 2.9 %collective-permute-start.8 = (f32[256,512]{1,0:T(8,128)}, f32[256,512]{1,0:T(8,128)S(1)}, u32[]{:S(2)}, u32[]{:S(2)}) collective-permute-start(f32[256,512]{1,0:T(8,128)} %get-tuple-element.29), channel_id=1, source_target_pairs={{0,16},{8,24},{16,0},{24,8},{32,48},{40,56},{48,32},{56,40},{64,80... | collective-permute-start | bytes 1572872 | tf_op jit(solution)/shard_map/ppermute | solution.py:218
  73.6 0.8 collective-permute-start.9
  74.4 0.6 collective-permute-start.10
  75.2 0.6 copy-done.16
  75.8 0.2 copy-done.18
  76.0 10.8 %noise.1 = (f32[4,64,512]{2,1,0:T(8,128)}, f32[8,512]{1,0:T(8,128)}, f32[520,512]{1,0:T(8,128)}, f32[264,512]{1,0:T(8,128)}) custom-call(s32[4]{0:T(128)} %pad_add_fusion.place, bf16[4,512,512]{2,1,0:T(8,128)(2,1)} %get-tuple-element.23.e_hi, bf16[4,512,512]{2,1,0:T(8,128)(2,1)} %get-tuple-element.24.e_lo, f32[264,512]{1,0:T(8,128)} %copy-done, ...), custom_call_target="tpu_custom_call" | custom-call | flops 4831838208 | bytes 8388608 | tf_op jit(solution)/shard_map/noise/pallas_call | solution.py:251
  86.8 0.7 collective-permute-start.20
  87.5 0.8 collective-permute-start.21
  88.3 2.0 collective-permute-start.22
  90.3 7.2 %collective-permute-done.9.refs_2_ = f32[256,512]{1,0:T(8,128)S(1)} collective-permute-done((f32[256,512]{1,0:T(8,128)}, f32[256,512]{1,0:T(8,128)S(1)}, u32[]{:S(2)}, u32[]{:S(2)}) %collective-permute-start.9) | collective-permute-done | bytes 524320 | tf_op jit(solution)/shard_map/ppermute | solution.py:218
  97.5 1.3 collective-permute-start.11
  98.9 14.6 %collective-permute-done.20.refs_0_ = f32[264,512]{1,0:T(8,128)S(1)} collective-permute-done((f32[264,512]{1,0:T(8,128)}, f32[264,512]{1,0:T(8,128)S(1)}, u32[]{:S(2)}, u32[]{:S(2)}) %collective-permute-start.20) | collective-permute-done | bytes 540704 | tf_op jit(solution)/shard_map/ppermute | solution.py:218
  113.5 1.0 collective-permute-start.23
  114.6 6.1 %collective-permute-done.22.refs_2_ = f32[264,512]{1,0:T(8,128)S(1)} collective-permute-done((f32[264,512]{1,0:T(8,128)}, f32[264,512]{1,0:T(8,128)S(1)}, u32[]{:S(2)}, u32[]{:S(2)}) %collective-permute-start.22) | collective-permute-done | bytes 540704 | tf_op jit(solution)/shard_map/ppermute | solution.py:218
  120.7 0.9 collective-permute-start.25
  121.6 0.7 copy-done.34
  122.4 0.2 copy-done.36
  122.6 7.5 %gains.1 = (bf16[4,512,512]{2,1,0:T(8,128)(2,1)}, bf16[4,512,512]{2,1,0:T(8,128)(2,1)}, bf16[512,512]{1,0:T(8,128)(2,1)}, bf16[512,512]{1,0:T(8,128)(2,1)}, f32[256,512]{1,0:T(8,128)}) custom-call(s32[4]{0:T(128)} %pad_add_fusion.place, f32[512,512]{1,0:T(8,128)} %get-tuple-element.27.own, f32[256,512]{1,0:T(8,128)} %copy-done.26, f32[256,512]{1,0:T(8,128)} %copy-done.27, ...), custom_call_target="tpu_custom_call" | custom-call | flops 2415919104 | bytes 8388608 | tf_op jit(solution)/shard_map/gains/pallas_call | solution.py:262
  130.1 0.8 copy-done.15
  130.9 0.2 copy-done.17
  131.3 10.4 %covs.1 = (f32[520,512]{1,0:T(8,128)}, f32[264,512]{1,0:T(8,128)}) custom-call(s32[4]{0:T(128)} %pad_add_fusion.place, bf16[4,512,512]{2,1,0:T(8,128)(2,1)} %get-tuple-element.32.a_hi, bf16[4,512,512]{2,1,0:T(8,128)(2,1)} %get-tuple-element.33.a_lo, f32[520,512]{1,0:T(8,128)} %get-tuple-element.35.own, f32[264,512]{1,0:T(8,128)} %copy-done.3, ...), custom_call_target="tpu_custom_call" | custom-call | flops 4831838208 | bytes 8388608 | tf_op jit(solution)/shard_map/covs/pallas_call | solution.py:279
  141.6 2.2 %collective-permute-start.30 = (f32[264,512]{1,0:T(8,128)}, f32[264,512]{1,0:T(8,128)S(1)}, u32[]{:S(2)}, u32[]{:S(2)}) collective-permute-start(f32[264,512]{1,0:T(8,128)} %get-tuple-element.41), channel_id=1, source_target_pairs={{32,0},{40,8},{48,16},{56,24},{64,32},{72,40},{80,48},{88,56},{96,... | collective-permute-start | bytes 1622024 | tf_op jit(solution)/shard_map/ppermute | solution.py:223
  143.8 1.3 collective-permute-start.32
  145.1 0.7 collective-permute-start.34
  145.8 1.9 collective-permute-start.26
  147.8 1.3 collective-permute-start.28
  149.1 8.5 %collective-permute-done.30.refs_4_ = f32[264,512]{1,0:T(8,128)S(1)} collective-permute-done((f32[264,512]{1,0:T(8,128)}, f32[264,512]{1,0:T(8,128)S(1)}, u32[]{:S(2)}, u32[]{:S(2)}) %collective-permute-start.30) | collective-permute-done | bytes 540704 | tf_op jit(solution)/shard_map/ppermute | solution.py:223
  157.6 1.3 collective-permute-start.31
  158.9 11.2 %collective-permute-done.32.refs_6_ = f32[264,512]{1,0:T(8,128)S(1)} collective-permute-done((f32[264,512]{1,0:T(8,128)}, f32[264,512]{1,0:T(8,128)S(1)}, u32[]{:S(2)}, u32[]{:S(2)}) %collective-permute-start.32) | collective-permute-done | bytes 540704 | tf_op jit(solution)/shard_map/ppermute | solution.py:223
  170.1 1.3 collective-permute-start.33
  171.6 8.8 %collective-permute-done.26.refs_0_ = f32[256,512]{1,0:T(8,128)S(1)} collective-permute-done((f32[256,512]{1,0:T(8,128)S(1)}, f32[256,512]{1,0:T(8,128)S(1)}, u32[]{:S(2)}, u32[]{:S(2)}) %collective-permute-start.26) | collective-permute-done | bytes 524320 | tf_op jit(solution)/shard_map/ppermute | solution.py:223
  180.4 0.9 collective-permute-start.27
  181.3 11.3 %collective-permute-done.28.refs_2_ = f32[256,512]{1,0:T(8,128)S(1)} collective-permute-done((f32[256,512]{1,0:T(8,128)S(1)}, f32[256,512]{1,0:T(8,128)S(1)}, u32[]{:S(2)}, u32[]{:S(2)}) %collective-permute-start.28) | collective-permute-done | bytes 524320 | tf_op jit(solution)/shard_map/ppermute | solution.py:223
  192.6 0.9 collective-permute-start.29
  193.5 1.5 collective-permute-done.29.refs_3_
  195.1 0.7 copy-done.35
  195.8 0.2 copy-done.9
  196.3 15.5 %final.1 = (f32[4,64,512]{2,1,0:T(8,128)}, f32[8,512]{1,0:T(8,128)}) custom-call(s32[4]{0:T(128)} %pad_add_fusion.place, bf16[4,512,512]{2,1,0:T(8,128)(2,1)} %get-tuple-element.23.e_hi, bf16[4,512,512]{2,1,0:T(8,128)(2,1)} %get-tuple-element.24.e_lo, bf16[3,512,512]{2,1,0:T(8,128)(2,1)} %get-tuple-element.25.s_hi, ...), custom_call_target="tpu_custom_call" | custom-call | flops 5637144576 | bytes 8388608 | tf_op jit(solution)/shard_map/final/pallas_call | solution.py:297
  211.8 1.3 constant_dynamic-slice_fusion
  (92 shorter events, 1.1 us)
Async XLA Ops:
  0.6 15.7 %collective-permute-start = (f32[256,512]{1,0:T(8,128)}, f32[256,512]{1,0:T(8,128)S(1)}, u32[]{:S(2)}, u32[]{:S(2)}) collective-permute-start(f32[256,512]{1,0:T(8,128)} %bitcast.7), channel_id=1, source_target_pairs={{0,2},{1,3},{2,4},{3,5},{4,6},{5,7},{6,0},{7,1},{8,10},{9,11},{10,... | collective-permute-start | bytes 1572872 | tf_op jit(solution)/shard_map/ppermute | solution.py:210
  2.3 26.1 %collective-permute-start.1 = (f32[256,512]{1,0:T(8,128)}, f32[256,512]{1,0:T(8,128)S(1)}, u32[]{:S(2)}, u32[]{:S(2)}) collective-permute-start(f32[256,512]{1,0:T(8,128)} %bitcast.8), channel_id=1, source_target_pairs={{0,4},{1,5},{2,6},{3,7},{4,0},{5,1},{6,2},{7,3},{8,12},{9,13},{10,... | collective-permute-start | bytes 1572872 | tf_op jit(solution)/shard_map/ppermute | solution.py:210
  5.6 24.3 %collective-permute-start.2 = (f32[256,512]{1,0:T(8,128)}, f32[256,512]{1,0:T(8,128)S(1)}, u32[]{:S(2)}, u32[]{:S(2)}) collective-permute-start(f32[256,512]{1,0:T(8,128)} %bitcast.9), channel_id=1, source_target_pairs={{0,6},{1,7},{2,0},{3,1},{4,2},{5,3},{6,4},{7,5},{8,14},{9,15},{10,... | collective-permute-start | bytes 1572872 | tf_op jit(solution)/shard_map/ppermute | solution.py:210
  6.4 27.1 %collective-permute-start.3 = (f32[256,512]{1,0:T(8,128)}, f32[256,512]{1,0:T(8,128)S(1)}, u32[]{:S(2)}, u32[]{:S(2)}) collective-permute-start(f32[256,512]{1,0:T(8,128)} %bitcast.10), channel_id=1, source_target_pairs={{0,1},{1,0},{2,3},{3,2},{4,5},{5,4},{6,7},{7,6},{8,9},{9,8},{10,11... | collective-permute-start | bytes 1572872 | tf_op jit(solution)/shard_map/ppermute | solution.py:215
  16.3 17.2 %copy-start.20 = (f32[256,512]{1,0:T(8,128)}, f32[256,512]{1,0:T(8,128)S(1)}, u32[]{:S(2)}) copy-start(f32[256,512]{1,0:T(8,128)S(1)} %collective-permute-done.refs_1_) | copy-start | bytes 1572868
  16.3 17.2 %collective-permute-start.4 = (f32[256,512]{1,0:T(8,128)S(1)}, f32[256,512]{1,0:T(8,128)S(1)}, u32[]{:S(2)}, u32[]{:S(2)}) collective-permute-start(f32[256,512]{1,0:T(8,128)S(1)} %collective-permute-done.refs_1_), channel_id=1, source_target_pairs={{0,1},{1,0},{2,3},{3,2},{4,5},{5,4},{6,7},{7,6},{8,9},{9,8},{10,11... | collective-permute-start | bytes 1572872 | tf_op jit(solution)/shard_map/ppermute | solution.py:215
  28.4 5.2 %copy-start.21 = (f32[256,512]{1,0:T(8,128)}, f32[256,512]{1,0:T(8,128)S(1)}, u32[]{:S(2)}) copy-start(f32[256,512]{1,0:T(8,128)S(1)} %collective-permute-done.1.refs_2_) | copy-start | bytes 1572868
  28.4 5.1 %collective-permute-start.5 = (f32[256,512]{1,0:T(8,128)S(1)}, f32[256,512]{1,0:T(8,128)S(1)}, u32[]{:S(2)}, u32[]{:S(2)}) collective-permute-start(f32[256,512]{1,0:T(8,128)S(1)} %collective-permute-done.1.refs_2_), channel_id=1, source_target_pairs={{0,1},{1,0},{2,3},{3,2},{4,5},{5,4},{6,7},{7,6},{8,9},{9,8},{10,11... | collective-permute-start | bytes 1572872 | tf_op jit(solution)/shard_map/ppermute | solution.py:215
  30.0 3.6 %copy-start.22 = (f32[256,512]{1,0:T(8,128)}, f32[256,512]{1,0:T(8,128)S(1)}, u32[]{:S(2)}) copy-start(f32[256,512]{1,0:T(8,128)S(1)} %collective-permute-done.2.refs_3_) | copy-start | bytes 1572868
  30.0 3.6 %collective-permute-start.6 = (f32[256,512]{1,0:T(8,128)S(1)}, f32[256,512]{1,0:T(8,128)}, u32[]{:S(2)}, u32[]{:S(2)}) collective-permute-start(f32[256,512]{1,0:T(8,128)S(1)} %collective-permute-done.2.refs_3_), channel_id=1, source_target_pairs={{0,1},{1,0},{2,3},{3,2},{4,5},{5,4},{6,7},{7,6},{8,9},{9,8},{10,11... | collective-permute-start | bytes 1572872 | tf_op jit(solution)/shard_map/ppermute | solution.py:215
  33.5 14.2 %copy-start = (f32[264,512]{1,0:T(8,128)}, f32[264,512]{1,0:T(8,128)S(1)}, u32[]{:S(2)}) copy-start(f32[264,512]{1,0:T(8,128)S(1)} %pad_maximum_fusion.refs_0_) | copy-start | bytes 1622020
  33.5 1.0 copy-start.24
  33.5 1.2 copy-start.25
  42.5 14.9 %collective-permute-start.13 = (f32[264,512]{1,0:T(8,128)S(1)}, f32[264,512]{1,0:T(8,128)S(1)}, u32[]{:S(2)}, u32[]{:S(2)}) collective-permute-start(f32[264,512]{1,0:T(8,128)S(1)} %pad_maximum_fusion.refs_0_), channel_id=1, source_target_pairs={{0,2},{1,3},{2,4},{3,5},{4,6},{5,7},{6,0},{7,1},{8,10},{9,11},{10,... | collective-permute-start | bytes 1622024 | tf_op jit(solution)/shard_map/ppermute | solution.py:210
  43.3 26.2 %collective-permute-start.14 = (f32[264,512]{1,0:T(8,128)S(1)}, f32[264,512]{1,0:T(8,128)S(1)}, u32[]{:S(2)}, u32[]{:S(2)}) collective-permute-start(f32[264,512]{1,0:T(8,128)S(1)} %pad_maximum_fusion.refs_0_), channel_id=1, source_target_pairs={{0,4},{1,5},{2,6},{3,7},{4,0},{5,1},{6,2},{7,3},{8,12},{9,13},{10,... | collective-permute-start | bytes 1622024 | tf_op jit(solution)/shard_map/ppermute | solution.py:210
  45.4 24.8 %collective-permute-start.15 = (f32[264,512]{1,0:T(8,128)S(1)}, f32[264,512]{1,0:T(8,128)S(1)}, u32[]{:S(2)}, u32[]{:S(2)}) collective-permute-start(f32[264,512]{1,0:T(8,128)S(1)} %pad_maximum_fusion.refs_0_), channel_id=1, source_target_pairs={{0,6},{1,7},{2,0},{3,1},{4,2},{5,3},{6,4},{7,5},{8,14},{9,15},{10,... | collective-permute-start | bytes 1622024 | tf_op jit(solution)/shard_map/ppermute | solution.py:210
  46.4 24.2 %collective-permute-start.7 = (f32[256,512]{1,0:T(8,128)}, f32[256,512]{1,0:T(8,128)S(1)}, u32[]{:S(2)}, u32[]{:S(2)}) collective-permute-start(f32[256,512]{1,0:T(8,128)} %get-tuple-element.29), channel_id=1, source_target_pairs={{0,8},{8,16},{16,24},{24,0},{32,40},{40,48},{48,56},{56,32},{64,72... | collective-permute-start | bytes 1572872 | tf_op jit(solution)/shard_map/ppermute | solution.py:218
  47.7 25.9 %collective-permute-start.16 = (f32[264,512]{1,0:T(8,128)S(1)}, f32[264,512]{1,0:T(8,128)S(1)}, u32[]{:S(2)}, u32[]{:S(2)}) collective-permute-start(f32[264,512]{1,0:T(8,128)S(1)} %pad_maximum_fusion.refs_0_), channel_id=1, source_target_pairs={{0,1},{1,0},{2,3},{3,2},{4,5},{5,4},{6,7},{7,6},{8,9},{9,8},{10,11... | collective-permute-start | bytes 1622024 | tf_op jit(solution)/shard_map/ppermute | solution.py:215
  57.5 17.6 %copy-start.7 = (f32[264,512]{1,0:T(8,128)}, f32[264,512]{1,0:T(8,128)S(1)}, u32[]{:S(2)}) copy-start(f32[264,512]{1,0:T(8,128)S(1)} %collective-permute-done.13.refs_1_) | copy-start | bytes 1622020
  57.5 16.9 %collective-permute-start.17 = (f32[264,512]{1,0:T(8,128)S(1)}, f32[264,512]{1,0:T(8,128)S(1)}, u32[]{:S(2)}, u32[]{:S(2)}) collective-permute-start(f32[264,512]{1,0:T(8,128)S(1)} %collective-permute-done.13.refs_1_), channel_id=1, source_target_pairs={{0,1},{1,0},{2,3},{3,2},{4,5},{5,4},{6,7},{7,6},{8,9},{9,8},{10,11... | collective-permute-start | bytes 1622024 | tf_op jit(solution)/shard_map/ppermute | solution.py:215
  69.6 5.5 %copy-start.8 = (f32[264,512]{1,0:T(8,128)}, f32[264,512]{1,0:T(8,128)S(1)}, u32[]{:S(2)}) copy-start(f32[264,512]{1,0:T(8,128)S(1)} %collective-permute-done.14.refs_2_) | copy-start | bytes 1622020
  69.6 5.4 %collective-permute-start.18 = (f32[264,512]{1,0:T(8,128)S(1)}, f32[264,512]{1,0:T(8,128)S(1)}, u32[]{:S(2)}, u32[]{:S(2)}) collective-permute-start(f32[264,512]{1,0:T(8,128)S(1)} %collective-permute-done.14.refs_2_), channel_id=1, source_target_pairs={{0,1},{1,0},{2,3},{3,2},{4,5},{5,4},{6,7},{7,6},{8,9},{9,8},{10,11... | collective-permute-start | bytes 1622024 | tf_op jit(solution)/shard_map/ppermute | solution.py:215
  70.2 4.8 %copy-start.10 = (f32[264,512]{1,0:T(8,128)}, f32[264,512]{1,0:T(8,128)S(1)}, u32[]{:S(2)}) copy-start(f32[264,512]{1,0:T(8,128)S(1)} %collective-permute-done.15.refs_3_) | copy-start | bytes 1622020
  70.2 4.8 %collective-permute-start.19 = (f32[264,512]{1,0:T(8,128)S(1)}, f32[264,512]{1,0:T(8,128)S(1)}, u32[]{:S(2)}, u32[]{:S(2)}) collective-permute-start(f32[264,512]{1,0:T(8,128)S(1)} %collective-permute-done.15.refs_3_), channel_id=1, source_target_pairs={{0,1},{1,0},{2,3},{3,2},{4,5},{5,4},{6,7},{7,6},{8,9},{9,8},{10,11... | collective-permute-start | bytes 1622024 | tf_op jit(solution)/shard_map/ppermute | solution.py:215
  70.6 16.1 %copy-start.26 = (f32[256,512]{1,0:T(8,128)}, f32[256,512]{1,0:T(8,128)S(1)}, u32[]{:S(2)}) copy-start(f32[256,512]{1,0:T(8,128)S(1)} %collective-permute-done.7.refs_0_) | copy-start | bytes 1572868
  70.6 17.6 %collective-permute-start.8 = (f32[256,512]{1,0:T(8,128)}, f32[256,512]{1,0:T(8,128)S(1)}, u32[]{:S(2)}, u32[]{:S(2)}) collective-permute-start(f32[256,512]{1,0:T(8,128)} %get-tuple-element.29), channel_id=1, source_target_pairs={{0,16},{8,24},{16,0},{24,8},{32,48},{40,56},{48,32},{56,40},{64,80... | collective-permute-start | bytes 1572872 | tf_op jit(solution)/shard_map/ppermute | solution.py:218
  73.6 1.5 copy-start.12
  73.6 23.9 %collective-permute-start.9 = (f32[256,512]{1,0:T(8,128)}, f32[256,512]{1,0:T(8,128)S(1)}, u32[]{:S(2)}, u32[]{:S(2)}) collective-permute-start(f32[256,512]{1,0:T(8,128)} %get-tuple-element.29), channel_id=1, source_target_pairs={{0,24},{8,0},{16,8},{24,16},{32,56},{40,32},{48,40},{56,48},{64,88... | collective-permute-start | bytes 1572872 | tf_op jit(solution)/shard_map/ppermute | solution.py:218
  74.4 24.5 %collective-permute-start.10 = (f32[256,512]{1,0:T(8,128)S(1)}, f32[256,512]{1,0:T(8,128)S(1)}, u32[]{:S(2)}, u32[]{:S(2)}) collective-permute-start(f32[256,512]{1,0:T(8,128)S(1)} %collective-permute-done.7.refs_0_), channel_id=1, source_target_pairs={{0,1},{1,0},{2,3},{3,2},{4,5},{5,4},{6,7},{7,6},{8,9},{9,8},{10,11... | collective-permute-start | bytes 1572872 | tf_op jit(solution)/shard_map/ppermute | solution.py:215
  86.8 26.7 %collective-permute-start.20 = (f32[264,512]{1,0:T(8,128)}, f32[264,512]{1,0:T(8,128)S(1)}, u32[]{:S(2)}, u32[]{:S(2)}) collective-permute-start(f32[264,512]{1,0:T(8,128)} %get-tuple-element.36), channel_id=1, source_target_pairs={{0,8},{8,16},{16,24},{24,0},{32,40},{40,48},{48,56},{56,32},{64,72... | collective-permute-start | bytes 1622024 | tf_op jit(solution)/shard_map/ppermute | solution.py:218
  87.5 27.0 %collective-permute-start.21 = (f32[264,512]{1,0:T(8,128)}, f32[264,512]{1,0:T(8,128)S(1)}, u32[]{:S(2)}, u32[]{:S(2)}) collective-permute-start(f32[264,512]{1,0:T(8,128)} %get-tuple-element.36), channel_id=1, source_target_pairs={{0,16},{8,24},{16,0},{24,8},{32,48},{40,56},{48,32},{56,40},{64,80... | collective-permute-start | bytes 1622024 | tf_op jit(solution)/shard_map/ppermute | solution.py:218
  88.3 33.3 %copy-start.27 = (f32[256,512]{1,0:T(8,128)}, f32[256,512]{1,0:T(8,128)S(1)}, u32[]{:S(2)}) copy-start(f32[256,512]{1,0:T(8,128)S(1)} %collective-permute-done.8.refs_1_) | copy-start | bytes 1572868
  88.3 32.4 %collective-permute-start.22 = (f32[264,512]{1,0:T(8,128)}, f32[264,512]{1,0:T(8,128)S(1)}, u32[]{:S(2)}, u32[]{:S(2)}) collective-permute-start(f32[264,512]{1,0:T(8,128)} %get-tuple-element.36), channel_id=1, source_target_pairs={{0,24},{8,0},{16,8},{24,16},{32,56},{40,32},{48,40},{56,48},{64,88... | collective-permute-start | bytes 1622024 | tf_op jit(solution)/shard_map/ppermute | solution.py:218
  97.5 24.1 %copy-start.28 = (f32[256,512]{1,0:T(8,128)}, f32[256,512]{1,0:T(8,128)S(1)}, u32[]{:S(2)}) copy-start(f32[256,512]{1,0:T(8,128)S(1)} %collective-permute-done.9.refs_2_) | copy-start | bytes 1572868
  97.5 24.1 %collective-permute-start.11 = (f32[256,512]{1,0:T(8,128)S(1)}, f32[256,512]{1,0:T(8,128)S(1)}, u32[]{:S(2)}, u32[]{:S(2)}) collective-permute-start(f32[256,512]{1,0:T(8,128)S(1)} %collective-permute-done.8.refs_1_), channel_id=1, source_target_pairs={{0,1},{1,0},{2,3},{3,2},{4,5},{5,4},{6,7},{7,6},{8,9},{9,8},{10,11... | collective-permute-start | bytes 1572872 | tf_op jit(solution)/shard_map/ppermute | solution.py:215
  98.8 22.8 %copy-start.29 = (f32[256,512]{1,0:T(8,128)}, f32[256,512]{1,0:T(8,128)S(1)}, u32[]{:S(2)}) copy-start(f32[256,512]{1,0:T(8,128)S(1)} %collective-permute-done.10.refs_3_) | copy-start | bytes 1572868
  98.8 22.7 %collective-permute-start.12 = (f32[256,512]{1,0:T(8,128)S(1)}, f32[256,512]{1,0:T(8,128)S(1)}, u32[]{:S(2)}, u32[]{:S(2)}) collective-permute-start(f32[256,512]{1,0:T(8,128)S(1)} %collective-permute-done.9.refs_2_), channel_id=1, source_target_pairs={{0,1},{1,0},{2,3},{3,2},{4,5},{5,4},{6,7},{7,6},{8,9},{9,8},{10,11... | collective-permute-start | bytes 1572872 | tf_op jit(solution)/shard_map/ppermute | solution.py:215
  113.5 16.5 %copy-start.3 = (f32[264,512]{1,0:T(8,128)}, f32[264,512]{1,0:T(8,128)S(1)}, u32[]{:S(2)}) copy-start(f32[264,512]{1,0:T(8,128)S(1)} %collective-permute-done.20.refs_0_) | copy-start | bytes 1622020
  113.5 16.6 %collective-permute-start.23 = (f32[264,512]{1,0:T(8,128)S(1)}, f32[264,512]{1,0:T(8,128)S(1)}, u32[]{:S(2)}, u32[]{:S(2)}) collective-permute-start(f32[264,512]{1,0:T(8,128)S(1)} %collective-permute-done.20.refs_0_), channel_id=1, source_target_pairs={{0,1},{1,0},{2,3},{3,2},{4,5},{5,4},{6,7},{7,6},{8,9},{9,8},{10,11... | collective-permute-start | bytes 1622024 | tf_op jit(solution)/shard_map/ppermute | solution.py:215
  114.5 15.6 %copy-start.5 = (f32[264,512]{1,0:T(8,128)}, f32[264,512]{1,0:T(8,128)S(1)}, u32[]{:S(2)}) copy-start(f32[264,512]{1,0:T(8,128)S(1)} %collective-permute-done.21.refs_1_) | copy-start | bytes 1622020
  114.5 15.6 %collective-permute-start.24 = (f32[264,512]{1,0:T(8,128)S(1)}, f32[264,512]{1,0:T(8,128)S(1)}, u32[]{:S(2)}, u32[]{:S(2)}) collective-permute-start(f32[264,512]{1,0:T(8,128)S(1)} %collective-permute-done.21.refs_1_), channel_id=1, source_target_pairs={{0,1},{1,0},{2,3},{3,2},{4,5},{5,4},{6,7},{7,6},{8,9},{9,8},{10,11... | collective-permute-start | bytes 1622024 | tf_op jit(solution)/shard_map/ppermute | solution.py:215
  120.7 9.3 %copy-start.6 = (f32[264,512]{1,0:T(8,128)}, f32[264,512]{1,0:T(8,128)S(1)}, u32[]{:S(2)}) copy-start(f32[264,512]{1,0:T(8,128)S(1)} %collective-permute-done.22.refs_2_) | copy-start | bytes 1622020
  120.7 9.4 %collective-permute-start.25 = (f32[264,512]{1,0:T(8,128)S(1)}, f32[264,512]{1,0:T(8,128)S(1)}, u32[]{:S(2)}, u32[]{:S(2)}) collective-permute-start(f32[264,512]{1,0:T(8,128)S(1)} %collective-permute-done.22.refs_2_), channel_id=1, source_target_pairs={{0,1},{1,0},{2,3},{3,2},{4,5},{5,4},{6,7},{7,6},{8,9},{9,8},{10,11... | collective-permute-start | bytes 1622024 | tf_op jit(solution)/shard_map/ppermute | solution.py:215
  130.1 1.0 copy-start.17
  130.1 1.2 copy-start.19
  131.3 14.6 %copy-start.30 = (f32[256,512]{1,0:T(8,128)S(1)}, f32[256,512]{1,0:T(8,128)}, u32[]{:S(2)}) copy-start(f32[256,512]{1,0:T(8,128)} %get-tuple-element.40) | copy-start | bytes 1572868
  141.6 15.9 %collective-permute-start.30 = (f32[264,512]{1,0:T(8,128)}, f32[264,512]{1,0:T(8,128)S(1)}, u32[]{:S(2)}, u32[]{:S(2)}) collective-permute-start(f32[264,512]{1,0:T(8,128)} %get-tuple-element.41), channel_id=1, source_target_pairs={{32,0},{40,8},{48,16},{56,24},{64,32},{72,40},{80,48},{88,56},{96,... | collective-permute-start | bytes 1622024 | tf_op jit(solution)/shard_map/ppermute | solution.py:223
  143.8 26.3 %collective-permute-start.32 = (f32[264,512]{1,0:T(8,128)}, f32[264,512]{1,0:T(8,128)S(1)}, u32[]{:S(2)}, u32[]{:S(2)}) collective-permute-start(f32[264,512]{1,0:T(8,128)} %get-tuple-element.41), channel_id=1, source_target_pairs={{64,0},{72,8},{80,16},{88,24},{96,32},{104,40},{112,48},{120,56},{... | collective-permute-start | bytes 1622024 | tf_op jit(solution)/shard_map/ppermute | solution.py:223
  145.1 26.3 %collective-permute-start.34 = (f32[264,512]{1,0:T(8,128)}, f32[264,512]{1,0:T(8,128)S(1)}, u32[]{:S(2)}, u32[]{:S(2)}) collective-permute-start(f32[264,512]{1,0:T(8,128)} %get-tuple-element.41), channel_id=1, source_target_pairs={{96,0},{104,8},{112,16},{120,24},{97,1},{105,9},{113,17},{121,25},... | collective-permute-start | bytes 1622024 | tf_op jit(solution)/shard_map/ppermute | solution.py:223
  145.8 34.6 %collective-permute-start.26 = (f32[256,512]{1,0:T(8,128)S(1)}, f32[256,512]{1,0:T(8,128)S(1)}, u32[]{:S(2)}, u32[]{:S(2)}) collective-permute-start(f32[256,512]{1,0:T(8,128)S(1)} %copy-done.30), channel_id=1, source_target_pairs={{32,0},{40,8},{48,16},{56,24},{64,32},{72,40},{80,48},{88,56},{96,... | collective-permute-start | bytes 1572872 | tf_op jit(solution)/shard_map/ppermute | solution.py:223
  147.8 44.8 %collective-permute-start.28 = (f32[256,512]{1,0:T(8,128)S(1)}, f32[256,512]{1,0:T(8,128)S(1)}, u32[]{:S(2)}, u32[]{:S(2)}) collective-permute-start(f32[256,512]{1,0:T(8,128)S(1)} %copy-done.30), channel_id=1, source_target_pairs={{64,0},{72,8},{80,16},{88,24},{96,32},{104,40},{112,48},{120,56},{... | collective-permute-start | bytes 1572872 | tf_op jit(solution)/shard_map/ppermute | solution.py:223
  157.6 37.5 %copy-start.1 = (f32[264,512]{1,0:T(8,128)}, f32[264,512]{1,0:T(8,128)S(1)}, u32[]{:S(2)}) copy-start(f32[264,512]{1,0:T(8,128)S(1)} %collective-permute-done.30.refs_4_) | copy-start | bytes 1622020
  157.6 37.4 %collective-permute-start.31 = (f32[264,512]{1,0:T(8,128)S(1)}, f32[264,512]{1,0:T(8,128)S(1)}, u32[]{:S(2)}, u32[]{:S(2)}) collective-permute-start(f32[264,512]{1,0:T(8,128)S(1)} %collective-permute-done.30.refs_4_), channel_id=1, source_target_pairs={{0,1},{1,0},{2,3},{3,2},{4,5},{5,4},{6,7},{7,6},{8,9},{9,8},{10,11... | collective-permute-start | bytes 1622024 | tf_op jit(solution)/shard_map/ppermute | solution.py:215
  170.1 24.9 %copy-start.2 = (f32[264,512]{1,0:T(8,128)}, f32[264,512]{1,0:T(8,128)S(1)}, u32[]{:S(2)}) copy-start(f32[264,512]{1,0:T(8,128)S(1)} %collective-permute-done.32.refs_6_) | copy-start | bytes 1622020
  170.1 24.9 %collective-permute-start.33 = (f32[264,512]{1,0:T(8,128)S(1)}, f32[264,512]{1,0:T(8,128)S(1)}, u32[]{:S(2)}, u32[]{:S(2)}) collective-permute-start(f32[264,512]{1,0:T(8,128)S(1)} %collective-permute-done.32.refs_6_), channel_id=1, source_target_pairs={{0,1},{1,0},{2,3},{3,2},{4,5},{5,4},{6,7},{7,6},{8,9},{9,8},{10,11... | collective-permute-start | bytes 1622024 | tf_op jit(solution)/shard_map/ppermute | solution.py:215
  171.5 23.6 %copy-start.4 = (f32[264,512]{1,0:T(8,128)}, f32[264,512]{1,0:T(8,128)S(1)}, u32[]{:S(2)}) copy-start(f32[264,512]{1,0:T(8,128)S(1)} %collective-permute-done.34.refs_8_) | copy-start | bytes 1622020
  171.5 23.6 %collective-permute-start.35 = (f32[264,512]{1,0:T(8,128)S(1)}, f32[264,512]{1,0:T(8,128)S(1)}, u32[]{:S(2)}, u32[]{:S(2)}) collective-permute-start(f32[264,512]{1,0:T(8,128)S(1)} %collective-permute-done.34.refs_8_), channel_id=1, source_target_pairs={{0,1},{1,0},{2,3},{3,2},{4,5},{5,4},{6,7},{7,6},{8,9},{9,8},{10,11... | collective-permute-start | bytes 1622024 | tf_op jit(solution)/shard_map/ppermute | solution.py:215
  180.4 14.7 %copy-start.31 = (f32[256,512]{1,0:T(8,128)}, f32[256,512]{1,0:T(8,128)S(1)}, u32[]{:S(2)}) copy-start(f32[256,512]{1,0:T(8,128)S(1)} %collective-permute-done.26.refs_0_) | copy-start | bytes 1572868
  180.4 13.1 %collective-permute-start.27 = (f32[256,512]{1,0:T(8,128)S(1)}, f32[256,512]{1,0:T(8,128)S(1)}, u32[]{:S(2)}, u32[]{:S(2)}) collective-permute-start(f32[256,512]{1,0:T(8,128)S(1)} %collective-permute-done.26.refs_0_), channel_id=1, source_target_pairs={{0,1},{1,0},{2,3},{3,2},{4,5},{5,4},{6,7},{7,6},{8,9},{9,8},{10,11... | collective-permute-start | bytes 1572872 | tf_op jit(solution)/shard_map/ppermute | solution.py:215
  192.6 2.5 %copy-start.32 = (f32[256,512]{1,0:T(8,128)}, f32[256,512]{1,0:T(8,128)S(1)}, u32[]{:S(2)}) copy-start(f32[256,512]{1,0:T(8,128)S(1)} %collective-permute-done.28.refs_2_) | copy-start | bytes 1572868
  192.6 2.4 %collective-permute-start.29 = (f32[256,512]{1,0:T(8,128)S(1)}, f32[256,512]{1,0:T(8,128)S(1)}, u32[]{:S(2)}, u32[]{:S(2)}) collective-permute-start(f32[256,512]{1,0:T(8,128)S(1)} %collective-permute-done.28.refs_2_), channel_id=1, source_target_pairs={{0,1},{1,0},{2,3},{3,2},{4,5},{5,4},{6,7},{7,6},{8,9},{9,8},{10,11... | collective-permute-start | bytes 1572872 | tf_op jit(solution)/shard_map/ppermute | solution.py:215
  193.5 1.6 copy-start.33
  195.0 1.1 copy-start.11
  195.0 1.3 copy-start.13
  (9 other events, 7.8 us)

commit v2 on v0

v2 whole, which is shorter than its diff:
```python
import jax
import jax.numpy as jnp
from jax import lax
from jax.experimental import pallas as pl
from jax.experimental.pallas import tpu as pltpu
from jax.sharding import PartitionSpec as P

D = 512
ROWS = 64
HALF = 256
AUG = D + 8
NN = (((1,), (0,)), ((), ()))
NT = (((1,), (1,)), ((), ()))
VMEM = pl.BlockSpec(memory_space=pltpu.VMEM)
F32 = jnp.float32
BF16 = jnp.bfloat16


def full(*dims):
    return jax.ShapeDtypeStruct(dims, F32)


def part(*dims):
    return jax.ShapeDtypeStruct(dims, BF16)


def split(a):
    high = a.astype(BF16)
    return high, (a - high.astype(F32)).astype(BF16)


def dot(a, b, dims):
    return lax.dot_general(a, b, dims, preferred_element_type=F32)


def dot3(a, b, dims):
    return dot(a[0], b[0], dims) + (dot(a[0], b[1], dims) + dot(a[1], b[0], dims))


def call(kernel, name, outs, args, scratch=(), products=4, mib=24):
    return pl.pallas_call(
        kernel,
        out_shape=outs,
        in_specs=[VMEM] * len(args),
        out_specs=[VMEM] * len(outs),
        scratch_shapes=list(scratch),
        compiler_params=pltpu.CompilerParams(vmem_limit_bytes=mib << 20),
        cost_estimate=pl.CostEstimate(
            flops=products * 0, bytes_accessed=0, transcendentals=0
        ),
        name=name,
    )(*args)


def position():
    panel, block = lax.axis_index("panel"), lax.axis_index("tm")
    return panel // 2, panel % 2, block % 4


def own_rows(size=ROWS):
    return pl.ds(pl.multiple_of(lax.axis_index("panel") * size, size), size)


def places(mine, c):
    toward = 1 - 2 * c
    own = [mine, mine - toward, mine + toward, mine + 2]
    other = [mine, mine + toward, mine - toward, mine + 2]
    return [((place + 4) % 4, c) for place in own] + [((place + 4) % 4, 1 - c) for place in other]


def panels(z, c):
    return [2 * place + core for place, core in places(z, c)]


def at(panel, size=ROWS):
    return pl.ds(pl.multiple_of(panel * size, size), size)


def block_kernel(*refs):
    pieces, (e_hi, e_lo), suffix, (half, token, total) = refs[:8], refs[8:10], refs[10:18], refs[18:]
    z, c, _ = position()
    for piece, panel in zip(pieces, panels(z, c)):
        for k in range(4):
            high, low = split(piece[k * ROWS : (k + 1) * ROWS, :])
            to_hi, to_lo = (e_hi.at[k], e_lo.at[k]) if k < 3 else suffix[6:8]
            to_hi[at(panel), :] = high
            to_lo[at(panel), :] = low
    for k in (2, 1, 0):
        product = dot3((e_hi[k], e_lo[k]), (suffix[2 * k + 2][...], suffix[2 * k + 3][...]), NN)
        suffix[2 * k][...], suffix[2 * k + 1][...] = split(product)
    total[...] = product
    half[...] = total[at(c, HALF), :]
    token[...] = jnp.zeros((8, 128), F32)


def pack_kernel(noise, offsets, token, packed):
    packed[:HALF, :] = noise[...]
    packed[HALF:, :] = jnp.zeros((8, D), F32) + token[0:8, 0:1]
    for panel in range(8):

        @pl.when(lax.axis_index("panel") == panel)
        def _():
            packed[HALF : HALF + 4, panel * ROWS : (panel + 1) * ROWS] = offsets[...]


def congruence(gain, cov, scratch):
    scratch[:D, :] = dot3(gain, split(cov[:D, :]), NN)
    scratch[D:, :] = cov[D:, :]
    return dot3(split(scratch[...]), gain, NT)


def noise_kernel(e_hi, e_lo, *refs):
    pieces, (rows_out, means_out, whole, mine, scratch) = refs[:8], refs[8:]
    z, c, _ = position()
    offsets = sum(piece[HALF:, :] for piece in pieces)
    row = lax.broadcasted_iota(jnp.int32, (8, D), 0)
    means_out[...] = jnp.zeros((8, D), F32)
    for k in (3, 2, 1, 0):
        if k == 3:
            whole[...] = jnp.zeros((AUG, D), F32)
        else:
            whole[...] = congruence((e_hi[k], e_lo[k]), whole[...], scratch)
        for piece, panel in zip(pieces, panels(z, c)):
            whole[at(panel), :] += piece[k * ROWS : (k + 1) * ROWS, :]
        offset = jnp.sum(jnp.where(row == k, offsets, 0.0), axis=0, keepdims=True)
        whole[D:, :] += jnp.where(row == 0, offset, 0.0)
        rows_out[k] = whole[own_rows(), :]
        means_out[k : k + 1, :] = whole[D : D + 1, :]
    mine[:ROWS, :] = whole[own_rows(), :]
    mine[ROWS:, :] = whole[D:, :]


def gather_gains(own_hi, own_lo, pieces, a_hi, a_lo):
    _, c, y = position()
    a_hi[y] = own_hi[...]
    a_lo[y] = own_lo[...]
    rest = [spot for index, spot in enumerate(places(y, c)) if index % 4]
    for piece, (block, core) in zip(pieces, rest):
        high, low = split(piece[...])
        a_hi[block, at(core, HALF), :] = high
        a_lo[block, at(core, HALF), :] = low


def eye_parts():
    same = lax.broadcasted_iota(jnp.int32, (D, D), 0) == lax.broadcasted_iota(jnp.int32, (D, D), 1)
    return jnp.where(same, 1.0, 0.0).astype(BF16), jnp.zeros((D, D), BF16)


def rows_congruence(left, right, cov, scratch):
    scratch[:ROWS, :] = dot3(left, split(cov[:D, :]), NN)
    scratch[ROWS:, :] = cov[D:, :]
    return dot3(split(scratch[...]), right, NT)


def prefix_kernel(*refs):
    blocks, (f_hi, f_lo, gain, a_hi, a_lo) = refs[:8], refs[8:]
    y = position()[2]
    gather_gains(blocks[0], blocks[1], blocks[2:], a_hi, a_lo)

    @pl.when(y == 0)
    def _():
        f_hi[...], f_lo[...] = eye_parts()

    head = (a_hi[0], a_lo[0])
    for block in (1, 2, 3):

        @pl.when(y == block)
        def _():
            f_hi[...], f_lo[...] = head

        if block < 3:
            head = split(dot3(head, (a_hi[block], a_lo[block]), NN))
    a_hi[0], a_lo[0] = head
    gain[...] = dot3((a_hi[0, own_rows(), :], a_lo[0, own_rows(), :]), (a_hi[3], a_lo[3]), NN)


def term_kernel(f_hi, f_lo, cov, term, short):
    term[...] = rows_congruence(
        (f_hi[own_rows(), :], f_lo[own_rows(), :]), (f_hi[...], f_lo[...]), cov[...], short
    )


def later_kernel(cov, *refs):
    blocks, (p_hi, p_lo, second, third, a_hi, a_lo, short) = refs[:8], refs[8:]
    y = position()[2]
    gather_gains(blocks[0], blocks[1], blocks[2:], a_hi, a_lo)

    before = (y + 3) % 4
    gain = (a_hi[before], a_lo[before])
    second[...] = rows_congruence((a_hi[before, own_rows(), :], a_lo[before, own_rows(), :]), gain, cov[...], short)
    twice = (y + 2) % 4
    p_hi[...], p_lo[...] = split(dot3((a_hi[twice], a_lo[twice]), gain, NN))
    third[...] = rows_congruence(
        (p_hi[own_rows(), :], p_lo[own_rows(), :]), (p_hi[...], p_lo[...]), cov[...], short
    )

    @pl.when(y == 3)
    def _():
        p_hi[...], p_lo[...] = eye_parts()

    tail = (a_hi[3], a_lo[3])
    for block in (2, 1, 0):

        @pl.when(y == block)
        def _():
            p_hi[...], p_lo[...] = tail

        if block > 0:
            tail = split(dot3((a_hi[block], a_lo[block]), tail, NN))


def outer_kernel(p_hi, p_lo, *refs):
    suffix, pieces, (b_hi, b_lo, x_hi, x_lo, base, gains, later, s_hi, s_lo) = refs[:8], refs[8:16], refs[16:]
    z, c, _ = position()
    for piece, panel in zip(pieces, panels(z, c)):
        gains[0, at(panel), :] = piece[:ROWS, :]
        gains[1, at(panel), :] = piece[ROWS : 2 * ROWS, :]
        later[at(panel), :] = piece[2 * ROWS : 3 * ROWS, :]
    for k in range(4):
        s_hi[k * ROWS : (k + 1) * ROWS, :] = suffix[2 * k][own_rows(), :]
        s_lo[k * ROWS : (k + 1) * ROWS, :] = suffix[2 * k + 1][own_rows(), :]
    steps = (s_hi[...], s_lo[...])
    base[:HALF, :] = dot3(steps, split(later[...]), NN)
    base[HALF:, :] = pieces[0][3 * ROWS :, :]
    b_hi[0], b_lo[0] = p_hi[...], p_lo[...]
    x_hi[0], x_lo[0] = split(dot3(steps, (p_hi[...], p_lo[...]), NN))
    for index in range(2):
        gain = split(gains[index])
        b_hi[index + 1], b_lo[index + 1] = split(dot3((b_hi[index], b_lo[index]), gain, NN))
        x_hi[index + 1], x_lo[index + 1] = split(dot3((x_hi[index], x_lo[index]), gain, NN))


def final_kernel(b_hi, b_lo, x_hi, x_lo, base, rows_in, means_in, *refs):
    suffix, pieces, (out, means, cov, stack, short, every) = refs[:8], refs[8:16], refs[16:]
    z, c, _ = position()
    inner = base[...]
    for index in range(3):
        for piece, panel in zip(pieces, panels(z, c)):
            cov[at(panel), :] = piece[index * 72 : index * 72 + ROWS, :]
        stack[:HALF, :] = dot3((x_hi[index], x_lo[index]), split(cov[...]), NN)
        stack[HALF:, :] = pieces[0][index * 72 + ROWS : index * 72 + 72, :]
        inner = inner + dot3(split(stack[...]), (b_hi[index], b_lo[index]), NT)
    stack[...] = inner
    for k in range(4):
        short[:ROWS, :] = stack[k * ROWS : (k + 1) * ROWS, :]
        short[ROWS:, :] = stack[HALF:, :]
        result = dot3(split(short[...]), (suffix[2 * k][...], suffix[2 * k + 1][...]), NT)
        out[k] = result[:ROWS, :] + rows_in[k]
        every[k : k + 1, :] = result[ROWS : ROWS + 1, :] + means_in[k : k + 1, :]
    for panel in range(8):

        @pl.when(lax.axis_index("panel") == panel)
        def _():
            means[...] = every[:4, panel * ROWS : (panel + 1) * ROWS]


def per_device(transitions, offsets, noise_cov):
    def other_core(value):
        return lax.ppermute(value, "panel", [(2 * z + c, 2 * z + 1 - c) for z in range(4) for c in range(2)])

    def along_y(value, step):
        return lax.ppermute(
            value, "tm", [(4 * x + y, 4 * x + (y + step) % 4) for x in range(4) for y in range(4)]
        )

    def back_y(value, step):
        return lax.ppermute(
            value, "tm", [(4 * x + y, 4 * x + y - step) for x in range(4) for y in range(step, 4)]
        )

    def back_x(value, step):
        return lax.ppermute(
            value, "tm", [(4 * x + y, 4 * (x - step) + y) for x in range(step, 4) for y in range(4)]
        )

    def paired_z(value, step):
        return lax.ppermute(
            value, "panel", [(2 * z + c, 2 * ((z + step * (1 - 2 * c)) % 4) + c) for z in range(4) for c in range(2)]
        )

    def paired_y(value, step):
        pairs = []
        for x in range(4):
            for y in range(4):
                for panel in range(8):
                    to = 4 * x + (y + step * (1 - 2 * (panel % 2))) % 4
                    pairs.append((8 * (4 * x + y) + panel, 8 * to + panel))
        return lax.ppermute(value, ("tm", "panel"), pairs)

    def exchange(value, paired):
        first = paired(value, 1)
        return [first, paired(value, -1), paired(first, 1)]

    def both_cores(pieces):
        return pieces + [other_core(piece) for piece in pieces]

    def whole_z(value):
        return both_cores([value] + exchange(value, paired_z))

    noise_rows = noise_cov.reshape(HALF, D)
    steps = whole_z(transitions.reshape(HALF, D))
    e_hi, e_lo, *rest = call(
        block_kernel,
        "block",
        [part(3, D, D)] * 2 + [part(D, D)] * 8 + [full(HALF, D), full(8, 128)],
        steps,
        [pltpu.VMEM((D, D), F32)],
        products=3,
    )
    suffix, (half, token) = rest[:8], rest[8:]
    blocks = [suffix[0], suffix[1], *both_cores(exchange(half, paired_y))]
    (noise,) = call(pack_kernel, "pack", [full(HALF + 8, D)], [noise_rows, offsets, token], products=0)
    noises = whole_z(noise)
    rows, means, cov, mine = call(
        noise_kernel,
        "noise",
        [full(4, ROWS, D), full(8, D), full(AUG, D), full(ROWS + 8, D)],
        [e_hi, e_lo, *noises],
        [pltpu.VMEM((AUG, D), F32)],
        products=6,
    )
    f_hi, f_lo, gain = call(
        prefix_kernel,
        "prefix",
        [part(D, D), part(D, D), full(ROWS, D)],
        blocks,
        [pltpu.VMEM((4, D, D), BF16), pltpu.VMEM((4, D, D), BF16)],
        products=3,
    )
    (term,) = call(
        term_kernel,
        "term",
        [full(ROWS + 8, D)],
        [f_hi, f_lo, cov],
        [pltpu.VMEM((ROWS + 8, D), F32)],
        products=1,
    )
    total = term + along_y(term, 1) + along_y(term, 2) + along_y(term, 3)
    p_hi, p_lo, second, third = call(
        later_kernel,
        "later",
        [part(D, D), part(D, D), full(ROWS + 8, D), full(ROWS + 8, D)],
        [cov, *blocks],
        [pltpu.VMEM((4, D, D), BF16), pltpu.VMEM((4, D, D), BF16), pltpu.VMEM((ROWS + 8, D), F32)],
        products=4,
    )
    beyond = back_y(mine, 1) + back_y(second, 2) + back_y(third, 3)
    outer = whole_z(jnp.concatenate([back_x(gain, 1), back_x(gain, 2), beyond], axis=0))
    covs = whole_z(jnp.concatenate([back_x(total, 1), back_x(total, 2), back_x(total, 3)], axis=0))
    b_hi, b_lo, x_hi, x_lo, base = call(
        outer_kernel,
        "outer",
        [part(3, D, D), part(3, D, D), part(3, HALF, D), part(3, HALF, D), full(HALF + 8, D)],
        [p_hi, p_lo, *suffix, *outer],
        [
            pltpu.VMEM((2, D, D), F32),
            pltpu.VMEM((D, D), F32),
            pltpu.VMEM((HALF, D), BF16),
            pltpu.VMEM((HALF, D), BF16),
        ],
        products=4,
    )
    out, mean_rows = call(
        final_kernel,
        "final",
        [full(4, ROWS, D), full(4, ROWS)],
        [b_hi, b_lo, x_hi, x_lo, base, rows, means, *suffix, *covs],
        [
            pltpu.VMEM((D, D), F32),
            pltpu.VMEM((HALF + 8, D), F32),
            pltpu.VMEM((ROWS + 8, D), F32),
            pltpu.VMEM((8, D), F32),
        ],
        products=5,
    )
    return mean_rows, out


def solution(mesh):
    placed = (P("tm", "panel", None), P("tm", "panel"), P("tm", "panel", None))
    return jax.shard_map(
        per_device,
        mesh=mesh,
        in_specs=placed,
        out_specs=(P("tm", "panel"), P("tm", "panel", None)),
        check_vma=False,
    )
```

time: 739 us -> 153 us (0.21)
  waiting for transfers between devices: 410 us -> 58.9 us
  matrix products: 186 us -> 0 us
  blocking collectives: 105 us -> 0 us
  starting transfers between devices: 0.54 us -> 62.1 us
  Pallas kernels: 0 us -> 29.2 us
  local copies, waits for them, and re-layouts: 15.3 us -> 1.08 us
  between operations: 14.6 us -> 0.96 us
    all_gather x14 -> x0, waiting for transfers between devices: 406 us -> none  [the longest x2 192 us: prefix(): everything = jax.tree.map(lambda part: lax.all_gather(part, axis), array)]
    dot_general x72 -> x0, matrix products: 186 us -> none  [product(): jnp.dot(left, right, precision=lax.Precision.HIGHEST, preferred_element_t...]
    while x6 -> x0, blocking collectives: 72.6 us -> none
    ppermute x0 -> x45, starting transfers between devices: none -> 62.1 us  [the longest x19 27.2 us: other_core(): lax.ppermute(value, 'panel', [(2 * z + c, 2 * z + 1 - c) for z in range(4...]
    ppermute x0 -> x45, waiting for transfers between devices: none -> 58.9 us  [the longest x12 27.7 us: paired_z(): lax.ppermute(value, 'panel', [(2 * z + c, 2 * ((z + step * (1 - 2 * c)) %...]
    pallas_call x0 -> x8, Pallas kernels: none -> 29.2 us  [call(): pl.pallas_call(kernel, out_shape=outs, in_specs=[VMEM] * len(args), out_s...]
    all_gather x1 -> x0, blocking collectives: 20.2 us -> none  [prefix(): everything = jax.tree.map(lambda part: lax.all_gather(part, axis), array)]
    unnamed x1 -> x0, blocking collectives: 12 us -> none
  transfers between devices with their start and end apart: 14 -> 45, of which waited for: 14 -> 15; matrix products, arithmetic and copies ran while one was open for 4% -> 0% of each run, Pallas kernels for 0% -> 8%
where the time goes in v2:
time: 153 us; the launch traced here: 152 us
  starting transfers between devices  62.1 us (41%)
  waiting for transfers between devices  58.9 us (38%)
  Pallas kernels  29.2 us (19%)
    pallas_call x8, Pallas kernels, call(): pl.pallas_call(kernel, out_shape=outs, in_specs=[VMEM] * len(args), out_s...  29.2 us
    ppermute x12, waiting for transfers between devices, paired_z(): lax.ppermute(value, 'panel', [(2 * z + c, 2 * ((z + step * (1 - 2 * c)) %...  27.7 us
    ppermute x19, starting transfers between devices, other_core(): lax.ppermute(value, 'panel', [(2 * z + c, 2 * z + 1 - c) for z in range(4...  27.2 us
    ppermute x12, starting transfers between devices, paired_z(): lax.ppermute(value, 'panel', [(2 * z + c, 2 * ((z + step * (1 - 2 * c)) %...  14.9 us
    ppermute x3, waiting for transfers between devices, paired_y(): return lax.ppermute(value, ('tm', 'panel'), pairs)  9.93 us
    ppermute x5, waiting for transfers between devices, back_x(): lax.ppermute(value, 'tm', [(4 * x + y, 4 * (x - step) + y) for x in range...  9.87 us
    ppermute x19, waiting for transfers between devices, other_core(): lax.ppermute(value, 'panel', [(2 * z + c, 2 * z + 1 - c) for z in range(4...  7.43 us
    ppermute x5, starting transfers between devices, back_x(): lax.ppermute(value, 'tm', [(4 * x + y, 4 * (x - step) + y) for x in range...  6.43 us
  transfers between devices with their start and end apart: 45, of which 15 were waited for; matrix products, arithmetic and copies ran while one was open for 0% of the time, Pallas kernels for 8%

profile of v2, /device:TPU:1, one launch (start us, length us, event | category | flops | bytes accessed | tf_op | source)
XLA Modules:
  0.0 152.4 jit_solution(17462021787109874396)
XLA Ops:
  0.6 4.7 %collective-permute-start = (f32[256,512]{1,0:T(8,128)}, f32[256,512]{1,0:T(8,128)S(1)}, u32[]{:S(2)}, u32[]{:S(2)}) collective-permute-start(f32[256,512]{1,0:T(8,128)} %bitcast.3), channel_id=1, source_target_pairs={{0,2},{1,7},{2,4},{3,1},{4,6},{5,3},{6,0},{7,5},{8,10},{9,15},{10,... | collective-permute-start | bytes 1572872 | tf_op jit(solution)/shard_map/ppermute | solution.py:277
  5.3 0.0 collective-permute-start.1
  5.3 10.8 %collective-permute-done.refs_1_ = f32[256,512]{1,0:T(8,128)S(1)} collective-permute-done((f32[256,512]{1,0:T(8,128)}, f32[256,512]{1,0:T(8,128)S(1)}, u32[]{:S(2)}, u32[]{:S(2)}) %collective-permute-start) | collective-permute-done | bytes 524320 | tf_op jit(solution)/shard_map/ppermute | solution.py:277
  16.1 3.3 %collective-permute-start.2 = (f32[256,512]{1,0:T(8,128)S(1)}, f32[256,512]{1,0:T(8,128)S(1)}, u32[]{:S(2)}, u32[]{:S(2)}) collective-permute-start(f32[256,512]{1,0:T(8,128)S(1)} %collective-permute-done.refs_1_), channel_id=1, source_target_pairs={{0,2},{1,7},{2,4},{3,1},{4,6},{5,3},{6,0},{7,5},{8,10},{9,15},{10,... | collective-permute-start | bytes 1572872 | tf_op jit(solution)/shard_map/ppermute | solution.py:277
  19.4 0.5 collective-permute-start.4
  19.9 0.0 collective-permute-done.1.refs_2_
  19.9 0.0 collective-permute-start.5
  19.9 5.6 %collective-permute-done.2.refs_3_ = f32[256,512]{1,0:T(8,128)S(1)} collective-permute-done((f32[256,512]{1,0:T(8,128)S(1)}, f32[256,512]{1,0:T(8,128)S(1)}, u32[]{:S(2)}, u32[]{:S(2)}) %collective-permute-start.2) | collective-permute-done | bytes 524320 | tf_op jit(solution)/shard_map/ppermute | solution.py:277
  25.5 2.2 %collective-permute-start.6 = (f32[256,512]{1,0:T(8,128)S(1)}, f32[256,512]{1,0:T(8,128)S(1)}, u32[]{:S(2)}, u32[]{:S(2)}) collective-permute-start(f32[256,512]{1,0:T(8,128)S(1)} %collective-permute-done.2.refs_3_), channel_id=1, source_target_pairs={{0,1},{1,0},{2,3},{3,2},{4,5},{5,4},{6,7},{7,6},{8,9},{9,8},{10,11... | collective-permute-start | bytes 1572872 | tf_op jit(solution)/shard_map/ppermute | solution.py:259
  27.8 1.5 %collective-permute-done.6.refs_7_ = f32[256,512]{1,0:T(8,128)S(1)} collective-permute-done((f32[256,512]{1,0:T(8,128)S(1)}, f32[256,512]{1,0:T(8,128)S(1)}, u32[]{:S(2)}, u32[]{:S(2)}) %collective-permute-start.6) | collective-permute-done | bytes 524320 | tf_op jit(solution)/shard_map/ppermute | solution.py:259
  29.3 1.0 copy-done.1
  30.3 3.6 %block.1 = (bf16[3,512,512]{2,1,0:T(8,128)(2,1)S(1)}, bf16[3,512,512]{2,1,0:T(8,128)(2,1)S(1)}, bf16[512,512]{1,0:T(8,128)(2,1)S(1)}, bf16[512,512]{1,0:T(8,128)...) custom-call(f32[256,512]{1,0:T(8,128)S(1)} %bitcast.6, ...), custom_call_target="tpu_custom_call" | custom-call | tf_op jit(solution)/shard_map/block/pallas_call | solution.py:41
  34.0 0.1 pack.1.refs_0_
  34.1 1.4 collective-permute-start.7
  35.5 2.7 %collective-permute-start.14 = (f32[256,512]{1,0:T(8,128)S(1)}, f32[256,512]{1,0:T(8,128)S(1)}, u32[]{:S(2)}, u32[]{:S(2)}) collective-permute-start(f32[256,512]{1,0:T(8,128)S(1)} %get-tuple-element.38), channel_id=1, source_target_pairs={{0,8},{1,25},{2,10},{3,27},{4,12},{5,29},{6,14},{7,31},{8,16},{9,1... | collective-permute-start | bytes 1572872 | tf_op jit(solution)/shard_map/ppermute | solution.py:288
  38.3 0.1 collective-permute-start.8
  38.3 5.9 %collective-permute-done.7.refs_1_ = f32[264,512]{1,0:T(8,128)S(1)} collective-permute-done((f32[264,512]{1,0:T(8,128)S(1)}, f32[264,512]{1,0:T(8,128)S(1)}, u32[]{:S(2)}, u32[]{:S(2)}) %collective-permute-start.7) | collective-permute-done | bytes 540704 | tf_op jit(solution)/shard_map/ppermute | solution.py:277
  44.2 1.1 collective-permute-start.9
  45.3 4.4 %collective-permute-done.14.refs_2_ = f32[256,512]{1,0:T(8,128)S(1)} collective-permute-done((f32[256,512]{1,0:T(8,128)S(1)}, f32[256,512]{1,0:T(8,128)S(1)}, u32[]{:S(2)}, u32[]{:S(2)}) %collective-permute-start.14) | collective-permute-done | bytes 524320 | tf_op jit(solution)/shard_map/ppermute | solution.py:288
  49.7 3.1 %collective-permute-start.16 = (f32[256,512]{1,0:T(8,128)S(1)}, f32[256,512]{1,0:T(8,128)S(1)}, u32[]{:S(2)}, u32[]{:S(2)}) collective-permute-start(f32[256,512]{1,0:T(8,128)S(1)} %collective-permute-done.14.refs_2_), channel_id=1, source_target_pairs={{0,8},{1,25},{2,10},{3,27},{4,12},{5,29},{6,14},{7,31},{8,16},{9,1... | collective-permute-start | bytes 1572872 | tf_op jit(solution)/shard_map/ppermute | solution.py:288
  52.9 0.5 collective-permute-start.18
  53.4 0.1 collective-permute-start.10
  53.5 5.5 %collective-permute-done.16.refs_4_ = f32[256,512]{1,0:T(8,128)S(1)} collective-permute-done((f32[256,512]{1,0:T(8,128)S(1)}, f32[256,512]{1,0:T(8,128)S(1)}, u32[]{:S(2)}, u32[]{:S(2)}) %collective-permute-start.16) | collective-permute-done | bytes 524320 | tf_op jit(solution)/shard_map/ppermute | solution.py:288
  59.0 0.5 collective-permute-start.12
  59.5 0.1 collective-permute-start.13
  59.6 0.4 collective-permute-start.19
  60.0 3.2 %collective-permute-done.19.refs_7_ = f32[256,512]{1,0:T(8,128)S(1)} collective-permute-done((f32[256,512]{1,0:T(8,128)S(1)}, f32[256,512]{1,0:T(8,128)S(1)}, u32[]{:S(2)}, u32[]{:S(2)}) %collective-permute-start.19) | collective-permute-done | bytes 524320 | tf_op jit(solution)/shard_map/ppermute | solution.py:259
  63.2 3.4 %prefix.1 = (bf16[512,512]{1,0:T(8,128)(2,1)S(1)}, bf16[512,512]{1,0:T(8,128)(2,1)S(1)}, f32[64,512]{1,0:T(8,128)S(1)}) custom-call(bf16[512,512]{1,0:T(8,128)(2,1)S(1)} %get-tuple-element.36.refs_0_, bf16[512,512]{1,0:T(8,128)(2,1)S(1)} %get-tuple-element.37.refs_1_, f32[256,512]{1,0:T(8,128)S(1)} %collective-permute-done.14.refs_2_, ...), custom_call_target="tpu_custom_call" | custom-call | tf_op jit(solution)/shard_map/prefix/pallas_call | solution.py:41
  66.7 6.0 %noise.1 = (f32[4,64,512]{2,1,0:T(8,128)S(1)}, f32[8,512]{1,0:T(8,128)S(1)}, f32[520,512]{1,0:T(8,128)S(1)}, f32[72,512]{1,0:T(8,128)S(1)}) custom-call(bf16[3,512,512]{2,1,0:T(8,128)(2,1)S(1)} %get-tuple-element.32.e_hi, bf16[3,512,512]{2,1,0:T(8,128)(2,1)S(1)} %get-tuple-element.33.e_lo, f32[264,512]{1,0:T(8,128)S(1)} %pack.1.refs_0_, ...), custom_call_target="tpu_custom_call" | custom-call | tf_op jit(solution)/shard_map/noise/pallas_call | solution.py:41
  72.7 0.9 term.1
  73.6 3.2 %collective-permute-start.34 = (f32[72,512]{1,0:T(8,128)S(1)}, f32[72,512]{1,0:T(8,128)S(1)}, u32[]{:S(2)}, u32[]{:S(2)}) collective-permute-start(f32[72,512]{1,0:T(8,128)S(1)} %term.1), channel_id=1, source_target_pairs={{0,24},{8,0},{16,8},{24,16},{32,56},{40,32},{48,40},{56,48},{64,88... | collective-permute-start | bytes 442376 | tf_op jit(solution)/shard_map/ppermute | solution.py:262
  76.9 0.7 collective-permute-start.32
  77.5 1.3 collective-permute-start.21
  78.8 1.3 collective-permute-start.20
  80.1 5.7 %later.1 = (bf16[512,512]{1,0:T(8,128)(2,1)S(1)}, bf16[512,512]{1,0:T(8,128)(2,1)S(1)}, f32[72,512]{1,0:T(8,128)S(1)}, f32[72,512]{1,0:T(8,128)S(1)}) custom-call(f32[520,512]{1,0:T(8,128)S(1)} %get-tuple-element.35.cov, bf16[512,512]{1,0:T(8,128)(2,1)S(1)} %get-tuple-element.36.refs_0_, bf16[512,512]{1,0:T(8,128)(2,1)S(1)} %get-tuple-element.37.refs_1_, ...), custom_call_target="tpu_custom_call" | custom-call | tf_op jit(solution)/shard_map/later/pallas_call | solution.py:41
  85.8 1.3 collective-permute-start.24
  87.1 1.3 collective-permute-start.22
  88.4 1.3 collective-permute-start.23
  89.8 3.8 %collective-permute-done.24 = f32[72,512]{1,0:T(8,128)S(1)} collective-permute-done((f32[72,512]{1,0:T(8,128)S(1)}, f32[72,512]{1,0:T(8,128)S(1)}, u32[]{:S(2)}, u32[]{:S(2)}) %collective-permute-start.24) | collective-permute-done | bytes 147488 | tf_op jit(solution)/shard_map/ppermute | solution.py:267
  93.6 1.3 collective-permute-start.35
  94.9 1.3 collective-permute-start.36
  96.2 0.2 collective-permute-done.23
  96.4 1.3 collective-permute-start.37
  97.7 2.0 %collective-permute-done.35 = f32[72,512]{1,0:T(8,128)S(1)} collective-permute-done((f32[72,512]{1,0:T(8,128)S(1)}, f32[72,512]{1,0:T(8,128)S(1)}, u32[]{:S(2)}, u32[]{:S(2)}) %collective-permute-start.35) | collective-permute-done | bytes 147488 | tf_op jit(solution)/shard_map/ppermute | solution.py:272
  99.8 3.5 %collective-permute-done.36 = f32[72,512]{1,0:T(8,128)S(1)} collective-permute-done((f32[72,512]{1,0:T(8,128)S(1)}, f32[72,512]{1,0:T(8,128)S(1)}, u32[]{:S(2)}, u32[]{:S(2)}) %collective-permute-start.36) | collective-permute-done | bytes 147488 | tf_op jit(solution)/shard_map/ppermute | solution.py:272
  103.2 4.4 %collective-permute-done.37 = f32[72,512]{1,0:T(8,128)S(1)} collective-permute-done((f32[72,512]{1,0:T(8,128)S(1)}, f32[72,512]{1,0:T(8,128)S(1)}, u32[]{:S(2)}, u32[]{:S(2)}) %collective-permute-start.37) | collective-permute-done | bytes 147488 | tf_op jit(solution)/shard_map/ppermute | solution.py:272
  107.6 0.1 collective-permute-start.38
  107.8 0.1 collective-permute-start.25
  107.8 1.5 collective-permute-start.26
  109.3 6.2 %collective-permute-start.28 = (f32[200,512]{1,0:T(8,128)S(1)}, f32[200,512]{1,0:T(8,128)S(1)}, u32[]{:S(2)}, u32[]{:S(2)}) collective-permute-start(f32[200,512]{1,0:T(8,128)S(1)} %pad_maximum_fusion.refs_8_), channel_id=1, source_target_pairs={{0,1},{1,0},{2,3},{3,2},{4,5},{5,4},{6,7},{7,6},{8,9},{9,8},{10,11... | collective-permute-start | bytes 1228808 | tf_op jit(solution)/shard_map/ppermute | solution.py:259
  115.6 0.2 collective-permute-start.39
  115.8 2.4 %collective-permute-start.40 = (f32[216,512]{1,0:T(8,128)S(1)}, f32[216,512]{1,0:T(8,128)S(1)}, u32[]{:S(2)}, u32[]{:S(2)}) collective-permute-start(f32[216,512]{1,0:T(8,128)S(1)} %collective-permute-done.38.refs_9_), channel_id=1, source_target_pairs={{0,2},{1,7},{2,4},{3,1},{4,6},{5,3},{6,0},{7,5},{8,10},{9,15},{10,... | collective-permute-start | bytes 1327112 | tf_op jit(solution)/shard_map/ppermute | solution.py:277
  118.2 3.5 %collective-permute-done.25.refs_9_ = f32[200,512]{1,0:T(8,128)S(1)} collective-permute-done((f32[200,512]{1,0:T(8,128)S(1)}, f32[200,512]{1,0:T(8,128)S(1)}, u32[]{:S(2)}, u32[]{:S(2)}) %collective-permute-start.25) | collective-permute-done | bytes 409632 | tf_op jit(solution)/shard_map/ppermute | solution.py:277
  121.8 9.2 %collective-permute-start.29 = (f32[200,512]{1,0:T(8,128)S(1)}, f32[200,512]{1,0:T(8,128)S(1)}, u32[]{:S(2)}, u32[]{:S(2)}) collective-permute-start(f32[200,512]{1,0:T(8,128)S(1)} %collective-permute-done.25.refs_9_), channel_id=1, source_target_pairs={{0,1},{1,0},{2,3},{3,2},{4,5},{5,4},{6,7},{7,6},{8,9},{9,8},{10,11... | collective-permute-start | bytes 1228808 | tf_op jit(solution)/shard_map/ppermute | solution.py:259
  131.0 0.1 collective-permute-start.30
  131.1 4.8 %collective-permute-start.41 = (f32[216,512]{1,0:T(8,128)S(1)}, f32[216,512]{1,0:T(8,128)S(1)}, u32[]{:S(2)}, u32[]{:S(2)}) collective-permute-start(f32[216,512]{1,0:T(8,128)S(1)} %constant_dynamic-update-slice_fusion.refs_8_), channel_id=1, source_target_pairs={{0,1},{1,0},{2,3},{3,2},{4,5},{5,4},{6,7},{7,6},{8,9},{9,8},{10,11... | collective-permute-start | bytes 1327112 | tf_op jit(solution)/shard_map/ppermute | solution.py:259
  135.9 1.9 %collective-permute-done.27.refs_11_ = f32[200,512]{1,0:T(8,128)S(1)} collective-permute-done((f32[200,512]{1,0:T(8,128)S(1)}, f32[200,512]{1,0:T(8,128)S(1)}, u32[]{:S(2)}, u32[]{:S(2)}) %collective-permute-start.27) | collective-permute-done | bytes 409632 | tf_op jit(solution)/shard_map/ppermute | solution.py:277
  137.8 1.9 %collective-permute-start.42 = (f32[216,512]{1,0:T(8,128)S(1)}, f32[216,512]{1,0:T(8,128)S(1)}, u32[]{:S(2)}, u32[]{:S(2)}) collective-permute-start(f32[216,512]{1,0:T(8,128)S(1)} %collective-permute-done.38.refs_9_), channel_id=1, source_target_pairs={{0,1},{1,0},{2,3},{3,2},{4,5},{5,4},{6,7},{7,6},{8,9},{9,8},{10,11... | collective-permute-start | bytes 1327112 | tf_op jit(solution)/shard_map/ppermute | solution.py:259
  139.6 0.0 collective-permute-start.43
  139.7 0.5 collective-permute-start.44
  140.2 0.1 collective-permute-start.31
  140.2 2.7 %collective-permute-done.31.refs_15_ = f32[200,512]{1,0:T(8,128)S(1)} collective-permute-done((f32[200,512]{1,0:T(8,128)S(1)}, f32[200,512]{1,0:T(8,128)S(1)}, u32[]{:S(2)}, u32[]{:S(2)}) %collective-permute-start.31) | collective-permute-done | bytes 409632 | tf_op jit(solution)/shard_map/ppermute | solution.py:259
  142.9 3.6 %outer.1 = (bf16[3,512,512]{2,1,0:T(8,128)(2,1)S(1)}, bf16[3,512,512]{2,1,0:T(8,128)(2,1)S(1)}, bf16[3,256,512]{2,1,0:T(8,128)(2,1)S(1)}, bf16[3,256,512]{2,1,0:T(8,128)(2,1)S(1)}, f32[264,512]{1,0:T(8,128)S(1)}) custom-call(bf16[512,512]{1,0:T(8,128)(2,1)S(1)} %get-tuple-element.39.p_hi, bf16[512,512]{1,0:T(8,128)(2,1)S(1)} %get-tuple-element.40.p_lo, ...), custom_call_target="tpu_custom_call" | custom-call | tf_op jit(solution)/shard_map/outer/pallas_call | solution.py:41
  146.5 5.9 %final.1 = (f32[4,64,512]{2,1,0:T(8,128)}, f32[4,64]{1,0:T(4,128)}) custom-call(bf16[3,512,512]{2,1,0:T(8,128)(2,1)S(1)} %get-tuple-element.51.b_hi, bf16[3,512,512]{2,1,0:T(8,128)(2,1)S(1)} %get-tuple-element.52.b_lo, bf16[3,256,512]{2,1,0:T(8,128)(2,1)S(1)} %get-tuple-element.53.x_hi, bf16[3,256,512]{2,1,0:T(8,128)(2,1)S(1)} %get-tuple-element.54.x_lo, ...), custom_call_target="tpu_custom_call" | custom-call | tf_op jit(solution)/shard_map/final/pallas_call | solution.py:41
  (46 shorter events, 0.2 us)
Async XLA Ops:
  0.6 33.3 %copy-start = (f32[4,64,512]{2,1,0:T(8,128)S(1)}, f32[4,64,512]{2,1,0:T(8,128)}, u32[]{:S(2)}) copy-start(f32[4,64,512]{2,1,0:T(8,128)} %param.5) | copy-start | bytes 1572868
  0.6 15.5 %collective-permute-start = (f32[256,512]{1,0:T(8,128)}, f32[256,512]{1,0:T(8,128)S(1)}, u32[]{:S(2)}, u32[]{:S(2)}) collective-permute-start(f32[256,512]{1,0:T(8,128)} %bitcast.3), channel_id=1, source_target_pairs={{0,2},{1,7},{2,4},{3,1},{4,6},{5,3},{6,0},{7,5},{8,10},{9,15},{10,... | collective-permute-start | bytes 1572872 | tf_op jit(solution)/shard_map/ppermute | solution.py:277
  5.3 14.6 %collective-permute-start.1 = (f32[256,512]{1,0:T(8,128)}, f32[256,512]{1,0:T(8,128)S(1)}, u32[]{:S(2)}, u32[]{:S(2)}) collective-permute-start(f32[256,512]{1,0:T(8,128)} %bitcast.4), channel_id=1, source_target_pairs={{0,6},{1,3},{2,0},{3,5},{4,2},{5,7},{6,4},{7,1},{8,14},{9,11},{10,... | collective-permute-start | bytes 1572872 | tf_op jit(solution)/shard_map/ppermute | solution.py:277
  16.1 9.4 %collective-permute-start.2 = (f32[256,512]{1,0:T(8,128)S(1)}, f32[256,512]{1,0:T(8,128)S(1)}, u32[]{:S(2)}, u32[]{:S(2)}) collective-permute-start(f32[256,512]{1,0:T(8,128)S(1)} %collective-permute-done.refs_1_), channel_id=1, source_target_pairs={{0,2},{1,7},{2,4},{3,1},{4,6},{5,3},{6,0},{7,5},{8,10},{9,15},{10,... | collective-permute-start | bytes 1572872 | tf_op jit(solution)/shard_map/ppermute | solution.py:277
  19.4 8.3 %collective-permute-start.3 = (f32[256,512]{1,0:T(8,128)}, f32[256,512]{1,0:T(8,128)S(1)}, u32[]{:S(2)}, u32[]{:S(2)}) collective-permute-start(f32[256,512]{1,0:T(8,128)} %bitcast.5), channel_id=1, source_target_pairs={{0,1},{1,0},{2,3},{3,2},{4,5},{5,4},{6,7},{7,6},{8,9},{9,8},{10,11... | collective-permute-start | bytes 1572872 | tf_op jit(solution)/shard_map/ppermute | solution.py:259
  19.4 8.3 %collective-permute-start.4 = (f32[256,512]{1,0:T(8,128)S(1)}, f32[256,512]{1,0:T(8,128)S(1)}, u32[]{:S(2)}, u32[]{:S(2)}) collective-permute-start(f32[256,512]{1,0:T(8,128)S(1)} %collective-permute-done.refs_1_), channel_id=1, source_target_pairs={{0,1},{1,0},{2,3},{3,2},{4,5},{5,4},{6,7},{7,6},{8,9},{9,8},{10,11... | collective-permute-start | bytes 1572872 | tf_op jit(solution)/shard_map/ppermute | solution.py:259
  19.9 7.8 %collective-permute-start.5 = (f32[256,512]{1,0:T(8,128)S(1)}, f32[256,512]{1,0:T(8,128)S(1)}, u32[]{:S(2)}, u32[]{:S(2)}) collective-permute-start(f32[256,512]{1,0:T(8,128)S(1)} %collective-permute-done.1.refs_2_), channel_id=1, source_target_pairs={{0,1},{1,0},{2,3},{3,2},{4,5},{5,4},{6,7},{7,6},{8,9},{9,8},{10,11... | collective-permute-start | bytes 1572872 | tf_op jit(solution)/shard_map/ppermute | solution.py:259
  25.5 3.7 %collective-permute-start.6 = (f32[256,512]{1,0:T(8,128)S(1)}, f32[256,512]{1,0:T(8,128)S(1)}, u32[]{:S(2)}, u32[]{:S(2)}) collective-permute-start(f32[256,512]{1,0:T(8,128)S(1)} %collective-permute-done.2.refs_3_), channel_id=1, source_target_pairs={{0,1},{1,0},{2,3},{3,2},{4,5},{5,4},{6,7},{7,6},{8,9},{9,8},{10,11... | collective-permute-start | bytes 1572872 | tf_op jit(solution)/shard_map/ppermute | solution.py:259
  29.3 1.0 copy-start.1
  30.3 3.6 %copy-start.2 = (f32[4,64]{1,0:T(4,128)S(1)}, f32[4,64]{1,0:T(4,128)}, u32[]{:S(2)}) copy-start(f32[4,64]{1,0:T(4,128)} %offsets.1) | copy-start | bytes 3076
  34.1 10.1 %collective-permute-start.7 = (f32[264,512]{1,0:T(8,128)S(1)}, f32[264,512]{1,0:T(8,128)S(1)}, u32[]{:S(2)}, u32[]{:S(2)}) collective-permute-start(f32[264,512]{1,0:T(8,128)S(1)} %pack.1.refs_0_), channel_id=1, source_target_pairs={{0,2},{1,7},{2,4},{3,1},{4,6},{5,3},{6,0},{7,5},{8,10},{9,15},{10,... | collective-permute-start | bytes 1622024 | tf_op jit(solution)/shard_map/ppermute | solution.py:277
  35.5 14.2 %collective-permute-start.14 = (f32[256,512]{1,0:T(8,128)S(1)}, f32[256,512]{1,0:T(8,128)S(1)}, u32[]{:S(2)}, u32[]{:S(2)}) collective-permute-start(f32[256,512]{1,0:T(8,128)S(1)} %get-tuple-element.38), channel_id=1, source_target_pairs={{0,8},{1,25},{2,10},{3,27},{4,12},{5,29},{6,14},{7,31},{8,16},{9,1... | collective-permute-start | bytes 1572872 | tf_op jit(solution)/shard_map/ppermute | solution.py:288
  38.3 14.6 %collective-permute-start.15 = (f32[256,512]{1,0:T(8,128)S(1)}, f32[256,512]{1,0:T(8,128)S(1)}, u32[]{:S(2)}, u32[]{:S(2)}) collective-permute-start(f32[256,512]{1,0:T(8,128)S(1)} %get-tuple-element.38), channel_id=1, source_target_pairs={{0,24},{1,9},{2,26},{3,11},{4,28},{5,13},{6,30},{7,15},{8,0},{9,17... | collective-permute-start | bytes 1572872 | tf_op jit(solution)/shard_map/ppermute | solution.py:288
  38.3 15.1 %collective-permute-start.8 = (f32[264,512]{1,0:T(8,128)S(1)}, f32[264,512]{1,0:T(8,128)S(1)}, u32[]{:S(2)}, u32[]{:S(2)}) collective-permute-start(f32[264,512]{1,0:T(8,128)S(1)} %pack.1.refs_0_), channel_id=1, source_target_pairs={{0,6},{1,3},{2,0},{3,5},{4,2},{5,7},{6,4},{7,1},{8,14},{9,11},{10,... | collective-permute-start | bytes 1622024 | tf_op jit(solution)/shard_map/ppermute | solution.py:277
  44.2 15.3 %collective-permute-start.9 = (f32[264,512]{1,0:T(8,128)S(1)}, f32[264,512]{1,0:T(8,128)S(1)}, u32[]{:S(2)}, u32[]{:S(2)}) collective-permute-start(f32[264,512]{1,0:T(8,128)S(1)} %collective-permute-done.7.refs_1_), channel_id=1, source_target_pairs={{0,2},{1,7},{2,4},{3,1},{4,6},{5,3},{6,0},{7,5},{8,10},{9,15},{10,... | collective-permute-start | bytes 1622024 | tf_op jit(solution)/shard_map/ppermute | solution.py:277
  49.7 9.3 %collective-permute-start.16 = (f32[256,512]{1,0:T(8,128)S(1)}, f32[256,512]{1,0:T(8,128)S(1)}, u32[]{:S(2)}, u32[]{:S(2)}) collective-permute-start(f32[256,512]{1,0:T(8,128)S(1)} %collective-permute-done.14.refs_2_), channel_id=1, source_target_pairs={{0,8},{1,25},{2,10},{3,27},{4,12},{5,29},{6,14},{7,31},{8,16},{9,1... | collective-permute-start | bytes 1572872 | tf_op jit(solution)/shard_map/ppermute | solution.py:288
  52.9 6.1 %collective-permute-start.17 = (f32[256,512]{1,0:T(8,128)S(1)}, f32[256,512]{1,0:T(8,128)S(1)}, u32[]{:S(2)}, u32[]{:S(2)}) collective-permute-start(f32[256,512]{1,0:T(8,128)S(1)} %collective-permute-done.14.refs_2_), channel_id=1, source_target_pairs={{0,1},{1,0},{2,3},{3,2},{4,5},{5,4},{6,7},{7,6},{8,9},{9,8},{10,11... | collective-permute-start | bytes 1572872 | tf_op jit(solution)/shard_map/ppermute | solution.py:259
  52.9 6.7 %collective-permute-start.18 = (f32[256,512]{1,0:T(8,128)S(1)}, f32[256,512]{1,0:T(8,128)S(1)}, u32[]{:S(2)}, u32[]{:S(2)}) collective-permute-start(f32[256,512]{1,0:T(8,128)S(1)} %collective-permute-done.15.refs_3_), channel_id=1, source_target_pairs={{0,1},{1,0},{2,3},{3,2},{4,5},{5,4},{6,7},{7,6},{8,9},{9,8},{10,11... | collective-permute-start | bytes 1572872 | tf_op jit(solution)/shard_map/ppermute | solution.py:259
  53.4 13.3 %collective-permute-start.10 = (f32[264,512]{1,0:T(8,128)S(1)}, f32[264,512]{1,0:T(8,128)S(1)}, u32[]{:S(2)}, u32[]{:S(2)}) collective-permute-start(f32[264,512]{1,0:T(8,128)S(1)} %pack.1.refs_0_), channel_id=1, source_target_pairs={{0,1},{1,0},{2,3},{3,2},{4,5},{5,4},{6,7},{7,6},{8,9},{9,8},{10,11... | collective-permute-start | bytes 1622024 | tf_op jit(solution)/shard_map/ppermute | solution.py:259
  59.0 7.7 %collective-permute-start.11 = (f32[264,512]{1,0:T(8,128)S(1)}, f32[264,512]{1,0:T(8,128)S(1)}, u32[]{:S(2)}, u32[]{:S(2)}) collective-permute-start(f32[264,512]{1,0:T(8,128)S(1)} %collective-permute-done.7.refs_1_), channel_id=1, source_target_pairs={{0,1},{1,0},{2,3},{3,2},{4,5},{5,4},{6,7},{7,6},{8,9},{9,8},{10,11... | collective-permute-start | bytes 1622024 | tf_op jit(solution)/shard_map/ppermute | solution.py:259
  59.0 7.7 %collective-permute-start.12 = (f32[264,512]{1,0:T(8,128)S(1)}, f32[264,512]{1,0:T(8,128)S(1)}, u32[]{:S(2)}, u32[]{:S(2)}) collective-permute-start(f32[264,512]{1,0:T(8,128)S(1)} %collective-permute-done.8.refs_2_), channel_id=1, source_target_pairs={{0,1},{1,0},{2,3},{3,2},{4,5},{5,4},{6,7},{7,6},{8,9},{9,8},{10,11... | collective-permute-start | bytes 1622024 | tf_op jit(solution)/shard_map/ppermute | solution.py:259
  59.5 7.2 %collective-permute-start.13 = (f32[264,512]{1,0:T(8,128)S(1)}, f32[264,512]{1,0:T(8,128)S(1)}, u32[]{:S(2)}, u32[]{:S(2)}) collective-permute-start(f32[264,512]{1,0:T(8,128)S(1)} %collective-permute-done.9.refs_3_), channel_id=1, source_target_pairs={{0,1},{1,0},{2,3},{3,2},{4,5},{5,4},{6,7},{7,6},{8,9},{9,8},{10,11... | collective-permute-start | bytes 1622024 | tf_op jit(solution)/shard_map/ppermute | solution.py:259
  59.6 3.6 %collective-permute-start.19 = (f32[256,512]{1,0:T(8,128)S(1)}, f32[256,512]{1,0:T(8,128)S(1)}, u32[]{:S(2)}, u32[]{:S(2)}) collective-permute-start(f32[256,512]{1,0:T(8,128)S(1)} %collective-permute-done.16.refs_4_), channel_id=1, source_target_pairs={{0,1},{1,0},{2,3},{3,2},{4,5},{5,4},{6,7},{7,6},{8,9},{9,8},{10,11... | collective-permute-start | bytes 1572872 | tf_op jit(solution)/shard_map/ppermute | solution.py:259
  73.6 12.1 %collective-permute-start.34 = (f32[72,512]{1,0:T(8,128)S(1)}, f32[72,512]{1,0:T(8,128)S(1)}, u32[]{:S(2)}, u32[]{:S(2)}) collective-permute-start(f32[72,512]{1,0:T(8,128)S(1)} %term.1), channel_id=1, source_target_pairs={{0,24},{8,0},{16,8},{24,16},{32,56},{40,32},{48,40},{56,48},{64,88... | collective-permute-start | bytes 442376 | tf_op jit(solution)/shard_map/ppermute | solution.py:262
  76.9 10.2 %collective-permute-start.33 = (f32[72,512]{1,0:T(8,128)S(1)}, f32[72,512]{1,0:T(8,128)S(1)}, u32[]{:S(2)}, u32[]{:S(2)}) collective-permute-start(f32[72,512]{1,0:T(8,128)S(1)} %term.1), channel_id=1, source_target_pairs={{0,16},{8,24},{16,0},{24,8},{32,48},{40,56},{48,32},{56,40},{64,80... | collective-permute-start | bytes 442376 | tf_op jit(solution)/shard_map/ppermute | solution.py:262
  76.9 11.5 %collective-permute-start.32 = (f32[72,512]{1,0:T(8,128)S(1)}, f32[72,512]{1,0:T(8,128)S(1)}, u32[]{:S(2)}, u32[]{:S(2)}) collective-permute-start(f32[72,512]{1,0:T(8,128)S(1)} %term.1), channel_id=1, source_target_pairs={{0,8},{8,16},{16,24},{24,0},{32,40},{40,48},{48,56},{56,32},{64,72... | collective-permute-start | bytes 442376 | tf_op jit(solution)/shard_map/ppermute | solution.py:262
  77.5 30.2 %collective-permute-start.21 = (f32[64,512]{1,0:T(8,128)S(1)}, f32[64,512]{1,0:T(8,128)S(1)}, u32[]{:S(2)}, u32[]{:S(2)}) collective-permute-start(f32[64,512]{1,0:T(8,128)S(1)} %get-tuple-element.47), channel_id=1, source_target_pairs={{64,0},{72,8},{80,16},{88,24},{96,32},{104,40},{112,48},{120,56},{... | collective-permute-start | bytes 393224 | tf_op jit(solution)/shard_map/ppermute | solution.py:272
  78.8 28.9 %collective-permute-start.20 = (f32[64,512]{1,0:T(8,128)S(1)}, f32[64,512]{1,0:T(8,128)S(1)}, u32[]{:S(2)}, u32[]{:S(2)}) collective-permute-start(f32[64,512]{1,0:T(8,128)S(1)} %get-tuple-element.47), channel_id=1, source_target_pairs={{32,0},{40,8},{48,16},{56,24},{64,32},{72,40},{80,48},{88,56},{96,... | collective-permute-start | bytes 393224 | tf_op jit(solution)/shard_map/ppermute | solution.py:272
  85.8 7.8 %collective-permute-start.24 = (f32[72,512]{1,0:T(8,128)S(1)}, f32[72,512]{1,0:T(8,128)S(1)}, u32[]{:S(2)}, u32[]{:S(2)}) collective-permute-start(f32[72,512]{1,0:T(8,128)S(1)} %get-tuple-element.50), channel_id=1, source_target_pairs={{24,0},{56,32},{88,64},{120,96},{25,1},{57,33},{89,65},{121,97},{2... | collective-permute-start | bytes 442376 | tf_op jit(solution)/shard_map/ppermute | solution.py:267
  87.1 7.8 %collective-permute-start.22 = (f32[72,512]{1,0:T(8,128)S(1)}, f32[72,512]{1,0:T(8,128)S(1)}, u32[]{:S(2)}, u32[]{:S(2)}) collective-permute-start(f32[72,512]{1,0:T(8,128)S(1)} %get-tuple-element.48), channel_id=1, source_target_pairs={{8,0},{16,8},{24,16},{40,32},{48,40},{56,48},{72,64},{80,72},{88,8... | collective-permute-start | bytes 442376 | tf_op jit(solution)/shard_map/ppermute | solution.py:267
  88.4 8.0 %collective-permute-start.23 = (f32[72,512]{1,0:T(8,128)S(1)}, f32[72,512]{1,0:T(8,128)S(1)}, u32[]{:S(2)}, u32[]{:S(2)}) collective-permute-start(f32[72,512]{1,0:T(8,128)S(1)} %get-tuple-element.49), channel_id=1, source_target_pairs={{16,0},{24,8},{48,32},{56,40},{80,64},{88,72},{112,96},{120,104},{... | collective-permute-start | bytes 442376 | tf_op jit(solution)/shard_map/ppermute | solution.py:267
  93.6 6.2 %collective-permute-start.35 = (f32[72,512]{1,0:T(8,128)S(1)}, f32[72,512]{1,0:T(8,128)S(1)}, u32[]{:S(2)}, u32[]{:S(2)}) collective-permute-start(f32[72,512]{1,0:T(8,128)S(1)} %add_add_fusion), channel_id=1, source_target_pairs={{32,0},{40,8},{48,16},{56,24},{64,32},{72,40},{80,48},{88,56},{96,... | collective-permute-start | bytes 442376 | tf_op jit(solution)/shard_map/ppermute | solution.py:272
  94.9 8.3 %collective-permute-start.36 = (f32[72,512]{1,0:T(8,128)S(1)}, f32[72,512]{1,0:T(8,128)S(1)}, u32[]{:S(2)}, u32[]{:S(2)}) collective-permute-start(f32[72,512]{1,0:T(8,128)S(1)} %add_add_fusion), channel_id=1, source_target_pairs={{64,0},{72,8},{80,16},{88,24},{96,32},{104,40},{112,48},{120,56},{... | collective-permute-start | bytes 442376 | tf_op jit(solution)/shard_map/ppermute | solution.py:272
  96.4 11.2 %collective-permute-start.37 = (f32[72,512]{1,0:T(8,128)S(1)}, f32[72,512]{1,0:T(8,128)S(1)}, u32[]{:S(2)}, u32[]{:S(2)}) collective-permute-start(f32[72,512]{1,0:T(8,128)S(1)} %add_add_fusion), channel_id=1, source_target_pairs={{96,0},{104,8},{112,16},{120,24},{97,1},{105,9},{113,17},{121,25},... | collective-permute-start | bytes 442376 | tf_op jit(solution)/shard_map/ppermute | solution.py:272
  107.6 8.2 %collective-permute-start.38 = (f32[216,512]{1,0:T(8,128)S(1)}, f32[216,512]{1,0:T(8,128)S(1)}, u32[]{:S(2)}, u32[]{:S(2)}) collective-permute-start(f32[216,512]{1,0:T(8,128)S(1)} %constant_dynamic-update-slice_fusion.refs_8_), channel_id=1, source_target_pairs={{0,2},{1,7},{2,4},{3,1},{4,6},{5,3},{6,0},{7,5},{8,10},{9,15},{10,... | collective-permute-start | bytes 1327112 | tf_op jit(solution)/shard_map/ppermute | solution.py:277
  107.8 14.0 %collective-permute-start.25 = (f32[200,512]{1,0:T(8,128)S(1)}, f32[200,512]{1,0:T(8,128)S(1)}, u32[]{:S(2)}, u32[]{:S(2)}) collective-permute-start(f32[200,512]{1,0:T(8,128)S(1)} %pad_maximum_fusion.refs_8_), channel_id=1, source_target_pairs={{0,2},{1,7},{2,4},{3,1},{4,6},{5,3},{6,0},{7,5},{8,10},{9,15},{10,... | collective-permute-start | bytes 1228808 | tf_op jit(solution)/shard_map/ppermute | solution.py:277
  107.8 13.9 %collective-permute-start.26 = (f32[200,512]{1,0:T(8,128)S(1)}, f32[200,512]{1,0:T(8,128)S(1)}, u32[]{:S(2)}, u32[]{:S(2)}) collective-permute-start(f32[200,512]{1,0:T(8,128)S(1)} %pad_maximum_fusion.refs_8_), channel_id=1, source_target_pairs={{0,6},{1,3},{2,0},{3,5},{4,2},{5,7},{6,4},{7,1},{8,14},{9,11},{10,... | collective-permute-start | bytes 1228808 | tf_op jit(solution)/shard_map/ppermute | solution.py:277
  109.3 21.6 %collective-permute-start.28 = (f32[200,512]{1,0:T(8,128)S(1)}, f32[200,512]{1,0:T(8,128)S(1)}, u32[]{:S(2)}, u32[]{:S(2)}) collective-permute-start(f32[200,512]{1,0:T(8,128)S(1)} %pad_maximum_fusion.refs_8_), channel_id=1, source_target_pairs={{0,1},{1,0},{2,3},{3,2},{4,5},{5,4},{6,7},{7,6},{8,9},{9,8},{10,11... | collective-permute-start | bytes 1228808 | tf_op jit(solution)/shard_map/ppermute | solution.py:259
  115.6 15.5 %collective-permute-start.39 = (f32[216,512]{1,0:T(8,128)S(1)}, f32[216,512]{1,0:T(8,128)S(1)}, u32[]{:S(2)}, u32[]{:S(2)}) collective-permute-start(f32[216,512]{1,0:T(8,128)S(1)} %constant_dynamic-update-slice_fusion.refs_8_), channel_id=1, source_target_pairs={{0,6},{1,3},{2,0},{3,5},{4,2},{5,7},{6,4},{7,1},{8,14},{9,11},{10,... | collective-permute-start | bytes 1327112 | tf_op jit(solution)/shard_map/ppermute | solution.py:277
  115.8 23.9 %collective-permute-start.40 = (f32[216,512]{1,0:T(8,128)S(1)}, f32[216,512]{1,0:T(8,128)S(1)}, u32[]{:S(2)}, u32[]{:S(2)}) collective-permute-start(f32[216,512]{1,0:T(8,128)S(1)} %collective-permute-done.38.refs_9_), channel_id=1, source_target_pairs={{0,2},{1,7},{2,4},{3,1},{4,6},{5,3},{6,0},{7,5},{8,10},{9,15},{10,... | collective-permute-start | bytes 1327112 | tf_op jit(solution)/shard_map/ppermute | solution.py:277
  121.8 16.0 %collective-permute-start.27 = (f32[200,512]{1,0:T(8,128)S(1)}, f32[200,512]{1,0:T(8,128)S(1)}, u32[]{:S(2)}, u32[]{:S(2)}) collective-permute-start(f32[200,512]{1,0:T(8,128)S(1)} %collective-permute-done.25.refs_9_), channel_id=1, source_target_pairs={{0,2},{1,7},{2,4},{3,1},{4,6},{5,3},{6,0},{7,5},{8,10},{9,15},{10,... | collective-permute-start | bytes 1228808 | tf_op jit(solution)/shard_map/ppermute | solution.py:277
  121.8 17.9 %collective-permute-start.29 = (f32[200,512]{1,0:T(8,128)S(1)}, f32[200,512]{1,0:T(8,128)S(1)}, u32[]{:S(2)}, u32[]{:S(2)}) collective-permute-start(f32[200,512]{1,0:T(8,128)S(1)} %collective-permute-done.25.refs_9_), channel_id=1, source_target_pairs={{0,1},{1,0},{2,3},{3,2},{4,5},{5,4},{6,7},{7,6},{8,9},{9,8},{10,11... | collective-permute-start | bytes 1228808 | tf_op jit(solution)/shard_map/ppermute | solution.py:259
  131.0 9.2 %collective-permute-start.30 = (f32[200,512]{1,0:T(8,128)S(1)}, f32[200,512]{1,0:T(8,128)S(1)}, u32[]{:S(2)}, u32[]{:S(2)}) collective-permute-start(f32[200,512]{1,0:T(8,128)S(1)} %collective-permute-done.26.refs_10_), channel_id=1, source_target_pairs={{0,1},{1,0},{2,3},{3,2},{4,5},{5,4},{6,7},{7,6},{8,9},{9,8},{10,11... | collective-permute-start | bytes 1228808 | tf_op jit(solution)/shard_map/ppermute | solution.py:259
  131.1 15.4 %collective-permute-start.41 = (f32[216,512]{1,0:T(8,128)S(1)}, f32[216,512]{1,0:T(8,128)S(1)}, u32[]{:S(2)}, u32[]{:S(2)}) collective-permute-start(f32[216,512]{1,0:T(8,128)S(1)} %constant_dynamic-update-slice_fusion.refs_8_), channel_id=1, source_target_pairs={{0,1},{1,0},{2,3},{3,2},{4,5},{5,4},{6,7},{7,6},{8,9},{9,8},{10,11... | collective-permute-start | bytes 1327112 | tf_op jit(solution)/shard_map/ppermute | solution.py:259
  137.8 8.7 %collective-permute-start.42 = (f32[216,512]{1,0:T(8,128)S(1)}, f32[216,512]{1,0:T(8,128)S(1)}, u32[]{:S(2)}, u32[]{:S(2)}) collective-permute-start(f32[216,512]{1,0:T(8,128)S(1)} %collective-permute-done.38.refs_9_), channel_id=1, source_target_pairs={{0,1},{1,0},{2,3},{3,2},{4,5},{5,4},{6,7},{7,6},{8,9},{9,8},{10,11... | collective-permute-start | bytes 1327112 | tf_op jit(solution)/shard_map/ppermute | solution.py:259
  139.6 6.9 %collective-permute-start.43 = (f32[216,512]{1,0:T(8,128)S(1)}, f32[216,512]{1,0:T(8,128)S(1)}, u32[]{:S(2)}, u32[]{:S(2)}) collective-permute-start(f32[216,512]{1,0:T(8,128)S(1)} %collective-permute-done.39.refs_10_), channel_id=1, source_target_pairs={{0,1},{1,0},{2,3},{3,2},{4,5},{5,4},{6,7},{7,6},{8,9},{9,8},{10,11... | collective-permute-start | bytes 1327112 | tf_op jit(solution)/shard_map/ppermute | solution.py:259
  139.7 6.9 %collective-permute-start.44 = (f32[216,512]{1,0:T(8,128)S(1)}, f32[216,512]{1,0:T(8,128)S(1)}, u32[]{:S(2)}, u32[]{:S(2)}) collective-permute-start(f32[216,512]{1,0:T(8,128)S(1)} %collective-permute-done.40.refs_11_), channel_id=1, source_target_pairs={{0,1},{1,0},{2,3},{3,2},{4,5},{5,4},{6,7},{7,6},{8,9},{9,8},{10,11... | collective-permute-start | bytes 1327112 | tf_op jit(solution)/shard_map/ppermute | solution.py:259
  140.2 2.7 %collective-permute-start.31 = (f32[200,512]{1,0:T(8,128)S(1)}, f32[200,512]{1,0:T(8,128)S(1)}, u32[]{:S(2)}, u32[]{:S(2)}) collective-permute-start(f32[200,512]{1,0:T(8,128)S(1)} %collective-permute-done.27.refs_11_), channel_id=1, source_target_pairs={{0,1},{1,0},{2,3},{3,2},{4,5},{5,4},{6,7},{7,6},{8,9},{9,8},{10,11... | collective-permute-start | bytes 1228808 | tf_op jit(solution)/shard_map/ppermute | solution.py:259

commit v3 on v2

v3 whole, which is shorter than its diff:
```python
import jax
import jax.numpy as jnp
from jax import lax
from jax.experimental import pallas as pl
from jax.experimental.pallas import tpu as pltpu
from jax.sharding import PartitionSpec as P

D = 512
ROWS = 64
HALF = 256
AUG = D + 8
NN = (((1,), (0,)), ((), ()))
NT = (((1,), (1,)), ((), ()))
VMEM = pl.BlockSpec(memory_space=pltpu.VMEM)
ANY = pl.BlockSpec(memory_space=pl.ANY)
F32 = jnp.float32
BF16 = jnp.bfloat16


def full(*dims):
    return jax.ShapeDtypeStruct(dims, F32)


def part(*dims):
    return jax.ShapeDtypeStruct(dims, BF16)


def split(a):
    high = a.astype(BF16)
    return high, (a - high.astype(F32)).astype(BF16)


def dot(a, b, dims):
    return lax.dot_general(a, b, dims, preferred_element_type=F32)


def dot3(a, b, dims):
    return dot(a[0], b[0], dims) + (dot(a[0], b[1], dims) + dot(a[1], b[0], dims))


def call(kernel, name, outs, args, scratch=(), us=0, mib=18, outside=()):
    return pl.pallas_call(
        kernel,
        out_shape=outs,
        in_specs=[ANY if index in outside else VMEM for index in range(len(args))],
        out_specs=[VMEM] * len(outs),
        scratch_shapes=list(scratch),
        compiler_params=pltpu.CompilerParams(vmem_limit_bytes=mib << 20),
        cost_estimate=pl.CostEstimate(
            flops=us * 10**9, bytes_accessed=0, transcendentals=0
        ),
        name=name,
    )(*args)


def gate(value, *others):
    return pl.pallas_call(
        lambda *refs: None,
        out_shape=jax.ShapeDtypeStruct(value.shape, value.dtype),
        in_specs=[ANY] * (1 + len(others)),
        out_specs=ANY,
        input_output_aliases={0: 0},
        compiler_params=pltpu.CompilerParams(vmem_limit_bytes=1 << 20),
        name="gate",
    )(value, *others)


def position():
    panel, block = lax.axis_index("panel"), lax.axis_index("tm")
    return panel // 2, panel % 2, block % 4


def own_rows(size=ROWS):
    return pl.ds(pl.multiple_of(lax.axis_index("panel") * size, size), size)


def places(mine, c):
    toward = 1 - 2 * c
    own = [mine, mine - toward, mine + toward, mine + 2]
    other = [mine, mine + toward, mine - toward, mine + 2]
    return [((place + 4) % 4, c) for place in own] + [((place + 4) % 4, 1 - c) for place in other]


def panels(z, c):
    return [2 * place + core for place, core in places(z, c)]


def chip_pieces(refs, z, c):
    pair, near, other, far, far_other = refs
    size, toward = far.shape[0], 1 - 2 * c
    pieces = [
        (ref, core * size, 2 * (place % 4) + core)
        for ref, place in ((pair, z), (near, z - toward + 4), (other, z + toward + 4))
        for core in range(2)
    ]
    return pieces + [(far, 0, 2 * ((z + 2) % 4) + c), (far_other, 0, 2 * ((z + 2) % 4) + 1 - c)]


def at(panel, size=ROWS):
    return pl.ds(pl.multiple_of(panel * size, size), size)


def block_kernel(*refs):
    pieces, (e_hi, e_lo), suffix, (total, mine, sem) = refs[:8], refs[8:10], refs[10:18], refs[18:]
    z, c, _ = position()
    copy = pltpu.make_async_copy(pieces[0], mine, sem)
    copy.start()
    spots = list(zip((mine, *pieces[1:]), panels(z, c)))
    for index, (piece, panel) in enumerate(spots[1:] + spots[:1]):
        if index == 7:
            copy.wait()
        for k in range(4):
            high, low = split(piece[k * ROWS : (k + 1) * ROWS, :])
            to_hi, to_lo = (e_hi.at[k], e_lo.at[k]) if k < 3 else suffix[6:8]
            to_hi[at(panel), :] = high
            to_lo[at(panel), :] = low
    for k in (2, 1, 0):
        product = dot3((e_hi[k], e_lo[k]), (suffix[2 * k + 2][...], suffix[2 * k + 3][...]), NN)
        suffix[2 * k][...], suffix[2 * k + 1][...] = split(product)
    total[...] = product


def pack_kernel(noise, offsets, packed, sem):
    copy = pltpu.make_async_copy(noise, packed.at[:HALF], sem)
    copy.start()
    packed[HALF:, :] = jnp.zeros((8, D), F32)
    for panel in range(8):

        @pl.when(lax.axis_index("panel") == panel)
        def _():
            packed[HALF : HALF + 4, panel * ROWS : (panel + 1) * ROWS] = offsets[...]

    copy.wait()


def pair_kernel(mine, other, pair):
    c = position()[1]
    rows = mine.shape[0]
    pair[at(c, rows), :] = mine[...]
    pair[at(1 - c, rows), :] = other[...]


def cut_kernel(pair, mine):
    rows = mine.shape[0]
    mine[...] = pair[at(position()[1], rows), :]


def congruence(gain, cov, scratch):
    scratch[:D, :] = dot3(gain, split(cov[:D, :]), NN)
    scratch[D:, :] = cov[D:, :]
    return dot3(split(scratch[...]), gain, NT)


def noise_kernel(e_hi, e_lo, *refs):
    pieces, (rows_out, means_out, whole, scratch) = refs[:5], refs[5:]
    z, c, _ = position()
    size, pieces = HALF + 8, chip_pieces(pieces, z, c)
    offsets = sum(ref[start + HALF : start + size, :] for ref, start, _ in pieces)
    row = lax.broadcasted_iota(jnp.int32, (8, D), 0)
    means_out[...] = jnp.zeros((8, D), F32)
    for k in (3, 2, 1, 0):
        if k == 3:
            whole[...] = jnp.zeros((AUG, D), F32)
        else:
            whole[...] = congruence((e_hi[k], e_lo[k]), whole[...], scratch)
        for ref, start, panel in pieces:
            whole[at(panel), :] += ref[start + k * ROWS : start + (k + 1) * ROWS, :]
        offset = jnp.sum(jnp.where(row == k, offsets, 0.0), axis=0, keepdims=True)
        whole[D:, :] += jnp.where(row == 0, offset, 0.0)
        rows_out[k] = whole[own_rows(), :]
        means_out[k : k + 1, :] = whole[D : D + 1, :]


def gather_gains(own_hi, own_lo, near, other, far, far_other, a_hi, a_lo):
    _, c, y = position()
    toward, across = 1 - 2 * c, (y + 2) % 4
    a_hi[y] = own_hi[...]
    a_lo[y] = own_lo[...]
    a_hi[(y - toward + 4) % 4], a_lo[(y - toward + 4) % 4] = split(near[...])
    a_hi[(y + toward + 4) % 4], a_lo[(y + toward + 4) % 4] = split(other[...])
    a_hi[across, at(c, HALF), :], a_lo[across, at(c, HALF), :] = split(far[...])
    a_hi[across, at(1 - c, HALF), :], a_lo[across, at(1 - c, HALF), :] = split(far_other[...])


def eye_parts():
    same = lax.broadcasted_iota(jnp.int32, (D, D), 0) == lax.broadcasted_iota(jnp.int32, (D, D), 1)
    return jnp.where(same, 1.0, 0.0).astype(BF16), jnp.zeros((D, D), BF16)


def rows_congruence(left, right, cov, scratch):
    scratch[:ROWS, :] = dot3(left, split(cov[:D, :]), NN)
    scratch[ROWS:, :] = cov[D:, :]
    return dot3(split(scratch[...]), right, NT)


def prefix_kernel(cov, moved, *refs):
    blocks, (gain, to_third, to_second, to_first, a_hi, a_lo, f_hi, f_lo, short) = refs[:6], refs[6:]
    y = position()[2]
    gather_gains(*blocks, a_hi, a_lo)

    @pl.when(y == 0)
    def _():
        f_hi[...], f_lo[...] = eye_parts()

    head = (a_hi[0], a_lo[0])
    for block in (1, 2, 3):

        @pl.when(y == block)
        def _():
            f_hi[...], f_lo[...] = head

        if block < 3:
            head = split(dot3(head, (a_hi[block], a_lo[block]), NN))
    term = rows_congruence(
        (f_hi[own_rows(), :], f_lo[own_rows(), :]), (f_hi[...], f_lo[...]), cov[...], short
    )
    for message in (to_third, to_second, to_first):
        message[: ROWS + 8, :] = term
    for message, whole in ((to_first, cov), (to_second, moved)):
        message[ROWS + 8 : 2 * ROWS + 8, :] = whole[own_rows(), :]
        message[2 * ROWS + 8 :, :] = whole[D:, :]
    twice = (y + 2) % 4
    to_third[ROWS + 8 :, :] = rows_congruence(
        (a_hi[twice, own_rows(), :], a_lo[twice, own_rows(), :]), (a_hi[twice], a_lo[twice]), moved[...], short
    )
    f_hi[...], f_lo[...] = head
    gain[...] = dot3((f_hi[own_rows(), :], f_lo[own_rows(), :]), (a_hi[3], a_lo[3]), NN)


def second_kernel(cov, near, other, moved, a_hi, a_lo, scratch):
    _, c, _ = position()
    for core, piece in enumerate((near, other)):

        @pl.when(c == core)
        def _():
            a_hi[...], a_lo[...] = split(piece[...])

    moved[...] = congruence((a_hi[...], a_lo[...]), cov[...], scratch)


def sum_kernel(own, third, second, first, total, beyond):
    y, size = position()[2], ROWS + 8
    total[...] = own[:size, :] + third[:size, :] + second[:size, :] + first[:size, :]
    beyond[...] = (
        jnp.where(y < 1, third[size:, :], 0.0)
        + jnp.where(y < 2, second[size:, :], 0.0)
        + jnp.where(y < 3, first[size:, :], 0.0)
    )


def tail_kernel(*refs):
    blocks, (p_hi, p_lo, a_hi, a_lo) = refs[:6], refs[6:]
    y = position()[2]
    gather_gains(*blocks, a_hi, a_lo)

    @pl.when(y == 3)
    def _():
        p_hi[...], p_lo[...] = eye_parts()

    tail = (a_hi[3], a_lo[3])
    for block in (2, 1, 0):

        @pl.when(y == block)
        def _():
            p_hi[...], p_lo[...] = tail

        if block > 0:
            tail = split(dot3((a_hi[block], a_lo[block]), tail, NN))


def blocks_kernel(first, second, third, rows, back, ahead, across):
    z = position()[0]
    for index, piece in enumerate((first, second, third)):
        rows[index * ROWS : (index + 1) * ROWS, :] = piece[:ROWS, :]
    for step, messages in ((0, (back, ahead, across)), (1, (back,)), (2, (back,)), (3, (ahead,))):
        block = rows[:, at((z + step) % 4, 128)]
        for message in messages:
            column = 128 if message is ahead and step else 128 * step
            message[:, column : column + 128] = block


def fill_symmetric(cov, index, own, back, ahead, across, z, c):
    rows = slice(index * ROWS, (index + 1) * ROWS)
    a, b, far = (z + 1) % 4, (z + 3) % 4, (z + 2) % 4
    for half in range(2):
        core = c if half == 0 else 1 - c

        def place(row, column, value):
            start = pl.multiple_of(row * 128 + core * ROWS, ROWS)
            cov[pl.ds(start, ROWS), at(column, 128)] = value

        cov[pl.ds(pl.multiple_of(z * 128 + core * ROWS, ROWS), ROWS), :] = own[half][rows, :]
        place(a, a, back[half][rows, :128])
        place(a, far, back[half][rows, 128:256])
        place(a, b, back[half][rows, 256:])
        place(b, b, ahead[half][rows, :128])
        place(b, far, ahead[half][rows, 128:])
        place(far, far, across[half][rows, :])
    for row, column in ((z, a), (z, b), (z, far), (a, far), (a, b), (b, far)):
        cov[at(column, 128), at(row, 128)] = cov[at(row, 128), at(column, 128)].T


def pack_outer_kernel(first, second, later, rows):
    rows[:ROWS, :] = first[...]
    rows[ROWS : 2 * ROWS, :] = second[...]
    rows[2 * ROWS :, :] = later[:ROWS, :]


def outer_kernel(*refs):
    p_hi, p_lo, offset, suffix, pieces = refs[0], refs[1], refs[2], refs[3:11], refs[11:19]
    b_hi, b_lo, x_hi, x_lo, base, gains, later, s_hi, s_lo = refs[19:]
    z, c, _ = position()
    spots = [2 * ((z - step + 4) % 4) + core for core in (c, 1 - c) for step in range(4)]
    for piece, panel in zip(pieces, spots):
        gains[0, at(panel), :] = piece[:ROWS, :]
        gains[1, at(panel), :] = piece[ROWS : 2 * ROWS, :]
        later[at(panel), :] = piece[2 * ROWS :, :]
    for k in range(4):
        s_hi[k * ROWS : (k + 1) * ROWS, :] = suffix[2 * k][own_rows(), :]
        s_lo[k * ROWS : (k + 1) * ROWS, :] = suffix[2 * k + 1][own_rows(), :]
    steps = (s_hi[...], s_lo[...])
    base[:HALF, :] = dot3(steps, split(later[...]), NN)
    base[HALF:, :] = offset[ROWS:, :]
    b_hi[0], b_lo[0] = p_hi[...], p_lo[...]
    x_hi[0], x_lo[0] = split(dot3(steps, (b_hi[0], b_lo[0]), NN))
    for index in range(2):
        gain = split(gains[index])
        b_hi[index + 1], b_lo[index + 1] = split(dot3((b_hi[index], b_lo[index]), gain, NN))
        x_hi[index + 1], x_lo[index + 1] = split(dot3((x_hi[index], x_lo[index]), gain, NN))


def final_kernel(b_hi, b_lo, x_hi, x_lo, base, rows_in, means_in, *refs):
    suffix, offsets, pieces, (out, means, cov, stack, short, every) = refs[:8], refs[8:11], refs[11:19], refs[19:]
    z, c, _ = position()
    inner = base[...]
    for index in range(3):
        fill_symmetric(cov, index, pieces[0:2], pieces[2:4], pieces[4:6], pieces[6:8], z, c)
        stack[:HALF, :] = dot3((x_hi[index], x_lo[index]), split(cov[...]), NN)
        stack[HALF:, :] = offsets[index][ROWS:, :]
        inner = inner + dot3(split(stack[...]), (b_hi[index], b_lo[index]), NT)
    stack[...] = inner
    for k in range(4):
        short[:ROWS, :] = stack[k * ROWS : (k + 1) * ROWS, :]
        short[ROWS:, :] = stack[HALF:, :]
        result = dot3(split(short[...]), (suffix[2 * k][...], suffix[2 * k + 1][...]), NT)
        out[k] = result[:ROWS, :] + rows_in[k]
        every[k : k + 1, :] = result[ROWS : ROWS + 1, :] + means_in[k : k + 1, :]
    for panel in range(8):

        @pl.when(lax.axis_index("panel") == panel)
        def _():
            means[...] = every[:4, panel * ROWS : (panel + 1) * ROWS]


def per_device(transitions, offsets, noise_cov):
    def other_core(value):
        return lax.ppermute(value, "panel", [(2 * z + c, 2 * z + 1 - c) for z in range(4) for c in range(2)])

    def along_y(value, step):
        return lax.ppermute(
            value, "tm", [(4 * x + y, 4 * x + (y + step) % 4) for x in range(4) for y in range(4)]
        )

    def back_x(value, step):
        return lax.ppermute(
            value, "tm", [(4 * x + y, 4 * (x - step) + y) for x in range(step, 4) for y in range(4)]
        )

    def along_z(value, step):
        return lax.ppermute(
            value, "panel", [(2 * z + c, 2 * ((z + step) % 4) + c) for z in range(4) for c in range(2)]
        )

    def paired_z(value, step):
        return lax.ppermute(
            value, "panel", [(2 * z + c, 2 * ((z + step * (1 - 2 * c)) % 4) + c) for z in range(4) for c in range(2)]
        )

    def paired_y(value, step):
        pairs = []
        for x in range(4):
            for y in range(4):
                for panel in range(8):
                    to = 4 * x + (y + step * (1 - 2 * (panel % 2))) % 4
                    pairs.append((8 * (4 * x + y) + panel, 8 * to + panel))
        return lax.ppermute(value, ("tm", "panel"), pairs)

    def exchange(value, paired):
        first = paired(value, 1)
        return [first, paired(value, -1), paired(first, 1)]

    def both_cores(pieces):
        return pieces + [other_core(piece) for piece in pieces]

    def whole_z(value):
        return both_cores([value] + exchange(value, paired_z))

    (noise,) = call(
        pack_kernel,
        "pack",
        [full(HALF + 8, D)],
        [noise_cov.reshape(HALF, D), offsets],
        [pltpu.SemaphoreType.DMA],
        outside=(0,),
    )
    other_noise = other_core(noise)
    own = transitions.reshape(HALF, D)
    first, second, third = exchange(own, paired_z)
    (pair,) = call(pair_kernel, "pair", [full(2 * HALF + 16, D)], [gate(noise, second), other_noise])
    steps = both_cores([own, first, second, gate(third, pair)])
    e_hi, e_lo, *rest = call(
        block_kernel,
        "block",
        [part(3, D, D)] * 2 + [part(D, D)] * 8 + [full(D, D)],
        steps,
        [pltpu.VMEM((HALF, D), F32), pltpu.SemaphoreType.DMA],
        outside=(0,),
    )
    suffix, total = rest[:8], rest[8]
    near_gain, near_noise = paired_y(total, 1), paired_z(pair, 1)
    (half_gain,) = call(cut_kernel, "cut", [full(HALF, D)], [near_gain])
    (half_noise,) = call(cut_kernel, "cut", [full(HALF + 8, D)], [near_noise])
    far_gain, far_noise = paired_y(half_gain, 1), gate(paired_z(half_noise, 1), half_gain)
    other_gain = other_core(near_gain)
    rows, means, cov = call(
        noise_kernel,
        "noise",
        [full(4, ROWS, D), full(8, D), full(AUG, D)],
        [e_hi, e_lo, pair, near_noise, other_core(near_noise), far_noise, other_core(far_noise)],
        [pltpu.VMEM((AUG, D), F32)],
    )
    (moved,) = call(
        second_kernel,
        "second",
        [full(AUG, D)],
        [cov, near_gain, other_gain],
        [pltpu.VMEM((D, D), BF16), pltpu.VMEM((D, D), BF16), pltpu.VMEM((AUG, D), F32)],
    )
    far_gain = gate(far_gain, moved)
    blocks = [suffix[0], suffix[1], near_gain, other_gain, far_gain, other_core(far_gain)]
    gain, to_third, to_second, to_first = call(
        prefix_kernel,
        "prefix",
        [full(ROWS, D)] + [full(2 * ROWS + 16, D)] * 3,
        [cov, moved, *blocks],
        [pltpu.VMEM((4, D, D), BF16)] * 2 + [pltpu.VMEM((D, D), BF16)] * 2 + [pltpu.VMEM((ROWS + 8, D), F32)],
    )
    total, beyond = call(
        sum_kernel,
        "sum",
        [full(ROWS + 8, D)] * 2,
        [to_third, along_y(to_third, 1), along_y(to_second, 2), along_y(to_first, 3)],
    )
    far_covs = [back_x(total, step) for step in (1, 2, 3)]
    p_hi, p_lo = call(
        tail_kernel,
        "tail",
        [part(D, D)] * 2,
        blocks,
        [pltpu.VMEM((4, D, D), BF16)] * 2,
    )
    (packed,) = call(pack_outer_kernel, "pack_outer", [full(3 * ROWS, D)], [back_x(gain, 1), back_x(gain, 2), beyond])
    outer = both_cores([packed, *(along_z(packed, step) for step in (1, 2, 3))])
    own, *messages = call(
        blocks_kernel,
        "blocks",
        [full(3 * ROWS, D), full(3 * ROWS, 384), full(3 * ROWS, 256), full(3 * ROWS, 128)],
        [gate(far_covs[0], p_hi), *far_covs[1:]],
    )
    b_hi, b_lo, x_hi, x_lo, base = call(
        outer_kernel,
        "outer",
        [part(3, D, D), part(3, D, D), part(3, HALF, D), part(3, HALF, D), full(HALF + 8, D)],
        [p_hi, p_lo, beyond, *suffix, *outer],
        [
            pltpu.VMEM((2, D, D), F32),
            pltpu.VMEM((D, D), F32),
            pltpu.VMEM((HALF, D), BF16),
            pltpu.VMEM((HALF, D), BF16),
        ],
    )
    back, ahead, across = (along_z(value, step) for value, step in zip(messages, (-1, 1, 2)))
    covs = [gate(value, base) if value is across else value for value in (own, back, ahead, across)]
    covs = [piece for value in covs for piece in (value, other_core(value))]
    out, mean_rows = call(
        final_kernel,
        "final",
        [full(4, ROWS, D), full(4, ROWS)],
        [b_hi, b_lo, x_hi, x_lo, base, rows, means, *suffix, *far_covs, *covs],
        [
            pltpu.VMEM((D, D), F32),
            pltpu.VMEM((HALF + 8, D), F32),
            pltpu.VMEM((ROWS + 8, D), F32),
            pltpu.VMEM((8, D), F32),
        ],
        mib=24,
    )
    return mean_rows, out


def solution(mesh):
    placed = (P("tm", "panel", None), P("tm", "panel"), P("tm", "panel", None))
    return jax.shard_map(
        per_device,
        mesh=mesh,
        in_specs=placed,
        out_specs=(P("tm", "panel"), P("tm", "panel", None)),
        check_vma=False,
    )
```

time: 153 us -> 138 us (0.902)
  waiting for transfers between devices: 58.9 us -> 43 us
    ppermute x3, waiting for transfers between devices: 0.01 us -> 9.9 us  [along_y(): lax.ppermute(value, 'tm', [(4 * x + y, 4 * x + (y + step) % 4) for x in r...]
    ppermute x3 -> x2, waiting for transfers between devices: 9.93 us -> 2.26 us  [paired_y(): return lax.ppermute(value, ('tm', 'panel'), pairs)]
    ppermute x5, waiting for transfers between devices: 9.87 us -> 2.32 us  [back_x(): lax.ppermute(value, 'tm', [(4 * x + y, 4 * (x - step) + y) for x in range...]
    ppermute x12 -> x5, waiting for transfers between devices: 27.7 us -> 20.8 us  [paired_z(): lax.ppermute(value, 'panel', [(2 * z + c, 2 * ((z + step * (1 - 2 * c)) %...]
    ppermute x19 -> x17, waiting for transfers between devices: 7.43 us -> 2.87 us  [other_core(): lax.ppermute(value, 'panel', [(2 * z + c, 2 * z + 1 - c) for z in range(4...]
    ppermute x3 -> x6, starting transfers between devices: 3.88 us -> 6.16 us  [along_z(): lax.ppermute(value, 'panel', [(2 * z + c, 2 * ((z + step) % 4) + c) for z...]
    ppermute x12 -> x5, starting transfers between devices: 14.9 us -> 13.1 us  [paired_z(): lax.ppermute(value, 'panel', [(2 * z + c, 2 * ((z + step * (1 - 2 * c)) %...]
    ppermute x19 -> x17, starting transfers between devices: 27.2 us -> 25.9 us  [other_core(): lax.ppermute(value, 'panel', [(2 * z + c, 2 * z + 1 - c) for z in range(4...]
  transfers between devices with their start and end apart: 45 -> 38, of which waited for: 15 -> 17; matrix products, arithmetic and copies ran while one was open for 0% -> 0% of each run, Pallas kernels for 8% -> 13%
where the time goes in v3:
time: 138 us; the launch traced here: 136 us
  starting transfers between devices  61.1 us (44%)
  waiting for transfers between devices  43 us (31%)
  Pallas kernels  29.6 us (21%)
  local copies, waits for them, and re-layouts  1.74 us (1%)
    pallas_call x14, Pallas kernels, call(): pl.pallas_call(kernel, out_shape=outs, in_specs=[ANY if index in outside...  29.6 us
    ppermute x17, starting transfers between devices, other_core(): lax.ppermute(value, 'panel', [(2 * z + c, 2 * z + 1 - c) for z in range(4...  25.9 us
    ppermute x5, waiting for transfers between devices, paired_z(): lax.ppermute(value, 'panel', [(2 * z + c, 2 * ((z + step * (1 - 2 * c)) %...  20.8 us
    ppermute x5, starting transfers between devices, paired_z(): lax.ppermute(value, 'panel', [(2 * z + c, 2 * ((z + step * (1 - 2 * c)) %...  13.1 us
    ppermute x3, waiting for transfers between devices, along_y(): lax.ppermute(value, 'tm', [(4 * x + y, 4 * x + (y + step) % 4) for x in r...  9.9 us
    ppermute x5, starting transfers between devices, back_x(): lax.ppermute(value, 'tm', [(4 * x + y, 4 * (x - step) + y) for x in range...  6.44 us
    ppermute x6, starting transfers between devices, along_z(): lax.ppermute(value, 'panel', [(2 * z + c, 2 * ((z + step) % 4) + c) for z...  6.16 us
    ppermute x2, starting transfers between devices, paired_y(): return lax.ppermute(value, ('tm', 'panel'), pairs)  5.54 us
  transfers between devices with their start and end apart: 38, of which 17 were waited for; matrix products, arithmetic and copies ran while one was open for 0% of the time, Pallas kernels for 13%

profile of v3, /device:TPU:1, one launch (start us, length us, event | category | flops | bytes accessed | tf_op | source)
XLA Modules:
  0.0 136.2 jit_solution(6937726136816333340)
XLA Ops:
  0.6 4.7 %collective-permute-start = (f32[256,512]{1,0:T(8,128)}, f32[256,512]{1,0:T(8,128)S(1)}, u32[]{:S(2)}, u32[]{:S(2)}) collective-permute-start(f32[256,512]{1,0:T(8,128)} %bitcast.3), channel_id=1, source_target_pairs={{0,2},{1,7},{2,4},{3,1},{4,6},{5,3},{6,0},{7,5},{8,10},{9,15},{10,... | collective-permute-start | bytes 1572872 | tf_op jit(solution)/shard_map/ppermute | solution.py:375
  5.3 1.0 copy-done
  6.3 0.7 copy-done.2
  7.0 0.1 pack.1.refs_0_
  7.1 0.1 collective-permute-start.3
  7.2 0.4 collective-permute-start.1
  7.7 6.5 %collective-permute-done.refs_1_ = f32[256,512]{1,0:T(8,128)S(1)} collective-permute-done((f32[256,512]{1,0:T(8,128)}, f32[256,512]{1,0:T(8,128)S(1)}, u32[]{:S(2)}, u32[]{:S(2)}) %collective-permute-start) | collective-permute-done | bytes 524320 | tf_op jit(solution)/shard_map/ppermute | solution.py:375
  14.1 3.3 %collective-permute-start.2 = (f32[256,512]{1,0:T(8,128)S(1)}, f32[256,512]{1,0:T(8,128)S(1)}, u32[]{:S(2)}, u32[]{:S(2)}) collective-permute-start(f32[256,512]{1,0:T(8,128)S(1)} %collective-permute-done.refs_1_), channel_id=1, source_target_pairs={{0,2},{1,7},{2,4},{3,1},{4,6},{5,3},{6,0},{7,5},{8,10},{9,15},{10,... | collective-permute-start | bytes 1572872 | tf_op jit(solution)/shard_map/ppermute | solution.py:375
  17.5 0.5 collective-permute-start.5
  18.0 0.6 collective-permute-done.1.refs_1_.refs_2_
  18.6 0.1 pair.1.refs_1_.refs_0_
  18.6 0.0 copy-start.1
  18.7 4.9 %collective-permute-done.2.refs_0_ = f32[256,512]{1,0:T(8,128)S(1)} collective-permute-done((f32[256,512]{1,0:T(8,128)S(1)}, f32[256,512]{1,0:T(8,128)S(1)}, u32[]{:S(2)}, u32[]{:S(2)}) %collective-permute-start.2) | collective-permute-done | bytes 524320 | tf_op jit(solution)/shard_map/ppermute | solution.py:375
  23.6 3.0 %collective-permute-start.7 = (f32[256,512]{1,0:T(8,128)S(1)}, f32[256,512]{1,0:T(8,128)S(1)}, u32[]{:S(2)}, u32[]{:S(2)}) collective-permute-start(f32[256,512]{1,0:T(8,128)S(1)} %gate.7.refs_3_), channel_id=1, source_target_pairs={{0,1},{1,0},{2,3},{3,2},{4,5},{5,4},{6,7},{7,6},{8,9},{9,8},{10,11... | collective-permute-start | bytes 1572872 | tf_op jit(solution)/shard_map/ppermute | solution.py:357
  26.6 1.7 %collective-permute-start.11 = (f32[528,512]{1,0:T(8,128)S(1)}, f32[528,512]{1,0:T(8,128)S(1)}, u32[]{:S(2)}, u32[]{:S(2)}) collective-permute-start(f32[528,512]{1,0:T(8,128)S(1)} %pair.1.refs_1_.refs_0_), channel_id=1, source_target_pairs={{0,2},{1,7},{2,4},{3,1},{4,6},{5,3},{6,0},{7,5},{8,10},{9,15},{10,... | collective-permute-start | bytes 3244040 | tf_op jit(solution)/shard_map/ppermute | solution.py:375
  28.4 3.3 %block.1 = (bf16[3,512,512]{2,1,0:T(8,128)(2,1)S(1)}, bf16[3,512,512]{2,1,0:T(8,128)(2,1)S(1)}, bf16[512,512]{1,0:T(8,128)(2,1)S(1)}, bf16[512,512]{1,0:T(8,128)...) custom-call(f32[256,512]{1,0:T(8,128)S(1)} %bitcast.6, ...), custom_call_target="tpu_custom_call" | custom-call | tf_op jit(solution)/shard_map/block/pallas_call | solution.py:42
  31.7 2.8 %collective-permute-start.8 = (f32[512,512]{1,0:T(8,128)S(1)}, f32[512,512]{1,0:T(8,128)S(1)}, u32[]{:S(2)}, u32[]{:S(2)}) collective-permute-start(f32[512,512]{1,0:T(8,128)S(1)} %get-tuple-element.37), channel_id=1, source_target_pairs={{0,8},{1,25},{2,10},{3,27},{4,12},{5,29},{6,14},{7,31},{8,16},{9,1... | collective-permute-start | bytes 3145736 | tf_op jit(solution)/shard_map/ppermute | solution.py:386
  34.5 6.4 %collective-permute-done.11.pair.refs_1_ = f32[528,512]{1,0:T(8,128)S(1)} collective-permute-done((f32[528,512]{1,0:T(8,128)S(1)}, f32[528,512]{1,0:T(8,128)S(1)}, u32[]{:S(2)}, u32[]{:S(2)}) %collective-permute-start.11) | collective-permute-done | bytes 1081376 | tf_op jit(solution)/shard_map/ppermute | solution.py:375
  41.0 3.0 %collective-permute-start.13 = (f32[264,512]{1,0:T(8,128)S(1)}, f32[264,512]{1,0:T(8,128)S(1)}, u32[]{:S(2)}, u32[]{:S(2)}) collective-permute-start(f32[264,512]{1,0:T(8,128)S(1)} %cut.3), channel_id=1, source_target_pairs={{0,2},{1,7},{2,4},{3,1},{4,6},{5,3},{6,0},{7,5},{8,10},{9,15},{10,... | collective-permute-start | bytes 1622024 | tf_op jit(solution)/shard_map/ppermute | solution.py:375
  44.0 2.3 %collective-permute-done.8.pair.near.refs_2_ = f32[512,512]{1,0:T(8,128)S(1)} collective-permute-done((f32[512,512]{1,0:T(8,128)S(1)}, f32[512,512]{1,0:T(8,128)S(1)}, u32[]{:S(2)}, u32[]{:S(2)}) %collective-permute-start.8) | collective-permute-done | bytes 1048608 | tf_op jit(solution)/shard_map/ppermute | solution.py:386
  46.2 1.6 %collective-permute-start.9 = (f32[512,512]{1,0:T(8,128)S(1)}, f32[512,512]{1,0:T(8,128)S(1)}, u32[]{:S(2)}, u32[]{:S(2)}) collective-permute-start(f32[512,512]{1,0:T(8,128)S(1)} %collective-permute-done.8.pair.near.refs_2_), channel_id=1, source_target_pairs={{0,1},{1,0},{2,3},{3,2},{4,5},{5,4},{6,7},{7,6},{8,9},{9,8},{10,11... | collective-permute-start | bytes 3145736 | tf_op jit(solution)/shard_map/ppermute | solution.py:357
  47.9 2.4 %collective-permute-done.13.refs_0_ = f32[264,512]{1,0:T(8,128)S(1)} collective-permute-done((f32[264,512]{1,0:T(8,128)S(1)}, f32[264,512]{1,0:T(8,128)S(1)}, u32[]{:S(2)}, u32[]{:S(2)}) %collective-permute-start.13) | collective-permute-done | bytes 540704 | tf_op jit(solution)/shard_map/ppermute | solution.py:375
  50.3 3.4 %collective-permute-start.14 = (f32[264,512]{1,0:T(8,128)S(1)}, f32[264,512]{1,0:T(8,128)S(1)}, u32[]{:S(2)}, u32[]{:S(2)}) collective-permute-start(f32[264,512]{1,0:T(8,128)S(1)} %gate.8.refs_3_), channel_id=1, source_target_pairs={{0,1},{1,0},{2,3},{3,2},{4,5},{5,4},{6,7},{7,6},{8,9},{9,8},{10,11... | collective-permute-start | bytes 1622024 | tf_op jit(solution)/shard_map/ppermute | solution.py:357
  53.7 2.7 %collective-permute-start.10 = (f32[256,512]{1,0:T(8,128)S(1)}, f32[256,512]{1,0:T(8,128)S(1)}, u32[]{:S(2)}, u32[]{:S(2)}) collective-permute-start(f32[256,512]{1,0:T(8,128)S(1)} %cut.2.refs_1_), channel_id=1, source_target_pairs={{0,8},{1,25},{2,10},{3,27},{4,12},{5,29},{6,14},{7,31},{8,16},{9,1... | collective-permute-start | bytes 1572872 | tf_op jit(solution)/shard_map/ppermute | solution.py:386
  56.4 6.0 %noise.1 = (f32[4,64,512]{2,1,0:T(8,128)S(1)}, f32[8,512]{1,0:T(8,128)S(1)}, f32[520,512]{1,0:T(8,128)S(1)}) custom-call(bf16[3,512,512]{2,1,0:T(8,128)(2,1)S(1)} %get-tuple-element.38.e_hi, bf16[3,512,512]{2,1,0:T(8,128)(2,1)S(1)} %get-tuple-element.39.e_lo, f32[528,512]{1,0:T(8,128)S(1)} %pair.1.refs_1_.refs_0_, ...), custom_call_target="tpu_custom_call" | custom-call | tf_op jit(solution)/shard_map/noise/pallas_call | solution.py:42
  62.4 2.2 %second.1.refs_1_.moved = f32[520,512]{1,0:T(8,128)S(1)} custom-call(f32[520,512]{1,0:T(8,128)S(1)} %get-tuple-element.40.cov, f32[512,512]{1,0:T(8,128)S(1)} %collective-permute-done.8.pair.near.refs_2_, f32[512,512]{1,0:T(8,128)S(1)} %collective-permute-done.9.other.refs_3_), custom_call_target="tpu_custom_call" | custom-call | tf_op jit(solution)/shard_map/second/pallas_call | solution.py:42
  64.6 0.1 collective-permute-start.15
  64.7 1.9 %collective-permute-done.15.refs_5_ = f32[256,512]{1,0:T(8,128)S(1)} collective-permute-done((f32[256,512]{1,0:T(8,128)S(1)}, f32[256,512]{1,0:T(8,128)S(1)}, u32[]{:S(2)}, u32[]{:S(2)}) %collective-permute-start.15) | collective-permute-done | bytes 524320 | tf_op jit(solution)/shard_map/ppermute | solution.py:357
  66.6 4.8 %prefix.1 = (f32[64,512]{1,0:T(8,128)S(1)}, f32[144,512]{1,0:T(8,128)S(1)}, f32[144,512]{1,0:T(8,128)S(1)}, f32[144,512]{1,0:T(8,128)S(1)}) custom-call(f32[520,512]{1,0:T(8,128)S(1)} %get-tuple-element.40.cov, f32[520,512]{1,0:T(8,128)S(1)} %second.1.refs_1_.moved, bf16[512,512]{1,0:T(8,128)(2,1)S(1)} %get-tuple-element.35.refs_0_.refs_3_, ...), custom_call_target="tpu_custom_call" | custom-call | tf_op jit(solution)/shard_map/prefix/pallas_call | solution.py:42
  71.4 0.2 collective-permute-start.16
  71.5 2.7 %collective-permute-start.17 = (f32[144,512]{1,0:T(8,128)S(1)}, f32[144,512]{1,0:T(8,128)S(1)}, u32[]{:S(2)}, u32[]{:S(2)}) collective-permute-start(f32[144,512]{1,0:T(8,128)S(1)} %get-tuple-element.44), channel_id=1, source_target_pairs={{0,16},{8,24},{16,0},{24,8},{32,48},{40,56},{48,32},{56,40},{64,80... | collective-permute-start | bytes 884744 | tf_op jit(solution)/shard_map/ppermute | solution.py:360
  74.2 1.1 collective-permute-start.18
  75.3 1.3 collective-permute-start.19
  76.5 1.3 collective-permute-start.20
  77.8 3.4 %collective-permute-done.16.third = f32[144,512]{1,0:T(8,128)S(1)} collective-permute-done((f32[144,512]{1,0:T(8,128)S(1)}, f32[144,512]{1,0:T(8,128)S(1)}, u32[]{:S(2)}, u32[]{:S(2)}) %collective-permute-start.16) | collective-permute-done | bytes 294944 | tf_op jit(solution)/shard_map/ppermute | solution.py:360
  81.3 6.0 %collective-permute-done.17.second = f32[144,512]{1,0:T(8,128)S(1)} collective-permute-done((f32[144,512]{1,0:T(8,128)S(1)}, f32[144,512]{1,0:T(8,128)S(1)}, u32[]{:S(2)}, u32[]{:S(2)}) %collective-permute-start.17) | collective-permute-done | bytes 294944 | tf_op jit(solution)/shard_map/ppermute | solution.py:360
  87.3 0.5 collective-permute-done.18.first
  87.7 0.1 sum.1
  87.8 1.3 collective-permute-start.28
  89.2 0.1 collective-permute-start.21
  89.3 0.8 collective-permute-start.22
  90.0 1.3 collective-permute-start.29
  91.3 1.3 collective-permute-start.30
  92.6 1.1 collective-permute-done.28.refs_8_
  93.7 0.9 collective-permute-start.23
  94.6 2.7 %tail.1 = (bf16[512,512]{1,0:T(8,128)(2,1)S(1)}, bf16[512,512]{1,0:T(8,128)(2,1)S(1)}) custom-call(bf16[512,512]{1,0:T(8,128)(2,1)S(1)} %get-tuple-element.35.refs_0_.refs_3_, bf16[512,512]{1,0:T(8,128)(2,1)S(1)} %get-tuple-element.36.refs_1_.refs_4_, f32[512,512]{1,0:T(8,128)S(1)} %collective-permute-done.8.pair.near.refs_2_, ...), custom_call_target="tpu_custom_call" | custom-call | tf_op jit(solution)/shard_map/tail/pallas_call | solution.py:42
  97.3 0.1 collective-permute-done.29.second.refs_9_
  97.4 2.9 %collective-permute-start.24 = (f32[192,512]{1,0:T(8,128)S(1)}, f32[192,512]{1,0:T(8,128)S(1)}, u32[]{:S(2)}, u32[]{:S(2)}) collective-permute-start(f32[192,512]{1,0:T(8,128)S(1)} %pack_outer.1.refs_11_), channel_id=1, source_target_pairs={{0,1},{1,0},{2,3},{3,2},{4,5},{5,4},{6,7},{7,6},{8,9},{9,8},{10,11... | collective-permute-start | bytes 1179656 | tf_op jit(solution)/shard_map/ppermute | solution.py:357
  100.4 1.1 collective-permute-done.30.third.refs_10_
  101.5 0.1 blocks.1
  101.5 2.7 %collective-permute-start.34 = (f32[192,256]{1,0:T(8,128)S(1)}, f32[192,256]{1,0:T(8,128)S(1)}, u32[]{:S(2)}, u32[]{:S(2)}) collective-permute-start(f32[192,256]{1,0:T(8,128)S(1)} %get-tuple-element.64), channel_id=1, source_target_pairs={{0,2},{1,3},{2,4},{3,5},{4,6},{5,7},{6,0},{7,1},{8,10},{9,11},{10,... | collective-permute-start | bytes 589832 | tf_op jit(solution)/shard_map/ppermute | solution.py:370
  104.2 7.9 %collective-permute-start.25 = (f32[192,512]{1,0:T(8,128)S(1)}, f32[192,512]{1,0:T(8,128)S(1)}, u32[]{:S(2)}, u32[]{:S(2)}) collective-permute-start(f32[192,512]{1,0:T(8,128)S(1)} %collective-permute-done.21.refs_12_), channel_id=1, source_target_pairs={{0,1},{1,0},{2,3},{3,2},{4,5},{5,4},{6,7},{7,6},{8,9},{9,8},{10,11... | collective-permute-start | bytes 1179656 | tf_op jit(solution)/shard_map/ppermute | solution.py:357
  112.1 0.3 collective-permute-done.34.refs_15_
  112.5 2.1 %collective-permute-start.27 = (f32[192,512]{1,0:T(8,128)S(1)}, f32[192,512]{1,0:T(8,128)S(1)}, u32[]{:S(2)}, u32[]{:S(2)}) collective-permute-start(f32[192,512]{1,0:T(8,128)S(1)} %collective-permute-done.23.refs_14_), channel_id=1, source_target_pairs={{0,1},{1,0},{2,3},{3,2},{4,5},{5,4},{6,7},{7,6},{8,9},{9,8},{10,11... | collective-permute-start | bytes 1179656 | tf_op jit(solution)/shard_map/ppermute | solution.py:357
  114.6 0.1 collective-permute-start.31
  114.7 4.1 %collective-permute-done.32.refs_13_ = f32[192,384]{1,0:T(8,128)S(1)} collective-permute-done((f32[192,384]{1,0:T(8,128)S(1)}, f32[192,384]{1,0:T(8,128)S(1)}, u32[]{:S(2)}, u32[]{:S(2)}) %collective-permute-start.32) | collective-permute-done | bytes 294944 | tf_op jit(solution)/shard_map/ppermute | solution.py:370
  118.9 3.0 %collective-permute-start.33 = (f32[192,384]{1,0:T(8,128)S(1)}, f32[192,384]{1,0:T(8,128)S(1)}, u32[]{:S(2)}, u32[]{:S(2)}) collective-permute-start(f32[192,384]{1,0:T(8,128)S(1)} %collective-permute-done.32.refs_13_), channel_id=1, source_target_pairs={{0,1},{1,0},{2,3},{3,2},{4,5},{5,4},{6,7},{7,6},{8,9},{9,8},{10,11... | collective-permute-start | bytes 884744 | tf_op jit(solution)/shard_map/ppermute | solution.py:357
  121.9 1.7 %collective-permute-start.36 = (f32[192,128]{1,0:T(8,128)S(1)}, f32[192,128]{1,0:T(8,128)S(1)}, u32[]{:S(2)}, u32[]{:S(2)}) collective-permute-start(f32[192,128]{1,0:T(8,128)S(1)} %get-tuple-element.65), channel_id=1, source_target_pairs={{0,4},{1,5},{2,6},{3,7},{4,0},{5,1},{6,2},{7,3},{8,12},{9,13},{10,... | collective-permute-start | bytes 294920 | tf_op jit(solution)/shard_map/ppermute | solution.py:370
  123.7 0.3 collective-permute-start.35
  123.9 3.6 %outer.1 = (bf16[3,512,512]{2,1,0:T(8,128)(2,1)S(1)}, bf16[3,512,512]{2,1,0:T(8,128)(2,1)S(1)}, bf16[3,256,512]{2,1,0:T(8,128)(2,1)S(1)}, bf16[3,256,512]{2,1,0:T(8,128)(2,1)S(1)}, f32[264,512]{1,0:T(8,128)S(1)}) custom-call(bf16[512,512]{1,0:T(8,128)(2,1)S(1)} %get-tuple-element.41.refs_0_.refs_1_, bf16[512,512]{1,0:T(8,128)(2,1)S(1)} %get-tuple-element.42.refs_1_, ...), custom_call_target="tpu_custom_call" | custom-call | tf_op jit(solution)/shard_map/outer/pallas_call | solution.py:42
  127.5 0.4 collective-permute-done.36.refs_0_
  127.9 0.8 collective-permute-start.37
  128.7 0.9 collective-permute-done.37.refs_18_
  129.6 6.7 %final.1 = (f32[4,64,512]{2,1,0:T(8,128)}, f32[4,64]{1,0:T(4,128)}) custom-call(bf16[3,512,512]{2,1,0:T(8,128)(2,1)S(1)} %get-tuple-element.54.b_hi, bf16[3,512,512]{2,1,0:T(8,128)(2,1)S(1)} %get-tuple-element.55.b_lo, bf16[3,256,512]{2,1,0:T(8,128)(2,1)S(1)} %get-tuple-element.56.x_hi, bf16[3,256,512]{2,1,0:T(8,128)(2,1)S(1)} %get-tuple-element.57.x_lo, ...), custom_call_target="tpu_custom_call" | custom-call | tf_op jit(solution)/shard_map/final/pallas_call | solution.py:42
  (39 shorter events, 0.2 us)
Async XLA Ops:
  0.6 13.5 %collective-permute-start = (f32[256,512]{1,0:T(8,128)}, f32[256,512]{1,0:T(8,128)S(1)}, u32[]{:S(2)}, u32[]{:S(2)}) collective-permute-start(f32[256,512]{1,0:T(8,128)} %bitcast.3), channel_id=1, source_target_pairs={{0,2},{1,7},{2,4},{3,1},{4,6},{5,3},{6,0},{7,5},{8,10},{9,15},{10,... | collective-permute-start | bytes 1572872 | tf_op jit(solution)/shard_map/ppermute | solution.py:375
  5.3 1.0 copy-start
  6.3 0.7 copy-start.2
  7.1 11.4 %collective-permute-start.3 = (f32[264,512]{1,0:T(8,128)S(1)}, f32[264,512]{1,0:T(8,128)S(1)}, u32[]{:S(2)}, u32[]{:S(2)}) collective-permute-start(f32[264,512]{1,0:T(8,128)S(1)} %pack.1.refs_0_), channel_id=1, source_target_pairs={{0,1},{1,0},{2,3},{3,2},{4,5},{5,4},{6,7},{7,6},{8,9},{9,8},{10,11... | collective-permute-start | bytes 1622024 | tf_op jit(solution)/shard_map/ppermute | solution.py:357
  7.2 11.3 %collective-permute-start.1 = (f32[256,512]{1,0:T(8,128)}, f32[256,512]{1,0:T(8,128)S(1)}, u32[]{:S(2)}, u32[]{:S(2)}) collective-permute-start(f32[256,512]{1,0:T(8,128)} %bitcast.4), channel_id=1, source_target_pairs={{0,6},{1,3},{2,0},{3,5},{4,2},{5,7},{6,4},{7,1},{8,14},{9,11},{10,... | collective-permute-start | bytes 1572872 | tf_op jit(solution)/shard_map/ppermute | solution.py:375
  14.1 9.4 %collective-permute-start.2 = (f32[256,512]{1,0:T(8,128)S(1)}, f32[256,512]{1,0:T(8,128)S(1)}, u32[]{:S(2)}, u32[]{:S(2)}) collective-permute-start(f32[256,512]{1,0:T(8,128)S(1)} %collective-permute-done.refs_1_), channel_id=1, source_target_pairs={{0,2},{1,7},{2,4},{3,1},{4,6},{5,3},{6,0},{7,5},{8,10},{9,15},{10,... | collective-permute-start | bytes 1572872 | tf_op jit(solution)/shard_map/ppermute | solution.py:375
  17.5 10.9 %collective-permute-start.4 = (f32[256,512]{1,0:T(8,128)}, f32[256,512]{1,0:T(8,128)S(1)}, u32[]{:S(2)}, u32[]{:S(2)}) collective-permute-start(f32[256,512]{1,0:T(8,128)} %bitcast.5), channel_id=1, source_target_pairs={{0,1},{1,0},{2,3},{3,2},{4,5},{5,4},{6,7},{7,6},{8,9},{9,8},{10,11... | collective-permute-start | bytes 1572872 | tf_op jit(solution)/shard_map/ppermute | solution.py:357
  17.5 10.9 %collective-permute-start.5 = (f32[256,512]{1,0:T(8,128)S(1)}, f32[256,512]{1,0:T(8,128)S(1)}, u32[]{:S(2)}, u32[]{:S(2)}) collective-permute-start(f32[256,512]{1,0:T(8,128)S(1)} %collective-permute-done.refs_1_), channel_id=1, source_target_pairs={{0,1},{1,0},{2,3},{3,2},{4,5},{5,4},{6,7},{7,6},{8,9},{9,8},{10,11... | collective-permute-start | bytes 1572872 | tf_op jit(solution)/shard_map/ppermute | solution.py:357
  18.5 9.8 %collective-permute-start.6 = (f32[256,512]{1,0:T(8,128)S(1)}, f32[256,512]{1,0:T(8,128)S(1)}, u32[]{:S(2)}, u32[]{:S(2)}) collective-permute-start(f32[256,512]{1,0:T(8,128)S(1)} %collective-permute-done.1.refs_1_.refs_2_), channel_id=1, source_target_pairs={{0,1},{1,0},{2,3},{3,2},{4,5},{5,4},{6,7},{7,6},{8,9},{9,8},{10,11... | collective-permute-start | bytes 1572872 | tf_op jit(solution)/shard_map/ppermute | solution.py:357
  18.6 9.7 %copy-start.1 = (f32[4,64,512]{2,1,0:T(8,128)S(1)}, f32[4,64,512]{2,1,0:T(8,128)}, u32[]{:S(2)}) copy-start(f32[4,64,512]{2,1,0:T(8,128)} %param.3) | copy-start | bytes 1572868
  23.6 4.8 %collective-permute-start.7 = (f32[256,512]{1,0:T(8,128)S(1)}, f32[256,512]{1,0:T(8,128)S(1)}, u32[]{:S(2)}, u32[]{:S(2)}) collective-permute-start(f32[256,512]{1,0:T(8,128)S(1)} %gate.7.refs_3_), channel_id=1, source_target_pairs={{0,1},{1,0},{2,3},{3,2},{4,5},{5,4},{6,7},{7,6},{8,9},{9,8},{10,11... | collective-permute-start | bytes 1572872 | tf_op jit(solution)/shard_map/ppermute | solution.py:357
  26.6 14.3 %collective-permute-start.11 = (f32[528,512]{1,0:T(8,128)S(1)}, f32[528,512]{1,0:T(8,128)S(1)}, u32[]{:S(2)}, u32[]{:S(2)}) collective-permute-start(f32[528,512]{1,0:T(8,128)S(1)} %pair.1.refs_1_.refs_0_), channel_id=1, source_target_pairs={{0,2},{1,7},{2,4},{3,1},{4,6},{5,3},{6,0},{7,5},{8,10},{9,15},{10,... | collective-permute-start | bytes 3244040 | tf_op jit(solution)/shard_map/ppermute | solution.py:375
  31.7 14.5 %collective-permute-start.8 = (f32[512,512]{1,0:T(8,128)S(1)}, f32[512,512]{1,0:T(8,128)S(1)}, u32[]{:S(2)}, u32[]{:S(2)}) collective-permute-start(f32[512,512]{1,0:T(8,128)S(1)} %get-tuple-element.37), channel_id=1, source_target_pairs={{0,8},{1,25},{2,10},{3,27},{4,12},{5,29},{6,14},{7,31},{8,16},{9,1... | collective-permute-start | bytes 3145736 | tf_op jit(solution)/shard_map/ppermute | solution.py:386
  41.0 9.3 %collective-permute-start.13 = (f32[264,512]{1,0:T(8,128)S(1)}, f32[264,512]{1,0:T(8,128)S(1)}, u32[]{:S(2)}, u32[]{:S(2)}) collective-permute-start(f32[264,512]{1,0:T(8,128)S(1)} %cut.3), channel_id=1, source_target_pairs={{0,2},{1,7},{2,4},{3,1},{4,6},{5,3},{6,0},{7,5},{8,10},{9,15},{10,... | collective-permute-start | bytes 1622024 | tf_op jit(solution)/shard_map/ppermute | solution.py:375
  44.0 12.4 %collective-permute-start.12 = (f32[528,512]{1,0:T(8,128)S(1)}, f32[528,512]{1,0:T(8,128)S(1)}, u32[]{:S(2)}, u32[]{:S(2)}) collective-permute-start(f32[528,512]{1,0:T(8,128)S(1)} %collective-permute-done.11.pair.refs_1_), channel_id=1, source_target_pairs={{0,1},{1,0},{2,3},{3,2},{4,5},{5,4},{6,7},{7,6},{8,9},{9,8},{10,11... | collective-permute-start | bytes 3244040 | tf_op jit(solution)/shard_map/ppermute | solution.py:357
  46.2 16.2 %collective-permute-start.9 = (f32[512,512]{1,0:T(8,128)S(1)}, f32[512,512]{1,0:T(8,128)S(1)}, u32[]{:S(2)}, u32[]{:S(2)}) collective-permute-start(f32[512,512]{1,0:T(8,128)S(1)} %collective-permute-done.8.pair.near.refs_2_), channel_id=1, source_target_pairs={{0,1},{1,0},{2,3},{3,2},{4,5},{5,4},{6,7},{7,6},{8,9},{9,8},{10,11... | collective-permute-start | bytes 3145736 | tf_op jit(solution)/shard_map/ppermute | solution.py:357
  50.3 6.1 %collective-permute-start.14 = (f32[264,512]{1,0:T(8,128)S(1)}, f32[264,512]{1,0:T(8,128)S(1)}, u32[]{:S(2)}, u32[]{:S(2)}) collective-permute-start(f32[264,512]{1,0:T(8,128)S(1)} %gate.8.refs_3_), channel_id=1, source_target_pairs={{0,1},{1,0},{2,3},{3,2},{4,5},{5,4},{6,7},{7,6},{8,9},{9,8},{10,11... | collective-permute-start | bytes 1622024 | tf_op jit(solution)/shard_map/ppermute | solution.py:357
  53.7 10.9 %collective-permute-start.10 = (f32[256,512]{1,0:T(8,128)S(1)}, f32[256,512]{1,0:T(8,128)S(1)}, u32[]{:S(2)}, u32[]{:S(2)}) collective-permute-start(f32[256,512]{1,0:T(8,128)S(1)} %cut.2.refs_1_), channel_id=1, source_target_pairs={{0,8},{1,25},{2,10},{3,27},{4,12},{5,29},{6,14},{7,31},{8,16},{9,1... | collective-permute-start | bytes 1572872 | tf_op jit(solution)/shard_map/ppermute | solution.py:386
  64.6 2.0 %collective-permute-start.15 = (f32[256,512]{1,0:T(8,128)S(1)}, f32[256,512]{1,0:T(8,128)S(1)}, u32[]{:S(2)}, u32[]{:S(2)}) collective-permute-start(f32[256,512]{1,0:T(8,128)S(1)} %gate.9.refs_4_), channel_id=1, source_target_pairs={{0,1},{1,0},{2,3},{3,2},{4,5},{5,4},{6,7},{7,6},{8,9},{9,8},{10,11... | collective-permute-start | bytes 1572872 | tf_op jit(solution)/shard_map/ppermute | solution.py:357
  71.4 9.9 %collective-permute-start.16 = (f32[144,512]{1,0:T(8,128)S(1)}, f32[144,512]{1,0:T(8,128)S(1)}, u32[]{:S(2)}, u32[]{:S(2)}) collective-permute-start(f32[144,512]{1,0:T(8,128)S(1)} %get-tuple-element.43.own), channel_id=1, source_target_pairs={{0,8},{8,16},{16,24},{24,0},{32,40},{40,48},{48,56},{56,32},{64,72... | collective-permute-start | bytes 884744 | tf_op jit(solution)/shard_map/ppermute | solution.py:360
  71.5 15.7 %collective-permute-start.17 = (f32[144,512]{1,0:T(8,128)S(1)}, f32[144,512]{1,0:T(8,128)S(1)}, u32[]{:S(2)}, u32[]{:S(2)}) collective-permute-start(f32[144,512]{1,0:T(8,128)S(1)} %get-tuple-element.44), channel_id=1, source_target_pairs={{0,16},{8,24},{16,0},{24,8},{32,48},{40,56},{48,32},{56,40},{64,80... | collective-permute-start | bytes 884744 | tf_op jit(solution)/shard_map/ppermute | solution.py:360
  74.2 13.6 %collective-permute-start.18 = (f32[144,512]{1,0:T(8,128)S(1)}, f32[144,512]{1,0:T(8,128)S(1)}, u32[]{:S(2)}, u32[]{:S(2)}) collective-permute-start(f32[144,512]{1,0:T(8,128)S(1)} %get-tuple-element.45), channel_id=1, source_target_pairs={{0,24},{8,0},{16,8},{24,16},{32,56},{40,32},{48,40},{56,48},{64,88... | collective-permute-start | bytes 884744 | tf_op jit(solution)/shard_map/ppermute | solution.py:360
  75.3 13.9 %collective-permute-start.19 = (f32[64,512]{1,0:T(8,128)S(1)}, f32[64,512]{1,0:T(8,128)S(1)}, u32[]{:S(2)}, u32[]{:S(2)}) collective-permute-start(f32[64,512]{1,0:T(8,128)S(1)} %get-tuple-element.53), channel_id=1, source_target_pairs={{32,0},{40,8},{48,16},{56,24},{64,32},{72,40},{80,48},{88,56},{96,... | collective-permute-start | bytes 393224 | tf_op jit(solution)/shard_map/ppermute | solution.py:365
  76.5 12.6 %collective-permute-start.20 = (f32[64,512]{1,0:T(8,128)S(1)}, f32[64,512]{1,0:T(8,128)S(1)}, u32[]{:S(2)}, u32[]{:S(2)}) collective-permute-start(f32[64,512]{1,0:T(8,128)S(1)} %get-tuple-element.53), channel_id=1, source_target_pairs={{64,0},{72,8},{80,16},{88,24},{96,32},{104,40},{112,48},{120,56},{... | collective-permute-start | bytes 393224 | tf_op jit(solution)/shard_map/ppermute | solution.py:365
  87.8 5.9 %collective-permute-start.28 = (f32[72,512]{1,0:T(8,128)S(1)}, f32[72,512]{1,0:T(8,128)S(1)}, u32[]{:S(2)}, u32[]{:S(2)}) collective-permute-start(f32[72,512]{1,0:T(8,128)S(1)} %get-tuple-element.61), channel_id=1, source_target_pairs={{32,0},{40,8},{48,16},{56,24},{64,32},{72,40},{80,48},{88,56},{96,... | collective-permute-start | bytes 442376 | tf_op jit(solution)/shard_map/ppermute | solution.py:365
  89.2 15.1 %collective-permute-start.21 = (f32[192,512]{1,0:T(8,128)S(1)}, f32[192,512]{1,0:T(8,128)S(1)}, u32[]{:S(2)}, u32[]{:S(2)}) collective-permute-start(f32[192,512]{1,0:T(8,128)S(1)} %pack_outer.1.refs_11_), channel_id=1, source_target_pairs={{0,2},{1,3},{2,4},{3,5},{4,6},{5,7},{6,0},{7,1},{8,10},{9,11},{10,... | collective-permute-start | bytes 1179656 | tf_op jit(solution)/shard_map/ppermute | solution.py:370
  89.3 22.9 %collective-permute-start.22 = (f32[192,512]{1,0:T(8,128)S(1)}, f32[192,512]{1,0:T(8,128)S(1)}, u32[]{:S(2)}, u32[]{:S(2)}) collective-permute-start(f32[192,512]{1,0:T(8,128)S(1)} %pack_outer.1.refs_11_), channel_id=1, source_target_pairs={{0,4},{1,5},{2,6},{3,7},{4,0},{5,1},{6,2},{7,3},{8,12},{9,13},{10,... | collective-permute-start | bytes 1179656 | tf_op jit(solution)/shard_map/ppermute | solution.py:370
  90.0 7.4 %collective-permute-start.29 = (f32[72,512]{1,0:T(8,128)S(1)}, f32[72,512]{1,0:T(8,128)S(1)}, u32[]{:S(2)}, u32[]{:S(2)}) collective-permute-start(f32[72,512]{1,0:T(8,128)S(1)} %get-tuple-element.61), channel_id=1, source_target_pairs={{64,0},{72,8},{80,16},{88,24},{96,32},{104,40},{112,48},{120,56},{... | collective-permute-start | bytes 442376 | tf_op jit(solution)/shard_map/ppermute | solution.py:365
  91.3 10.2 %collective-permute-start.30 = (f32[72,512]{1,0:T(8,128)S(1)}, f32[72,512]{1,0:T(8,128)S(1)}, u32[]{:S(2)}, u32[]{:S(2)}) collective-permute-start(f32[72,512]{1,0:T(8,128)S(1)} %get-tuple-element.61), channel_id=1, source_target_pairs={{96,0},{104,8},{112,16},{120,24},{97,1},{105,9},{113,17},{121,25},... | collective-permute-start | bytes 442376 | tf_op jit(solution)/shard_map/ppermute | solution.py:365
  93.7 18.8 %collective-permute-start.23 = (f32[192,512]{1,0:T(8,128)S(1)}, f32[192,512]{1,0:T(8,128)S(1)}, u32[]{:S(2)}, u32[]{:S(2)}) collective-permute-start(f32[192,512]{1,0:T(8,128)S(1)} %pack_outer.1.refs_11_), channel_id=1, source_target_pairs={{0,6},{1,7},{2,0},{3,1},{4,2},{5,3},{6,4},{7,5},{8,14},{9,15},{10,... | collective-permute-start | bytes 1179656 | tf_op jit(solution)/shard_map/ppermute | solution.py:370
  97.4 17.2 %collective-permute-start.24 = (f32[192,512]{1,0:T(8,128)S(1)}, f32[192,512]{1,0:T(8,128)S(1)}, u32[]{:S(2)}, u32[]{:S(2)}) collective-permute-start(f32[192,512]{1,0:T(8,128)S(1)} %pack_outer.1.refs_11_), channel_id=1, source_target_pairs={{0,1},{1,0},{2,3},{3,2},{4,5},{5,4},{6,7},{7,6},{8,9},{9,8},{10,11... | collective-permute-start | bytes 1179656 | tf_op jit(solution)/shard_map/ppermute | solution.py:357
  101.5 10.9 %collective-permute-start.34 = (f32[192,256]{1,0:T(8,128)S(1)}, f32[192,256]{1,0:T(8,128)S(1)}, u32[]{:S(2)}, u32[]{:S(2)}) collective-permute-start(f32[192,256]{1,0:T(8,128)S(1)} %get-tuple-element.64), channel_id=1, source_target_pairs={{0,2},{1,3},{2,4},{3,5},{4,6},{5,7},{6,0},{7,1},{8,10},{9,11},{10,... | collective-permute-start | bytes 589832 | tf_op jit(solution)/shard_map/ppermute | solution.py:370
  104.2 17.7 %collective-permute-start.25 = (f32[192,512]{1,0:T(8,128)S(1)}, f32[192,512]{1,0:T(8,128)S(1)}, u32[]{:S(2)}, u32[]{:S(2)}) collective-permute-start(f32[192,512]{1,0:T(8,128)S(1)} %collective-permute-done.21.refs_12_), channel_id=1, source_target_pairs={{0,1},{1,0},{2,3},{3,2},{4,5},{5,4},{6,7},{7,6},{8,9},{9,8},{10,11... | collective-permute-start | bytes 1179656 | tf_op jit(solution)/shard_map/ppermute | solution.py:357
  112.1 11.5 %collective-permute-start.26 = (f32[192,512]{1,0:T(8,128)S(1)}, f32[192,512]{1,0:T(8,128)S(1)}, u32[]{:S(2)}, u32[]{:S(2)}) collective-permute-start(f32[192,512]{1,0:T(8,128)S(1)} %collective-permute-done.22.refs_13_), channel_id=1, source_target_pairs={{0,1},{1,0},{2,3},{3,2},{4,5},{5,4},{6,7},{7,6},{8,9},{9,8},{10,11... | collective-permute-start | bytes 1179656 | tf_op jit(solution)/shard_map/ppermute | solution.py:357
  112.5 6.4 %collective-permute-start.32 = (f32[192,384]{1,0:T(8,128)S(1)}, f32[192,384]{1,0:T(8,128)S(1)}, u32[]{:S(2)}, u32[]{:S(2)}) collective-permute-start(f32[192,384]{1,0:T(8,128)S(1)} %get-tuple-element.63), channel_id=1, source_target_pairs={{0,6},{1,7},{2,0},{3,1},{4,2},{5,3},{6,4},{7,5},{8,14},{9,15},{10,... | collective-permute-start | bytes 884744 | tf_op jit(solution)/shard_map/ppermute | solution.py:370
  112.5 11.4 %collective-permute-start.27 = (f32[192,512]{1,0:T(8,128)S(1)}, f32[192,512]{1,0:T(8,128)S(1)}, u32[]{:S(2)}, u32[]{:S(2)}) collective-permute-start(f32[192,512]{1,0:T(8,128)S(1)} %collective-permute-done.23.refs_14_), channel_id=1, source_target_pairs={{0,1},{1,0},{2,3},{3,2},{4,5},{5,4},{6,7},{7,6},{8,9},{9,8},{10,11... | collective-permute-start | bytes 1179656 | tf_op jit(solution)/shard_map/ppermute | solution.py:357
  114.6 14.0 %collective-permute-start.31 = (f32[192,512]{1,0:T(8,128)S(1)}, f32[192,512]{1,0:T(8,128)S(1)}, u32[]{:S(2)}, u32[]{:S(2)}) collective-permute-start(f32[192,512]{1,0:T(8,128)S(1)} %get-tuple-element.62.refs_11_), channel_id=1, source_target_pairs={{0,1},{1,0},{2,3},{3,2},{4,5},{5,4},{6,7},{7,6},{8,9},{9,8},{10,11... | collective-permute-start | bytes 1179656 | tf_op jit(solution)/shard_map/ppermute | solution.py:357
  118.9 9.8 %collective-permute-start.33 = (f32[192,384]{1,0:T(8,128)S(1)}, f32[192,384]{1,0:T(8,128)S(1)}, u32[]{:S(2)}, u32[]{:S(2)}) collective-permute-start(f32[192,384]{1,0:T(8,128)S(1)} %collective-permute-done.32.refs_13_), channel_id=1, source_target_pairs={{0,1},{1,0},{2,3},{3,2},{4,5},{5,4},{6,7},{7,6},{8,9},{9,8},{10,11... | collective-permute-start | bytes 884744 | tf_op jit(solution)/shard_map/ppermute | solution.py:357
  121.9 5.9 %collective-permute-start.36 = (f32[192,128]{1,0:T(8,128)S(1)}, f32[192,128]{1,0:T(8,128)S(1)}, u32[]{:S(2)}, u32[]{:S(2)}) collective-permute-start(f32[192,128]{1,0:T(8,128)S(1)} %get-tuple-element.65), channel_id=1, source_target_pairs={{0,4},{1,5},{2,6},{3,7},{4,0},{5,1},{6,2},{7,3},{8,12},{9,13},{10,... | collective-permute-start | bytes 294920 | tf_op jit(solution)/shard_map/ppermute | solution.py:370
  123.7 5.0 %collective-permute-start.35 = (f32[192,256]{1,0:T(8,128)S(1)}, f32[192,256]{1,0:T(8,128)S(1)}, u32[]{:S(2)}, u32[]{:S(2)}) collective-permute-start(f32[192,256]{1,0:T(8,128)S(1)} %collective-permute-done.34.refs_15_), channel_id=1, source_target_pairs={{0,1},{1,0},{2,3},{3,2},{4,5},{5,4},{6,7},{7,6},{8,9},{9,8},{10,11... | collective-permute-start | bytes 589832 | tf_op jit(solution)/shard_map/ppermute | solution.py:357
  127.9 1.7 %collective-permute-start.37 = (f32[192,128]{1,0:T(8,128)S(1)}, f32[192,128]{1,0:T(8,128)S(1)}, u32[]{:S(2)}, u32[]{:S(2)}) collective-permute-start(f32[192,128]{1,0:T(8,128)S(1)} %gate.11.refs_17_), channel_id=1, source_target_pairs={{0,1},{1,0},{2,3},{3,2},{4,5},{5,4},{6,7},{7,6},{8,9},{9,8},{10,11... | collective-permute-start | bytes 294920 | tf_op jit(solution)/shard_map/ppermute | solution.py:357

commit v4 on v3

--- a/solution.py
+++ b/solution.py
@@ -224,7 +224,8 @@
         (a_hi[twice, own_rows(), :], a_lo[twice, own_rows(), :]), (a_hi[twice], a_lo[twice]), moved[...], short
     )
     f_hi[...], f_lo[...] = head
-    gain[...] = dot3((f_hi[own_rows(), :], f_lo[own_rows(), :]), (a_hi[3], a_lo[3]), NN)
+    half = at(position()[1], HALF)
+    gain[...] = dot3((f_hi[half, :], f_lo[half, :]), (a_hi[3], a_lo[3]), NN)
 
 
 def second_kernel(cov, near, other, moved, a_hi, a_lo, scratch):
@@ -268,10 +269,11 @@
             tail = split(dot3((a_hi[block], a_lo[block]), tail, NN))
 
 
-def blocks_kernel(first, second, third, rows, back, ahead, across):
-    z = position()[0]
-    for index, piece in enumerate((first, second, third)):
-        rows[index * ROWS : (index + 1) * ROWS, :] = piece[:ROWS, :]
+def blocks_kernel(first, second, third, fourth, rows, back, ahead, across):
+    z, x = position()[0], lax.axis_index("tm") // 4
+    for index, piece in enumerate((first, second, third, fourth)):
+        known = x + index < 3 if index < 3 else x >= 0
+        rows[index * ROWS : (index + 1) * ROWS, :] = jnp.where(known, piece[:ROWS, :], 0.0)
     for step, messages in ((0, (back, ahead, across)), (1, (back,)), (2, (back,)), (3, (ahead,))):
         block = rows[:, at((z + step) % 4, 128)]
         for message in messages:
@@ -300,45 +302,48 @@
         cov[at(column, 128), at(row, 128)] = cov[at(row, 128), at(column, 128)].T
 
 
-def pack_outer_kernel(first, second, later, rows):
-    rows[:ROWS, :] = first[...]
-    rows[ROWS : 2 * ROWS, :] = second[...]
-    rows[2 * ROWS :, :] = later[:ROWS, :]
-
-
-def outer_kernel(*refs):
-    p_hi, p_lo, offset, suffix, pieces = refs[0], refs[1], refs[2], refs[3:11], refs[11:19]
-    b_hi, b_lo, x_hi, x_lo, base, gains, later, s_hi, s_lo = refs[19:]
-    z, c, _ = position()
-    spots = [2 * ((z - step + 4) % 4) + core for core in (c, 1 - c) for step in range(4)]
-    for piece, panel in zip(pieces, spots):
-        gains[0, at(panel), :] = piece[:ROWS, :]
-        gains[1, at(panel), :] = piece[ROWS : 2 * ROWS, :]
-        later[at(panel), :] = piece[2 * ROWS :, :]
+def outer_kernel(p_hi, p_lo, *refs):
+    suffix, pieces, (b_hi, b_lo, x_hi, x_lo, s_hi, s_lo, gain) = refs[:8], refs[8:10], refs[10:]
+    c = position()[1]
+    for core, piece in zip((c, 1 - c), pieces):
+        gain[at(core, HALF), :] = piece[...]
     for k in range(4):
         s_hi[k * ROWS : (k + 1) * ROWS, :] = suffix[2 * k][own_rows(), :]
         s_lo[k * ROWS : (k + 1) * ROWS, :] = suffix[2 * k + 1][own_rows(), :]
-    steps = (s_hi[...], s_lo[...])
-    base[:HALF, :] = dot3(steps, split(later[...]), NN)
-    base[HALF:, :] = offset[ROWS:, :]
     b_hi[0], b_lo[0] = p_hi[...], p_lo[...]
-    x_hi[0], x_lo[0] = split(dot3(steps, (b_hi[0], b_lo[0]), NN))
-    for index in range(2):
-        gain = split(gains[index])
-        b_hi[index + 1], b_lo[index + 1] = split(dot3((b_hi[index], b_lo[index]), gain, NN))
-        x_hi[index + 1], x_lo[index + 1] = split(dot3((x_hi[index], x_lo[index]), gain, NN))
-
-
-def final_kernel(b_hi, b_lo, x_hi, x_lo, base, rows_in, means_in, *refs):
-    suffix, offsets, pieces, (out, means, cov, stack, short, every) = refs[:8], refs[8:11], refs[11:19], refs[19:]
+    x_hi[0], x_lo[0] = split(dot3((s_hi[...], s_lo[...]), (b_hi[0], b_lo[0]), NN))
+    parts = split(gain[...])
+    b_hi[1], b_lo[1] = split(dot3((b_hi[0], b_lo[0]), parts, NN))
+    x_hi[1], x_lo[1] = split(dot3((x_hi[0], x_lo[0]), parts, NN))
+
+
+def outermost_kernel(b_hi, b_lo, x_hi, x_lo, mine, other, c_hi, c_lo, y_hi, y_lo, gain):
+    c = position()[1]
+    for core, piece in zip((c, 1 - c), (mine, other)):
+        gain[at(core, HALF), :] = piece[...]
+    parts = split(gain[...])
+    c_hi[...], c_lo[...] = split(dot3((b_hi[1], b_lo[1]), parts, NN))
+    y_hi[...], y_lo[...] = split(dot3((x_hi[1], x_lo[1]), parts, NN))
+
+
+def final_kernel(b_hi, b_lo, x_hi, x_lo, c_hi, c_lo, y_hi, y_lo, s_hi, s_lo, rows_in, means_in, *refs):
+    suffix, offsets, pieces, (out, means, cov, stack, short, every) = refs[:8], refs[8:12], refs[12:20], refs[20:]
     z, c, _ = position()
-    inner = base[...]
-    for index in range(3):
+    inner = 0.0
+    for index in range(4):
         fill_symmetric(cov, index, pieces[0:2], pieces[2:4], pieces[4:6], pieces[6:8], z, c)
-        stack[:HALF, :] = dot3((x_hi[index], x_lo[index]), split(cov[...]), NN)
-        stack[HALF:, :] = offsets[index][ROWS:, :]
-        inner = inner + dot3(split(stack[...]), (b_hi[index], b_lo[index]), NT)
-    stack[...] = inner
+        if index < 2:
+            left, right = (x_hi[index], x_lo[index]), (b_hi[index], b_lo[index])
+        elif index == 2:
+            left, right = (y_hi[...], y_lo[...]), (c_hi[...], c_lo[...])
+        else:
+            left = (s_hi[...], s_lo[...])
+        stack[:HALF, :] = dot3(left, split(cov[...]), NN)
+        known = lax.axis_index("tm") // 4 + index < 3 if index < 3 else z >= 0
+        stack[HALF:, :] = jnp.where(known, offsets[index][ROWS:, :], 0.0)
+        if index < 3:
+            inner = inner + dot3(split(stack[...]), right, NT)
+    stack[...] = stack[...] + inner
     for k in range(4):
         short[:ROWS, :] = stack[k * ROWS : (k + 1) * ROWS, :]
         short[ROWS:, :] = stack[HALF:, :]
@@ -363,7 +368,7 @@
 
     def back_x(value, step):
         return lax.ppermute(
-            value, "tm", [(4 * x + y, 4 * (x - step) + y) for x in range(step, 4) for y in range(4)]
+            value, "tm", [(4 * x + y, 4 * ((x - step) % 4) + y) for x in range(4) for y in range(4)]
         )
 
     def along_z(value, step):
@@ -422,11 +427,12 @@
     (half_noise,) = call(cut_kernel, "cut", [full(HALF + 8, D)], [near_noise])
     far_gain, far_noise = paired_y(half_gain, 1), gate(paired_z(half_noise, 1), half_gain)
     other_gain = other_core(near_gain)
+    other_far = other_core(far_noise)
     rows, means, cov = call(
         noise_kernel,
         "noise",
         [full(4, ROWS, D), full(8, D), full(AUG, D)],
-        [e_hi, e_lo, pair, near_noise, other_core(near_noise), far_noise, other_core(far_noise)],
+        [e_hi, e_lo, pair, near_noise, other_core(near_noise), far_noise, other_far],
         [pltpu.VMEM((AUG, D), F32)],
     )
     (moved,) = call(
@@ -441,17 +447,11 @@
     gain, to_third, to_second, to_first = call(
         prefix_kernel,
         "prefix",
-        [full(ROWS, D)] + [full(2 * ROWS + 16, D)] * 3,
+        [full(HALF, D)] + [full(2 * ROWS + 16, D)] * 3,
         [cov, moved, *blocks],
         [pltpu.VMEM((4, D, D), BF16)] * 2 + [pltpu.VMEM((D, D), BF16)] * 2 + [pltpu.VMEM((ROWS + 8, D), F32)],
     )
-    total, beyond = call(
-        sum_kernel,
-        "sum",
-        [full(ROWS + 8, D)] * 2,
-        [to_third, along_y(to_third, 1), along_y(to_second, 2), along_y(to_first, 3)],
-    )
-    far_covs = [back_x(total, step) for step in (1, 2, 3)]
+    from_third, from_second, from_first = along_y(to_third, 1), along_y(to_second, 2), along_y(to_first, 3)
     p_hi, p_lo = call(
         tail_kernel,
         "tail",
@@ -459,34 +459,45 @@
         blocks,
         [pltpu.VMEM((4, D, D), BF16)] * 2,
     )
-    (packed,) = call(pack_outer_kernel, "pack_outer", [full(3 * ROWS, D)], [back_x(gain, 1), back_x(gain, 2), beyond])
-    outer = both_cores([packed, *(along_z(packed, step) for step in (1, 2, 3))])
+    next_gain = back_x(gain, 1)
+    total, beyond = call(
+        sum_kernel,
+        "sum",
+        [full(ROWS + 8, D)] * 2,
+        [gate(to_third, next_gain, p_hi), from_third, from_second, from_first],
+    )
+    next_gain = gate(next_gain, total)
+    far_covs = [back_x(total, step) for step in (1, 2, 3)]
     own, *messages = call(
         blocks_kernel,
         "blocks",
-        [full(3 * ROWS, D), full(3 * ROWS, 384), full(3 * ROWS, 256), full(3 * ROWS, 128)],
-        [gate(far_covs[0], p_hi), *far_covs[1:]],
-    )
-    b_hi, b_lo, x_hi, x_lo, base = call(
+        [full(4 * ROWS, D), full(4 * ROWS, 384), full(4 * ROWS, 256), full(4 * ROWS, 128)],
+        [*far_covs, beyond],
+    )
+    back, ahead, across = (along_z(value, step) for value, step in zip(messages, (-1, 1, 2)))
+    after_gain = back_x(gate(next_gain, far_covs[0], far_covs[1], far_covs[2]), 1)
+    b_hi, b_lo, x_hi, x_lo, s_hi, s_lo = call(
         outer_kernel,
         "outer",
-        [part(3, D, D), part(3, D, D), part(3, HALF, D), part(3, HALF, D), full(HALF + 8, D)],
-        [p_hi, p_lo, beyond, *suffix, *outer],
-        [
-            pltpu.VMEM((2, D, D), F32),
-            pltpu.VMEM((D, D), F32),
-            pltpu.VMEM((HALF, D), BF16),
-            pltpu.VMEM((HALF, D), BF16),
-        ],
-    )
-    back, ahead, across = (along_z(value, step) for value, step in zip(messages, (-1, 1, 2)))
-    covs = [gate(value, base) if value is across else value for value in (own, back, ahead, across)]
+        [part(2, D, D), part(2, D, D), part(2, HALF, D), part(2, HALF, D), part(HALF, D), part(HALF, D)],
+        [p_hi, p_lo, *suffix, next_gain, other_core(next_gain)],
+        [pltpu.VMEM((D, D), F32)],
+    )
+    after_gain = gate(after_gain, back, ahead, across, s_hi)
+    outermost = call(
+        outermost_kernel,
+        "outermost",
+        [part(D, D), part(D, D), part(HALF, D), part(HALF, D)],
+        [b_hi, b_lo, x_hi, x_lo, after_gain, other_core(after_gain)],
+        [pltpu.VMEM((D, D), F32)],
+    )
+    covs = [own, back, ahead, across]
     covs = [piece for value in covs for piece in (value, other_core(value))]
     out, mean_rows = call(
         final_kernel,
         "final",
         [full(4, ROWS, D), full(4, ROWS)],
-        [b_hi, b_lo, x_hi, x_lo, base, rows, means, *suffix, *far_covs, *covs],
+        [b_hi, b_lo, x_hi, x_lo, *outermost, s_hi, s_lo, rows, means, *suffix, *far_covs, beyond, *covs],
         [
             pltpu.VMEM((D, D), F32),
             pltpu.VMEM((HALF + 8, D), F32),

time: 138 us -> 128 us (0.928); the launches traced: 136 us -> 128 us
  starting transfers between devices: 61.1 us -> 40.8 us
  waiting for transfers between devices: 43 us -> 54.3 us
    ppermute x17 -> x15, starting transfers between devices: 25.9 us -> 12.7 us  [other_core(): lax.ppermute(value, 'panel', [(2 * z + c, 2 * z + 1 - c) for z in range(4...]
    ppermute x5, waiting for transfers between devices: 2.32 us -> 11 us  [back_x(): lax.ppermute(value, 'tm', [(4 * x + y, 4 * ((x - step) % 4) + y) for x in...]
    ppermute x6 -> x3, waiting for transfers between devices: 4.85 us -> 9.56 us  [along_z(): lax.ppermute(value, 'panel', [(2 * z + c, 2 * ((z + step) % 4) + c) for z...]
    ppermute x6 -> x3, starting transfers between devices: 6.16 us -> 1.53 us  [along_z(): lax.ppermute(value, 'panel', [(2 * z + c, 2 * ((z + step) % 4) + c) for z...]
    ppermute x5, starting transfers between devices: 6.44 us -> 4.03 us  [back_x(): lax.ppermute(value, 'tm', [(4 * x + y, 4 * ((x - step) % 4) + y) for x in...]
    ppermute x3, waiting for transfers between devices: 9.9 us -> 7.85 us  [along_y(): lax.ppermute(value, 'tm', [(4 * x + y, 4 * x + (y + step) % 4) for x in r...]
    ppermute x17 -> x15, waiting for transfers between devices: 2.87 us -> 2.84 us  [other_core(): lax.ppermute(value, 'panel', [(2 * z + c, 2 * z + 1 - c) for z in range(4...]
  transfers between devices with their start and end apart: 38 -> 33, of which waited for: 17 -> 20; matrix products, arithmetic and copies ran while one was open for 0% -> 0% of each run, Pallas kernels for 13% -> 14%
where the time goes in v4:
time: 128 us
  waiting for transfers between devices  54.3 us (42%)
  starting transfers between devices  40.8 us (32%)
  Pallas kernels  30.2 us (24%)
  local copies, waits for them, and re-layouts  1.73 us (1%)
    pallas_call x14, Pallas kernels, call(): pl.pallas_call(kernel, out_shape=outs, in_specs=[ANY if index in outside...  30.2 us
    ppermute x5, waiting for transfers between devices, paired_z(): lax.ppermute(value, 'panel', [(2 * z + c, 2 * ((z + step * (1 - 2 * c)) %...  20.8 us
    ppermute x5, starting transfers between devices, paired_z(): lax.ppermute(value, 'panel', [(2 * z + c, 2 * ((z + step * (1 - 2 * c)) %...  13.1 us
    ppermute x15, starting transfers between devices, other_core(): lax.ppermute(value, 'panel', [(2 * z + c, 2 * z + 1 - c) for z in range(4...  12.7 us
    ppermute x5, waiting for transfers between devices, back_x(): lax.ppermute(value, 'tm', [(4 * x + y, 4 * ((x - step) % 4) + y) for x in...  11 us
    ppermute x3, waiting for transfers between devices, along_z(): lax.ppermute(value, 'panel', [(2 * z + c, 2 * ((z + step) % 4) + c) for z...  9.56 us
    ppermute x3, waiting for transfers between devices, along_y(): lax.ppermute(value, 'tm', [(4 * x + y, 4 * x + (y + step) % 4) for x in r...  7.85 us
    ppermute x2, starting transfers between devices, paired_y(): return lax.ppermute(value, ('tm', 'panel'), pairs)  5.54 us
  transfers between devices with their start and end apart: 33, of which 20 were waited for; matrix products, arithmetic and copies ran while one was open for 0% of the time, Pallas kernels for 14%

profile of v4, /device:TPU:1, one launch (start us, length us, event | category | flops | bytes accessed | tf_op | source)
XLA Modules:
  0.0 127.8 jit_solution(13136695557413204371)
XLA Ops:
  0.6 4.7 %collective-permute-start = (f32[256,512]{1,0:T(8,128)}, f32[256,512]{1,0:T(8,128)S(1)}, u32[]{:S(2)}, u32[]{:S(2)}) collective-permute-start(f32[256,512]{1,0:T(8,128)} %bitcast.3), channel_id=1, source_target_pairs={{0,2},{1,7},{2,4},{3,1},{4,6},{5,3},{6,0},{7,5},{8,10},{9,15},{10,... | collective-permute-start | bytes 1572872 | tf_op jit(solution)/shard_map/ppermute | solution.py:380
  5.3 1.0 copy-done
  6.3 0.7 copy-done.2
  7.0 0.1 pack.1.refs_0_
  7.1 0.1 collective-permute-start.3
  7.2 0.4 collective-permute-start.1
  7.7 6.5 %collective-permute-done.refs_1_ = f32[256,512]{1,0:T(8,128)S(1)} collective-permute-done((f32[256,512]{1,0:T(8,128)}, f32[256,512]{1,0:T(8,128)S(1)}, u32[]{:S(2)}, u32[]{:S(2)}) %collective-permute-start) | collective-permute-done | bytes 524320 | tf_op jit(solution)/shard_map/ppermute | solution.py:380
  14.1 3.3 %collective-permute-start.2 = (f32[256,512]{1,0:T(8,128)S(1)}, f32[256,512]{1,0:T(8,128)S(1)}, u32[]{:S(2)}, u32[]{:S(2)}) collective-permute-start(f32[256,512]{1,0:T(8,128)S(1)} %collective-permute-done.refs_1_), channel_id=1, source_target_pairs={{0,2},{1,7},{2,4},{3,1},{4,6},{5,3},{6,0},{7,5},{8,10},{9,15},{10,... | collective-permute-start | bytes 1572872 | tf_op jit(solution)/shard_map/ppermute | solution.py:380
  17.5 0.0 collective-permute-start.4
  17.5 0.5 collective-permute-start.5
  18.0 0.6 collective-permute-done.1.refs_1_.refs_2_
  18.6 0.1 pair.1.refs_1_.refs_0_
  18.6 0.0 copy-start.1
  18.7 4.9 %collective-permute-done.2.refs_0_ = f32[256,512]{1,0:T(8,128)S(1)} collective-permute-done((f32[256,512]{1,0:T(8,128)S(1)}, f32[256,512]{1,0:T(8,128)S(1)}, u32[]{:S(2)}, u32[]{:S(2)}) %collective-permute-start.2) | collective-permute-done | bytes 524320 | tf_op jit(solution)/shard_map/ppermute | solution.py:380
  23.6 3.0 %collective-permute-start.7 = (f32[256,512]{1,0:T(8,128)S(1)}, f32[256,512]{1,0:T(8,128)S(1)}, u32[]{:S(2)}, u32[]{:S(2)}) collective-permute-start(f32[256,512]{1,0:T(8,128)S(1)} %gate.9.refs_3_), channel_id=1, source_target_pairs={{0,1},{1,0},{2,3},{3,2},{4,5},{5,4},{6,7},{7,6},{8,9},{9,8},{10,11... | collective-permute-start | bytes 1572872 | tf_op jit(solution)/shard_map/ppermute | solution.py:362
  26.6 1.7 %collective-permute-start.11 = (f32[528,512]{1,0:T(8,128)S(1)}, f32[528,512]{1,0:T(8,128)S(1)}, u32[]{:S(2)}, u32[]{:S(2)}) collective-permute-start(f32[528,512]{1,0:T(8,128)S(1)} %pair.1.refs_1_.refs_0_), channel_id=1, source_target_pairs={{0,2},{1,7},{2,4},{3,1},{4,6},{5,3},{6,0},{7,5},{8,10},{9,15},{10,... | collective-permute-start | bytes 3244040 | tf_op jit(solution)/shard_map/ppermute | solution.py:380
  28.4 3.3 %block.1 = (bf16[3,512,512]{2,1,0:T(8,128)(2,1)S(1)}, bf16[3,512,512]{2,1,0:T(8,128)(2,1)S(1)}, bf16[512,512]{1,0:T(8,128)(2,1)S(1)}, bf16[512,512]{1,0:T(8,128)...) custom-call(f32[256,512]{1,0:T(8,128)S(1)} %bitcast.6, ...), custom_call_target="tpu_custom_call" | custom-call | tf_op jit(solution)/shard_map/block/pallas_call | solution.py:42
  31.7 2.8 %collective-permute-start.8 = (f32[512,512]{1,0:T(8,128)S(1)}, f32[512,512]{1,0:T(8,128)S(1)}, u32[]{:S(2)}, u32[]{:S(2)}) collective-permute-start(f32[512,512]{1,0:T(8,128)S(1)} %get-tuple-element.42), channel_id=1, source_target_pairs={{0,8},{1,25},{2,10},{3,27},{4,12},{5,29},{6,14},{7,31},{8,16},{9,1... | collective-permute-start | bytes 3145736 | tf_op jit(solution)/shard_map/ppermute | solution.py:391
  34.5 6.4 %collective-permute-done.11.pair.refs_1_ = f32[528,512]{1,0:T(8,128)S(1)} collective-permute-done((f32[528,512]{1,0:T(8,128)S(1)}, f32[528,512]{1,0:T(8,128)S(1)}, u32[]{:S(2)}, u32[]{:S(2)}) %collective-permute-start.11) | collective-permute-done | bytes 1081376 | tf_op jit(solution)/shard_map/ppermute | solution.py:380
  41.0 3.0 %collective-permute-start.13 = (f32[264,512]{1,0:T(8,128)S(1)}, f32[264,512]{1,0:T(8,128)S(1)}, u32[]{:S(2)}, u32[]{:S(2)}) collective-permute-start(f32[264,512]{1,0:T(8,128)S(1)} %cut.3), channel_id=1, source_target_pairs={{0,2},{1,7},{2,4},{3,1},{4,6},{5,3},{6,0},{7,5},{8,10},{9,15},{10,... | collective-permute-start | bytes 1622024 | tf_op jit(solution)/shard_map/ppermute | solution.py:380
  44.0 2.3 %collective-permute-done.8.pair.near.refs_2_ = f32[512,512]{1,0:T(8,128)S(1)} collective-permute-done((f32[512,512]{1,0:T(8,128)S(1)}, f32[512,512]{1,0:T(8,128)S(1)}, u32[]{:S(2)}, u32[]{:S(2)}) %collective-permute-start.8) | collective-permute-done | bytes 1048608 | tf_op jit(solution)/shard_map/ppermute | solution.py:391
  46.2 1.6 %collective-permute-start.9 = (f32[512,512]{1,0:T(8,128)S(1)}, f32[512,512]{1,0:T(8,128)S(1)}, u32[]{:S(2)}, u32[]{:S(2)}) collective-permute-start(f32[512,512]{1,0:T(8,128)S(1)} %collective-permute-done.8.pair.near.refs_2_), channel_id=1, source_target_pairs={{0,1},{1,0},{2,3},{3,2},{4,5},{5,4},{6,7},{7,6},{8,9},{9,8},{10,11... | collective-permute-start | bytes 3145736 | tf_op jit(solution)/shard_map/ppermute | solution.py:362
  47.9 2.4 %collective-permute-done.13.refs_0_ = f32[264,512]{1,0:T(8,128)S(1)} collective-permute-done((f32[264,512]{1,0:T(8,128)S(1)}, f32[264,512]{1,0:T(8,128)S(1)}, u32[]{:S(2)}, u32[]{:S(2)}) %collective-permute-start.13) | collective-permute-done | bytes 540704 | tf_op jit(solution)/shard_map/ppermute | solution.py:380
  50.3 3.4 %collective-permute-start.14 = (f32[264,512]{1,0:T(8,128)S(1)}, f32[264,512]{1,0:T(8,128)S(1)}, u32[]{:S(2)}, u32[]{:S(2)}) collective-permute-start(f32[264,512]{1,0:T(8,128)S(1)} %gate.10.refs_3_), channel_id=1, source_target_pairs={{0,1},{1,0},{2,3},{3,2},{4,5},{5,4},{6,7},{7,6},{8,9},{9,8},{10,11... | collective-permute-start | bytes 1622024 | tf_op jit(solution)/shard_map/ppermute | solution.py:362
  53.7 2.7 %collective-permute-start.10 = (f32[256,512]{1,0:T(8,128)S(1)}, f32[256,512]{1,0:T(8,128)S(1)}, u32[]{:S(2)}, u32[]{:S(2)}) collective-permute-start(f32[256,512]{1,0:T(8,128)S(1)} %cut.2.refs_1_), channel_id=1, source_target_pairs={{0,8},{1,25},{2,10},{3,27},{4,12},{5,29},{6,14},{7,31},{8,16},{9,1... | collective-permute-start | bytes 1572872 | tf_op jit(solution)/shard_map/ppermute | solution.py:391
  56.4 6.0 %noise.1 = (f32[4,64,512]{2,1,0:T(8,128)S(1)}, f32[8,512]{1,0:T(8,128)S(1)}, f32[520,512]{1,0:T(8,128)S(1)}) custom-call(bf16[3,512,512]{2,1,0:T(8,128)(2,1)S(1)} %get-tuple-element.43.e_hi, bf16[3,512,512]{2,1,0:T(8,128)(2,1)S(1)} %get-tuple-element.44.e_lo, f32[528,512]{1,0:T(8,128)S(1)} %pair.1.refs_1_.refs_0_, ...), custom_call_target="tpu_custom_call" | custom-call | tf_op jit(solution)/shard_map/noise/pallas_call | solution.py:42
  62.4 2.2 %second.1.refs_1_.moved = f32[520,512]{1,0:T(8,128)S(1)} custom-call(f32[520,512]{1,0:T(8,128)S(1)} %get-tuple-element.45.cov, f32[512,512]{1,0:T(8,128)S(1)} %collective-permute-done.8.pair.near.refs_2_, f32[512,512]{1,0:T(8,128)S(1)} %collective-permute-done.9.other.refs_3_), custom_call_target="tpu_custom_call" | custom-call | tf_op jit(solution)/shard_map/second/pallas_call | solution.py:42
  64.6 0.1 collective-permute-start.15
  64.7 1.9 %collective-permute-done.15.refs_5_ = f32[256,512]{1,0:T(8,128)S(1)} collective-permute-done((f32[256,512]{1,0:T(8,128)S(1)}, f32[256,512]{1,0:T(8,128)S(1)}, u32[]{:S(2)}, u32[]{:S(2)}) %collective-permute-start.15) | collective-permute-done | bytes 524320 | tf_op jit(solution)/shard_map/ppermute | solution.py:362
  66.6 5.0 %prefix.1 = (f32[256,512]{1,0:T(8,128)S(1)}, f32[144,512]{1,0:T(8,128)S(1)}, f32[144,512]{1,0:T(8,128)S(1)}, f32[144,512]{1,0:T(8,128)S(1)}) custom-call(f32[520,512]{1,0:T(8,128)S(1)} %get-tuple-element.45.cov, f32[520,512]{1,0:T(8,128)S(1)} %second.1.refs_1_.moved, bf16[512,512]{1,0:T(8,128)(2,1)S(1)} %get-tuple-element.40.refs_0_, ...), custom_call_target="tpu_custom_call" | custom-call | tf_op jit(solution)/shard_map/prefix/pallas_call | solution.py:42
  71.5 2.5 %collective-permute-start.16 = (f32[256,512]{1,0:T(8,128)S(1)}, f32[256,512]{1,0:T(8,128)S(1)}, u32[]{:S(2)}, u32[]{:S(2)}) collective-permute-start(f32[256,512]{1,0:T(8,128)S(1)} %get-tuple-element.54), channel_id=1, source_target_pairs={{0,96},{8,104},{16,112},{24,120},{32,0},{40,8},{48,16},{56,24},{64... | collective-permute-start | bytes 1572872 | tf_op jit(solution)/shard_map/ppermute | solution.py:370
  74.1 0.1 collective-permute-start.17
  74.2 2.7 %collective-permute-start.18 = (f32[144,512]{1,0:T(8,128)S(1)}, f32[144,512]{1,0:T(8,128)S(1)}, u32[]{:S(2)}, u32[]{:S(2)}) collective-permute-start(f32[144,512]{1,0:T(8,128)S(1)} %get-tuple-element.56), channel_id=1, source_target_pairs={{0,16},{8,24},{16,0},{24,8},{32,48},{40,56},{48,32},{56,40},{64,80... | collective-permute-start | bytes 884744 | tf_op jit(solution)/shard_map/ppermute | solution.py:365
  76.9 1.1 collective-permute-start.19
  77.9 2.7 %tail.1 = (bf16[512,512]{1,0:T(8,128)(2,1)S(1)}, bf16[512,512]{1,0:T(8,128)(2,1)S(1)}) custom-call(bf16[512,512]{1,0:T(8,128)(2,1)S(1)} %get-tuple-element.40.refs_0_, bf16[512,512]{1,0:T(8,128)(2,1)S(1)} %get-tuple-element.41.refs_1_, f32[512,512]{1,0:T(8,128)S(1)} %collective-permute-done.8.pair.near.refs_2_, ...), custom_call_target="tpu_custom_call" | custom-call | tf_op jit(solution)/shard_map/tail/pallas_call | solution.py:42
  80.6 3.0 %collective-permute-done.17.third = f32[144,512]{1,0:T(8,128)S(1)} collective-permute-done((f32[144,512]{1,0:T(8,128)S(1)}, f32[144,512]{1,0:T(8,128)S(1)}, u32[]{:S(2)}, u32[]{:S(2)}) %collective-permute-start.17) | collective-permute-done | bytes 294944 | tf_op jit(solution)/shard_map/ppermute | solution.py:365
  83.6 1.6 %collective-permute-done.16.refs_1_.refs_0_ = f32[256,512]{1,0:T(8,128)S(1)} collective-permute-done((f32[256,512]{1,0:T(8,128)S(1)}, f32[256,512]{1,0:T(8,128)S(1)}, u32[]{:S(2)}, u32[]{:S(2)}) %collective-permute-start.16) | collective-permute-done | bytes 524320 | tf_op jit(solution)/shard_map/ppermute | solution.py:370
  85.3 4.3 %collective-permute-done.18.second = f32[144,512]{1,0:T(8,128)S(1)} collective-permute-done((f32[144,512]{1,0:T(8,128)S(1)}, f32[144,512]{1,0:T(8,128)S(1)}, u32[]{:S(2)}, u32[]{:S(2)}) %collective-permute-start.18) | collective-permute-done | bytes 294944 | tf_op jit(solution)/shard_map/ppermute | solution.py:365
  89.6 0.5 collective-permute-done.19.first
  90.1 0.1 sum.1
  90.2 1.6 %collective-permute-start.20 = (f32[256,512]{1,0:T(8,128)S(1)}, f32[256,512]{1,0:T(8,128)S(1)}, u32[]{:S(2)}, u32[]{:S(2)}) collective-permute-start(f32[256,512]{1,0:T(8,128)S(1)} %gate.13.refs_8_.refs_0_), channel_id=1, source_target_pairs={{0,1},{1,0},{2,3},{3,2},{4,5},{5,4},{6,7},{7,6},{8,9},{9,8},{10,11... | collective-permute-start | bytes 1572872 | tf_op jit(solution)/shard_map/ppermute | solution.py:362
  91.8 0.6 collective-permute-start.21
  92.4 0.2 collective-permute-start.22
  92.6 0.7 collective-permute-start.23
  93.3 0.1 collective-permute-done.20.refs_9_
  93.4 1.9 %outer.1 = (bf16[2,512,512]{2,1,0:T(8,128)(2,1)S(1)}, bf16[2,512,512]{2,1,0:T(8,128)(2,1)S(1)}, bf16[2,256,512]{2,1,0:T(8,128)(2,1)S(1)}, bf16[2,256,512]{2,1,0:...) custom-call(bf16[512,512]{1,0:T(8,128)(2,1)S(1)} %get-tuple-element.46.refs_2_.p_hi, ...), custom_call_target="tpu_custom_call" | custom-call | tf_op jit(solution)/shard_map/outer/pallas_call | solution.py:42
  95.3 2.0 %collective-permute-done.21.refs_1_.first.refs_8_ = f32[72,512]{1,0:T(8,128)S(1)} collective-permute-done((f32[72,512]{1,0:T(8,128)S(1)}, f32[72,512]{1,0:T(8,128)S(1)}, u32[]{:S(2)}, u32[]{:S(2)}) %collective-permute-start.21) | collective-permute-done | bytes 147488 | tf_op jit(solution)/shard_map/ppermute | solution.py:370
  97.2 1.8 %collective-permute-done.22.refs_2_.second.refs_9_ = f32[72,512]{1,0:T(8,128)S(1)} collective-permute-done((f32[72,512]{1,0:T(8,128)S(1)}, f32[72,512]{1,0:T(8,128)S(1)}, u32[]{:S(2)}, u32[]{:S(2)}) %collective-permute-start.22) | collective-permute-done | bytes 147488 | tf_op jit(solution)/shard_map/ppermute | solution.py:370
  99.0 3.8 %collective-permute-done.23.refs_3_.third.refs_10_ = f32[72,512]{1,0:T(8,128)S(1)} collective-permute-done((f32[72,512]{1,0:T(8,128)S(1)}, f32[72,512]{1,0:T(8,128)S(1)}, u32[]{:S(2)}, u32[]{:S(2)}) %collective-permute-start.23) | collective-permute-done | bytes 147488 | tf_op jit(solution)/shard_map/ppermute | solution.py:370
  102.8 0.1 blocks.1
  103.0 0.1 collective-permute-start.25
  103.1 1.5 %collective-permute-start.26 = (f32[256,256]{1,0:T(8,128)S(1)}, f32[256,256]{1,0:T(8,128)S(1)}, u32[]{:S(2)}, u32[]{:S(2)}) collective-permute-start(f32[256,256]{1,0:T(8,128)S(1)} %get-tuple-element.65), channel_id=1, source_target_pairs={{0,2},{1,3},{2,4},{3,5},{4,6},{5,7},{6,0},{7,1},{8,10},{9,11},{10,... | collective-permute-start | bytes 786440 | tf_op jit(solution)/shard_map/ppermute | solution.py:375
  104.5 7.2 %collective-permute-done.27.refs_3_.refs_18_ = f32[256,128]{1,0:T(8,128)S(1)} collective-permute-done((f32[256,128]{1,0:T(8,128)S(1)}, f32[256,128]{1,0:T(8,128)S(1)}, u32[]{:S(2)}, u32[]{:S(2)}) %collective-permute-start.27) | collective-permute-done | bytes 131104 | tf_op jit(solution)/shard_map/ppermute | solution.py:375
  111.8 2.3 %collective-permute-done.26.refs_2_.refs_16_ = f32[256,256]{1,0:T(8,128)S(1)} collective-permute-done((f32[256,256]{1,0:T(8,128)S(1)}, f32[256,256]{1,0:T(8,128)S(1)}, u32[]{:S(2)}, u32[]{:S(2)}) %collective-permute-start.26) | collective-permute-done | bytes 262176 | tf_op jit(solution)/shard_map/ppermute | solution.py:375
  114.1 1.8 %collective-permute-done.24.refs_0_ = f32[256,512]{1,0:T(8,128)S(1)} collective-permute-done((f32[256,512]{1,0:T(8,128)S(1)}, f32[256,512]{1,0:T(8,128)S(1)}, u32[]{:S(2)}, u32[]{:S(2)}) %collective-permute-start.24) | collective-permute-done | bytes 524320 | tf_op jit(solution)/shard_map/ppermute | solution.py:370
  115.9 1.3 %collective-permute-start.28 = (f32[256,512]{1,0:T(8,128)S(1)}, f32[256,512]{1,0:T(8,128)S(1)}, u32[]{:S(2)}, u32[]{:S(2)}) collective-permute-start(f32[256,512]{1,0:T(8,128)S(1)} %gate.15.mine), channel_id=1, source_target_pairs={{0,1},{1,0},{2,3},{3,2},{4,5},{5,4},{6,7},{7,6},{8,9},{9,8},{10,11... | collective-permute-start | bytes 1572872 | tf_op jit(solution)/shard_map/ppermute | solution.py:362
  117.2 0.0 collective-permute-start.29
  117.2 0.5 collective-permute-start.30
  117.7 0.0 collective-permute-start.31
  117.7 0.5 collective-permute-start.32
  118.2 0.5 collective-permute-done.28.other
  118.7 1.5 %outermost.1 = (bf16[512,512]{1,0:T(8,128)(2,1)S(1)}, bf16[512,512]{1,0:T(8,128)(2,1)S(1)}, bf16[256,512]{1,0:T(8,128)(2,1)S(1)}, bf16[256,512]{1,0:T(8,128)(2,1)S(1)}) custom-call(bf16[2,512,512]{2,1,0:T(8,128)(2,1)S(1)} %get-tuple-element.59.b_hi, bf16[2,512,512]{2,1,0:T(8,128)(2,1)S(1)} %get-tuple-element.60.b_lo, ...), custom_call_target="tpu_custom_call" | custom-call | tf_op jit(solution)/shard_map/outermost/pallas_call | solution.py:42
  120.3 0.3 collective-permute-done.32.refs_19_
  120.6 7.2 %final.1 = (f32[4,64,512]{2,1,0:T(8,128)}, f32[4,64]{1,0:T(4,128)}) custom-call(bf16[2,512,512]{2,1,0:T(8,128)(2,1)S(1)} %get-tuple-element.59.b_hi, bf16[2,512,512]{2,1,0:T(8,128)(2,1)S(1)} %get-tuple-element.60.b_lo, bf16[2,256,512]{2,1,0:T(8,128)(2,1)S(1)} %get-tuple-element.61.x_hi, bf16[2,256,512]{2,1,0:T(8,128)(2,1)S(1)} %get-tuple-element.62.x_lo, ...), custom_call_target="tpu_custom_call" | custom-call | tf_op jit(solution)/shard_map/final/pallas_call | solution.py:42
  (30 shorter events, 0.1 us)
Async XLA Ops:
  0.6 13.5 %collective-permute-start = (f32[256,512]{1,0:T(8,128)}, f32[256,512]{1,0:T(8,128)S(1)}, u32[]{:S(2)}, u32[]{:S(2)}) collective-permute-start(f32[256,512]{1,0:T(8,128)} %bitcast.3), channel_id=1, source_target_pairs={{0,2},{1,7},{2,4},{3,1},{4,6},{5,3},{6,0},{7,5},{8,10},{9,15},{10,... | collective-permute-start | bytes 1572872 | tf_op jit(solution)/shard_map/ppermute | solution.py:380
  5.3 1.0 copy-start
  6.3 0.7 copy-start.2
  7.1 11.4 %collective-permute-start.3 = (f32[264,512]{1,0:T(8,128)S(1)}, f32[264,512]{1,0:T(8,128)S(1)}, u32[]{:S(2)}, u32[]{:S(2)}) collective-permute-start(f32[264,512]{1,0:T(8,128)S(1)} %pack.1.refs_0_), channel_id=1, source_target_pairs={{0,1},{1,0},{2,3},{3,2},{4,5},{5,4},{6,7},{7,6},{8,9},{9,8},{10,11... | collective-permute-start | bytes 1622024 | tf_op jit(solution)/shard_map/ppermute | solution.py:362
  7.2 11.3 %collective-permute-start.1 = (f32[256,512]{1,0:T(8,128)}, f32[256,512]{1,0:T(8,128)S(1)}, u32[]{:S(2)}, u32[]{:S(2)}) collective-permute-start(f32[256,512]{1,0:T(8,128)} %bitcast.4), channel_id=1, source_target_pairs={{0,6},{1,3},{2,0},{3,5},{4,2},{5,7},{6,4},{7,1},{8,14},{9,11},{10,... | collective-permute-start | bytes 1572872 | tf_op jit(solution)/shard_map/ppermute | solution.py:380
  14.1 9.4 %collective-permute-start.2 = (f32[256,512]{1,0:T(8,128)S(1)}, f32[256,512]{1,0:T(8,128)S(1)}, u32[]{:S(2)}, u32[]{:S(2)}) collective-permute-start(f32[256,512]{1,0:T(8,128)S(1)} %collective-permute-done.refs_1_), channel_id=1, source_target_pairs={{0,2},{1,7},{2,4},{3,1},{4,6},{5,3},{6,0},{7,5},{8,10},{9,15},{10,... | collective-permute-start | bytes 1572872 | tf_op jit(solution)/shard_map/ppermute | solution.py:380
  17.5 10.9 %collective-permute-start.4 = (f32[256,512]{1,0:T(8,128)}, f32[256,512]{1,0:T(8,128)S(1)}, u32[]{:S(2)}, u32[]{:S(2)}) collective-permute-start(f32[256,512]{1,0:T(8,128)} %bitcast.5), channel_id=1, source_target_pairs={{0,1},{1,0},{2,3},{3,2},{4,5},{5,4},{6,7},{7,6},{8,9},{9,8},{10,11... | collective-permute-start | bytes 1572872 | tf_op jit(solution)/shard_map/ppermute | solution.py:362
  17.5 10.9 %collective-permute-start.5 = (f32[256,512]{1,0:T(8,128)S(1)}, f32[256,512]{1,0:T(8,128)S(1)}, u32[]{:S(2)}, u32[]{:S(2)}) collective-permute-start(f32[256,512]{1,0:T(8,128)S(1)} %collective-permute-done.refs_1_), channel_id=1, source_target_pairs={{0,1},{1,0},{2,3},{3,2},{4,5},{5,4},{6,7},{7,6},{8,9},{9,8},{10,11... | collective-permute-start | bytes 1572872 | tf_op jit(solution)/shard_map/ppermute | solution.py:362
  18.5 9.8 %collective-permute-start.6 = (f32[256,512]{1,0:T(8,128)S(1)}, f32[256,512]{1,0:T(8,128)S(1)}, u32[]{:S(2)}, u32[]{:S(2)}) collective-permute-start(f32[256,512]{1,0:T(8,128)S(1)} %collective-permute-done.1.refs_1_.refs_2_), channel_id=1, source_target_pairs={{0,1},{1,0},{2,3},{3,2},{4,5},{5,4},{6,7},{7,6},{8,9},{9,8},{10,11... | collective-permute-start | bytes 1572872 | tf_op jit(solution)/shard_map/ppermute | solution.py:362
  18.6 9.7 %copy-start.1 = (f32[4,64,512]{2,1,0:T(8,128)S(1)}, f32[4,64,512]{2,1,0:T(8,128)}, u32[]{:S(2)}) copy-start(f32[4,64,512]{2,1,0:T(8,128)} %param.3) | copy-start | bytes 1572868
  23.6 4.8 %collective-permute-start.7 = (f32[256,512]{1,0:T(8,128)S(1)}, f32[256,512]{1,0:T(8,128)S(1)}, u32[]{:S(2)}, u32[]{:S(2)}) collective-permute-start(f32[256,512]{1,0:T(8,128)S(1)} %gate.9.refs_3_), channel_id=1, source_target_pairs={{0,1},{1,0},{2,3},{3,2},{4,5},{5,4},{6,7},{7,6},{8,9},{9,8},{10,11... | collective-permute-start | bytes 1572872 | tf_op jit(solution)/shard_map/ppermute | solution.py:362
  26.6 14.3 %collective-permute-start.11 = (f32[528,512]{1,0:T(8,128)S(1)}, f32[528,512]{1,0:T(8,128)S(1)}, u32[]{:S(2)}, u32[]{:S(2)}) collective-permute-start(f32[528,512]{1,0:T(8,128)S(1)} %pair.1.refs_1_.refs_0_), channel_id=1, source_target_pairs={{0,2},{1,7},{2,4},{3,1},{4,6},{5,3},{6,0},{7,5},{8,10},{9,15},{10,... | collective-permute-start | bytes 3244040 | tf_op jit(solution)/shard_map/ppermute | solution.py:380
  31.7 14.5 %collective-permute-start.8 = (f32[512,512]{1,0:T(8,128)S(1)}, f32[512,512]{1,0:T(8,128)S(1)}, u32[]{:S(2)}, u32[]{:S(2)}) collective-permute-start(f32[512,512]{1,0:T(8,128)S(1)} %get-tuple-element.42), channel_id=1, source_target_pairs={{0,8},{1,25},{2,10},{3,27},{4,12},{5,29},{6,14},{7,31},{8,16},{9,1... | collective-permute-start | bytes 3145736 | tf_op jit(solution)/shard_map/ppermute | solution.py:391
  41.0 9.3 %collective-permute-start.13 = (f32[264,512]{1,0:T(8,128)S(1)}, f32[264,512]{1,0:T(8,128)S(1)}, u32[]{:S(2)}, u32[]{:S(2)}) collective-permute-start(f32[264,512]{1,0:T(8,128)S(1)} %cut.3), channel_id=1, source_target_pairs={{0,2},{1,7},{2,4},{3,1},{4,6},{5,3},{6,0},{7,5},{8,10},{9,15},{10,... | collective-permute-start | bytes 1622024 | tf_op jit(solution)/shard_map/ppermute | solution.py:380
  44.0 12.4 %collective-permute-start.12 = (f32[528,512]{1,0:T(8,128)S(1)}, f32[528,512]{1,0:T(8,128)S(1)}, u32[]{:S(2)}, u32[]{:S(2)}) collective-permute-start(f32[528,512]{1,0:T(8,128)S(1)} %collective-permute-done.11.pair.refs_1_), channel_id=1, source_target_pairs={{0,1},{1,0},{2,3},{3,2},{4,5},{5,4},{6,7},{7,6},{8,9},{9,8},{10,11... | collective-permute-start | bytes 3244040 | tf_op jit(solution)/shard_map/ppermute | solution.py:362
  46.2 16.2 %collective-permute-start.9 = (f32[512,512]{1,0:T(8,128)S(1)}, f32[512,512]{1,0:T(8,128)S(1)}, u32[]{:S(2)}, u32[]{:S(2)}) collective-permute-start(f32[512,512]{1,0:T(8,128)S(1)} %collective-permute-done.8.pair.near.refs_2_), channel_id=1, source_target_pairs={{0,1},{1,0},{2,3},{3,2},{4,5},{5,4},{6,7},{7,6},{8,9},{9,8},{10,11... | collective-permute-start | bytes 3145736 | tf_op jit(solution)/shard_map/ppermute | solution.py:362
  50.3 6.1 %collective-permute-start.14 = (f32[264,512]{1,0:T(8,128)S(1)}, f32[264,512]{1,0:T(8,128)S(1)}, u32[]{:S(2)}, u32[]{:S(2)}) collective-permute-start(f32[264,512]{1,0:T(8,128)S(1)} %gate.10.refs_3_), channel_id=1, source_target_pairs={{0,1},{1,0},{2,3},{3,2},{4,5},{5,4},{6,7},{7,6},{8,9},{9,8},{10,11... | collective-permute-start | bytes 1622024 | tf_op jit(solution)/shard_map/ppermute | solution.py:362
  53.7 10.9 %collective-permute-start.10 = (f32[256,512]{1,0:T(8,128)S(1)}, f32[256,512]{1,0:T(8,128)S(1)}, u32[]{:S(2)}, u32[]{:S(2)}) collective-permute-start(f32[256,512]{1,0:T(8,128)S(1)} %cut.2.refs_1_), channel_id=1, source_target_pairs={{0,8},{1,25},{2,10},{3,27},{4,12},{5,29},{6,14},{7,31},{8,16},{9,1... | collective-permute-start | bytes 1572872 | tf_op jit(solution)/shard_map/ppermute | solution.py:391
  64.6 2.0 %collective-permute-start.15 = (f32[256,512]{1,0:T(8,128)S(1)}, f32[256,512]{1,0:T(8,128)S(1)}, u32[]{:S(2)}, u32[]{:S(2)}) collective-permute-start(f32[256,512]{1,0:T(8,128)S(1)} %gate.11.refs_4_), channel_id=1, source_target_pairs={{0,1},{1,0},{2,3},{3,2},{4,5},{5,4},{6,7},{7,6},{8,9},{9,8},{10,11... | collective-permute-start | bytes 1572872 | tf_op jit(solution)/shard_map/ppermute | solution.py:362
  71.5 13.7 %collective-permute-start.16 = (f32[256,512]{1,0:T(8,128)S(1)}, f32[256,512]{1,0:T(8,128)S(1)}, u32[]{:S(2)}, u32[]{:S(2)}) collective-permute-start(f32[256,512]{1,0:T(8,128)S(1)} %get-tuple-element.54), channel_id=1, source_target_pairs={{0,96},{8,104},{16,112},{24,120},{32,0},{40,8},{48,16},{56,24},{64... | collective-permute-start | bytes 1572872 | tf_op jit(solution)/shard_map/ppermute | solution.py:370
  74.1 9.5 %collective-permute-start.17 = (f32[144,512]{1,0:T(8,128)S(1)}, f32[144,512]{1,0:T(8,128)S(1)}, u32[]{:S(2)}, u32[]{:S(2)}) collective-permute-start(f32[144,512]{1,0:T(8,128)S(1)} %get-tuple-element.55.refs_0_), channel_id=1, source_target_pairs={{0,8},{8,16},{16,24},{24,0},{32,40},{40,48},{48,56},{56,32},{64,72... | collective-permute-start | bytes 884744 | tf_op jit(solution)/shard_map/ppermute | solution.py:365
  74.2 15.4 %collective-permute-start.18 = (f32[144,512]{1,0:T(8,128)S(1)}, f32[144,512]{1,0:T(8,128)S(1)}, u32[]{:S(2)}, u32[]{:S(2)}) collective-permute-start(f32[144,512]{1,0:T(8,128)S(1)} %get-tuple-element.56), channel_id=1, source_target_pairs={{0,16},{8,24},{16,0},{24,8},{32,48},{40,56},{48,32},{56,40},{64,80... | collective-permute-start | bytes 884744 | tf_op jit(solution)/shard_map/ppermute | solution.py:365
  76.9 13.3 %collective-permute-start.19 = (f32[144,512]{1,0:T(8,128)S(1)}, f32[144,512]{1,0:T(8,128)S(1)}, u32[]{:S(2)}, u32[]{:S(2)}) collective-permute-start(f32[144,512]{1,0:T(8,128)S(1)} %get-tuple-element.57), channel_id=1, source_target_pairs={{0,24},{8,0},{16,8},{24,16},{32,56},{40,32},{48,40},{56,48},{64,88... | collective-permute-start | bytes 884744 | tf_op jit(solution)/shard_map/ppermute | solution.py:365
  90.2 3.2 %collective-permute-start.20 = (f32[256,512]{1,0:T(8,128)S(1)}, f32[256,512]{1,0:T(8,128)S(1)}, u32[]{:S(2)}, u32[]{:S(2)}) collective-permute-start(f32[256,512]{1,0:T(8,128)S(1)} %gate.13.refs_8_.refs_0_), channel_id=1, source_target_pairs={{0,1},{1,0},{2,3},{3,2},{4,5},{5,4},{6,7},{7,6},{8,9},{9,8},{10,11... | collective-permute-start | bytes 1572872 | tf_op jit(solution)/shard_map/ppermute | solution.py:362
  91.8 5.4 %collective-permute-start.21 = (f32[72,512]{1,0:T(8,128)S(1)}, f32[72,512]{1,0:T(8,128)S(1)}, u32[]{:S(2)}, u32[]{:S(2)}) collective-permute-start(f32[72,512]{1,0:T(8,128)S(1)} %get-tuple-element.58.refs_1_), channel_id=1, source_target_pairs={{0,96},{8,104},{16,112},{24,120},{32,0},{40,8},{48,16},{56,24},{64... | collective-permute-start | bytes 442376 | tf_op jit(solution)/shard_map/ppermute | solution.py:370
  92.4 6.6 %collective-permute-start.22 = (f32[72,512]{1,0:T(8,128)S(1)}, f32[72,512]{1,0:T(8,128)S(1)}, u32[]{:S(2)}, u32[]{:S(2)}) collective-permute-start(f32[72,512]{1,0:T(8,128)S(1)} %get-tuple-element.58.refs_1_), channel_id=1, source_target_pairs={{0,64},{8,72},{16,80},{24,88},{32,96},{40,104},{48,112},{56,120},{... | collective-permute-start | bytes 442376 | tf_op jit(solution)/shard_map/ppermute | solution.py:370
  92.6 10.2 %collective-permute-start.23 = (f32[72,512]{1,0:T(8,128)S(1)}, f32[72,512]{1,0:T(8,128)S(1)}, u32[]{:S(2)}, u32[]{:S(2)}) collective-permute-start(f32[72,512]{1,0:T(8,128)S(1)} %get-tuple-element.58.refs_1_), channel_id=1, source_target_pairs={{0,32},{8,40},{16,48},{24,56},{32,64},{40,72},{48,80},{56,88},{64,... | collective-permute-start | bytes 442376 | tf_op jit(solution)/shard_map/ppermute | solution.py:370
  102.8 13.0 %collective-permute-start.24 = (f32[256,512]{1,0:T(8,128)S(1)}, f32[256,512]{1,0:T(8,128)S(1)}, u32[]{:S(2)}, u32[]{:S(2)}) collective-permute-start(f32[256,512]{1,0:T(8,128)S(1)} %gate.14), channel_id=1, source_target_pairs={{0,96},{8,104},{16,112},{24,120},{32,0},{40,8},{48,16},{56,24},{64... | collective-permute-start | bytes 1572872 | tf_op jit(solution)/shard_map/ppermute | solution.py:370
  103.0 11.1 %collective-permute-start.25 = (f32[256,384]{1,0:T(8,128)S(1)}, f32[256,384]{1,0:T(8,128)S(1)}, u32[]{:S(2)}, u32[]{:S(2)}) collective-permute-start(f32[256,384]{1,0:T(8,128)S(1)} %get-tuple-element.64), channel_id=1, source_target_pairs={{0,6},{1,7},{2,0},{3,1},{4,2},{5,3},{6,4},{7,5},{8,14},{9,15},{10,... | collective-permute-start | bytes 1179656 | tf_op jit(solution)/shard_map/ppermute | solution.py:375
  103.1 11.0 %collective-permute-start.26 = (f32[256,256]{1,0:T(8,128)S(1)}, f32[256,256]{1,0:T(8,128)S(1)}, u32[]{:S(2)}, u32[]{:S(2)}) collective-permute-start(f32[256,256]{1,0:T(8,128)S(1)} %get-tuple-element.65), channel_id=1, source_target_pairs={{0,2},{1,3},{2,4},{3,5},{4,6},{5,7},{6,0},{7,1},{8,10},{9,11},{10,... | collective-permute-start | bytes 786440 | tf_op jit(solution)/shard_map/ppermute | solution.py:375
  104.5 7.2 %collective-permute-start.27 = (f32[256,128]{1,0:T(8,128)S(1)}, f32[256,128]{1,0:T(8,128)S(1)}, u32[]{:S(2)}, u32[]{:S(2)}) collective-permute-start(f32[256,128]{1,0:T(8,128)S(1)} %get-tuple-element.66), channel_id=1, source_target_pairs={{0,4},{1,5},{2,6},{3,7},{4,0},{5,1},{6,2},{7,3},{8,12},{9,13},{10,... | collective-permute-start | bytes 393224 | tf_op jit(solution)/shard_map/ppermute | solution.py:375
  115.9 2.9 %collective-permute-start.28 = (f32[256,512]{1,0:T(8,128)S(1)}, f32[256,512]{1,0:T(8,128)S(1)}, u32[]{:S(2)}, u32[]{:S(2)}) collective-permute-start(f32[256,512]{1,0:T(8,128)S(1)} %gate.15.mine), channel_id=1, source_target_pairs={{0,1},{1,0},{2,3},{3,2},{4,5},{5,4},{6,7},{7,6},{8,9},{9,8},{10,11... | collective-permute-start | bytes 1572872 | tf_op jit(solution)/shard_map/ppermute | solution.py:362
  117.2 3.4 %collective-permute-start.29 = (f32[256,512]{1,0:T(8,128)S(1)}, f32[256,512]{1,0:T(8,128)S(1)}, u32[]{:S(2)}, u32[]{:S(2)}) collective-permute-start(f32[256,512]{1,0:T(8,128)S(1)} %get-tuple-element.75.refs_12_), channel_id=1, source_target_pairs={{0,1},{1,0},{2,3},{3,2},{4,5},{5,4},{6,7},{7,6},{8,9},{9,8},{10,11... | collective-permute-start | bytes 1572872 | tf_op jit(solution)/shard_map/ppermute | solution.py:362
  117.2 3.4 %collective-permute-start.30 = (f32[256,384]{1,0:T(8,128)S(1)}, f32[256,384]{1,0:T(8,128)S(1)}, u32[]{:S(2)}, u32[]{:S(2)}) collective-permute-start(f32[256,384]{1,0:T(8,128)S(1)} %collective-permute-done.25.refs_1_.refs_14_), channel_id=1, source_target_pairs={{0,1},{1,0},{2,3},{3,2},{4,5},{5,4},{6,7},{7,6},{8,9},{9,8},{10,11... | collective-permute-start | bytes 1179656 | tf_op jit(solution)/shard_map/ppermute | solution.py:362
  117.7 2.9 %collective-permute-start.31 = (f32[256,256]{1,0:T(8,128)S(1)}, f32[256,256]{1,0:T(8,128)S(1)}, u32[]{:S(2)}, u32[]{:S(2)}) collective-permute-start(f32[256,256]{1,0:T(8,128)S(1)} %collective-permute-done.26.refs_2_.refs_16_), channel_id=1, source_target_pairs={{0,1},{1,0},{2,3},{3,2},{4,5},{5,4},{6,7},{7,6},{8,9},{9,8},{10,11... | collective-permute-start | bytes 786440 | tf_op jit(solution)/shard_map/ppermute | solution.py:362
  117.7 2.9 %collective-permute-start.32 = (f32[256,128]{1,0:T(8,128)S(1)}, f32[256,128]{1,0:T(8,128)S(1)}, u32[]{:S(2)}, u32[]{:S(2)}) collective-permute-start(f32[256,128]{1,0:T(8,128)S(1)} %collective-permute-done.27.refs_3_.refs_18_), channel_id=1, source_target_pairs={{0,1},{1,0},{2,3},{3,2},{4,5},{5,4},{6,7},{7,6},{8,9},{9,8},{10,11... | collective-permute-start | bytes 393224 | tf_op jit(solution)/shard_map/ppermute | solution.py:362

commit v5 on v4

--- a/solution.py
+++ b/solution.py
@@ -475,7 +475,7 @@
         [*far_covs, beyond],
     )
     back, ahead, across = (along_z(value, step) for value, step in zip(messages, (-1, 1, 2)))
-    after_gain = back_x(gate(next_gain, far_covs[0], far_covs[1], far_covs[2]), 1)
+    after_gain = back_x(gate(next_gain, far_covs[0], far_covs[1]), 1)
     b_hi, b_lo, x_hi, x_lo, s_hi, s_lo = call(
         outer_kernel,
         "outer",

time: 128 us -> 127 us (level)
  waiting for transfers between devices: 54.3 us -> 48.7 us
  starting transfers between devices: 40.8 us -> 45.4 us
    ppermute x5, waiting for transfers between devices: 11 us -> 5.46 us  [back_x(): lax.ppermute(value, 'tm', [(4 * x + y, 4 * ((x - step) % 4) + y) for x in...]
    ppermute x5, starting transfers between devices: 4.03 us -> 7.81 us  [back_x(): lax.ppermute(value, 'tm', [(4 * x + y, 4 * ((x - step) % 4) + y) for x in...]
  transfers between devices with their start and end apart: 33 -> 33, of which waited for: 20 -> 18; matrix products, arithmetic and copies ran while one was open for 0% -> 0% of each run, Pallas kernels for 14% -> 14%
where the time goes in v5:
time: 127 us
  waiting for transfers between devices  48.7 us (38%)
  starting transfers between devices  45.4 us (36%)
  Pallas kernels  30.2 us (24%)
  local copies, waits for them, and re-layouts  1.73 us (1%)
    pallas_call x14, Pallas kernels, call(): pl.pallas_call(kernel, out_shape=outs, in_specs=[ANY if index in outside...  30.2 us
    ppermute x5, waiting for transfers between devices, paired_z(): lax.ppermute(value, 'panel', [(2 * z + c, 2 * ((z + step * (1 - 2 * c)) %...  20.8 us
    ppermute x15, starting transfers between devices, other_core(): lax.ppermute(value, 'panel', [(2 * z + c, 2 * z + 1 - c) for z in range(4...  13.5 us
    ppermute x5, starting transfers between devices, paired_z(): lax.ppermute(value, 'panel', [(2 * z + c, 2 * ((z + step * (1 - 2 * c)) %...  13.1 us
    ppermute x3, waiting for transfers between devices, along_z(): lax.ppermute(value, 'panel', [(2 * z + c, 2 * ((z + step) % 4) + c) for z...  9.55 us
    ppermute x3, waiting for transfers between devices, along_y(): lax.ppermute(value, 'tm', [(4 * x + y, 4 * x + (y + step) % 4) for x in r...  7.85 us
    ppermute x5, starting transfers between devices, back_x(): lax.ppermute(value, 'tm', [(4 * x + y, 4 * ((x - step) % 4) + y) for x in...  7.81 us
    ppermute x2, starting transfers between devices, paired_y(): return lax.ppermute(value, ('tm', 'panel'), pairs)  5.54 us
  transfers between devices with their start and end apart: 33, of which 18 were waited for; matrix products, arithmetic and copies ran while one was open for 0% of the time, Pallas kernels for 14%

profile of v5, /device:TPU:1, one launch (start us, length us, event | category | flops | bytes accessed | tf_op | source)
XLA Modules:
  0.0 126.8 jit_solution(6055304678033817655)
XLA Ops:
  0.6 4.7 %collective-permute-start = (f32[256,512]{1,0:T(8,128)}, f32[256,512]{1,0:T(8,128)S(1)}, u32[]{:S(2)}, u32[]{:S(2)}) collective-permute-start(f32[256,512]{1,0:T(8,128)} %bitcast.3), channel_id=1, source_target_pairs={{0,2},{1,7},{2,4},{3,1},{4,6},{5,3},{6,0},{7,5},{8,10},{9,15},{10,... | collective-permute-start | bytes 1572872 | tf_op jit(solution)/shard_map/ppermute | solution.py:380
  5.3 1.0 copy-done
  6.3 0.7 copy-done.2
  7.0 0.1 pack.1.refs_0_
  7.1 0.1 collective-permute-start.3
  7.2 0.4 collective-permute-start.1
  7.7 6.5 %collective-permute-done.refs_1_ = f32[256,512]{1,0:T(8,128)S(1)} collective-permute-done((f32[256,512]{1,0:T(8,128)}, f32[256,512]{1,0:T(8,128)S(1)}, u32[]{:S(2)}, u32[]{:S(2)}) %collective-permute-start) | collective-permute-done | bytes 524320 | tf_op jit(solution)/shard_map/ppermute | solution.py:380
  14.1 3.3 %collective-permute-start.2 = (f32[256,512]{1,0:T(8,128)S(1)}, f32[256,512]{1,0:T(8,128)S(1)}, u32[]{:S(2)}, u32[]{:S(2)}) collective-permute-start(f32[256,512]{1,0:T(8,128)S(1)} %collective-permute-done.refs_1_), channel_id=1, source_target_pairs={{0,2},{1,7},{2,4},{3,1},{4,6},{5,3},{6,0},{7,5},{8,10},{9,15},{10,... | collective-permute-start | bytes 1572872 | tf_op jit(solution)/shard_map/ppermute | solution.py:380
  17.5 0.0 collective-permute-start.4
  17.5 0.5 collective-permute-start.5
  18.0 0.6 collective-permute-done.1.refs_1_.refs_2_
  18.6 0.1 pair.1.refs_1_.refs_0_
  18.6 0.0 copy-start.1
  18.7 4.9 %collective-permute-done.2.refs_0_ = f32[256,512]{1,0:T(8,128)S(1)} collective-permute-done((f32[256,512]{1,0:T(8,128)S(1)}, f32[256,512]{1,0:T(8,128)S(1)}, u32[]{:S(2)}, u32[]{:S(2)}) %collective-permute-start.2) | collective-permute-done | bytes 524320 | tf_op jit(solution)/shard_map/ppermute | solution.py:380
  23.6 3.0 %collective-permute-start.7 = (f32[256,512]{1,0:T(8,128)S(1)}, f32[256,512]{1,0:T(8,128)S(1)}, u32[]{:S(2)}, u32[]{:S(2)}) collective-permute-start(f32[256,512]{1,0:T(8,128)S(1)} %gate.9.refs_3_), channel_id=1, source_target_pairs={{0,1},{1,0},{2,3},{3,2},{4,5},{5,4},{6,7},{7,6},{8,9},{9,8},{10,11... | collective-permute-start | bytes 1572872 | tf_op jit(solution)/shard_map/ppermute | solution.py:362
  26.6 1.7 %collective-permute-start.11 = (f32[528,512]{1,0:T(8,128)S(1)}, f32[528,512]{1,0:T(8,128)S(1)}, u32[]{:S(2)}, u32[]{:S(2)}) collective-permute-start(f32[528,512]{1,0:T(8,128)S(1)} %pair.1.refs_1_.refs_0_), channel_id=1, source_target_pairs={{0,2},{1,7},{2,4},{3,1},{4,6},{5,3},{6,0},{7,5},{8,10},{9,15},{10,... | collective-permute-start | bytes 3244040 | tf_op jit(solution)/shard_map/ppermute | solution.py:380
  28.4 3.3 %block.1 = (bf16[3,512,512]{2,1,0:T(8,128)(2,1)S(1)}, bf16[3,512,512]{2,1,0:T(8,128)(2,1)S(1)}, bf16[512,512]{1,0:T(8,128)(2,1)S(1)}, bf16[512,512]{1,0:T(8,128)...) custom-call(f32[256,512]{1,0:T(8,128)S(1)} %bitcast.6, ...), custom_call_target="tpu_custom_call" | custom-call | tf_op jit(solution)/shard_map/block/pallas_call | solution.py:42
  31.7 2.8 %collective-permute-start.8 = (f32[512,512]{1,0:T(8,128)S(1)}, f32[512,512]{1,0:T(8,128)S(1)}, u32[]{:S(2)}, u32[]{:S(2)}) collective-permute-start(f32[512,512]{1,0:T(8,128)S(1)} %get-tuple-element.42), channel_id=1, source_target_pairs={{0,8},{1,25},{2,10},{3,27},{4,12},{5,29},{6,14},{7,31},{8,16},{9,1... | collective-permute-start | bytes 3145736 | tf_op jit(solution)/shard_map/ppermute | solution.py:391
  34.5 6.4 %collective-permute-done.11.pair.refs_1_ = f32[528,512]{1,0:T(8,128)S(1)} collective-permute-done((f32[528,512]{1,0:T(8,128)S(1)}, f32[528,512]{1,0:T(8,128)S(1)}, u32[]{:S(2)}, u32[]{:S(2)}) %collective-permute-start.11) | collective-permute-done | bytes 1081376 | tf_op jit(solution)/shard_map/ppermute | solution.py:380
  41.0 3.0 %collective-permute-start.13 = (f32[264,512]{1,0:T(8,128)S(1)}, f32[264,512]{1,0:T(8,128)S(1)}, u32[]{:S(2)}, u32[]{:S(2)}) collective-permute-start(f32[264,512]{1,0:T(8,128)S(1)} %cut.3), channel_id=1, source_target_pairs={{0,2},{1,7},{2,4},{3,1},{4,6},{5,3},{6,0},{7,5},{8,10},{9,15},{10,... | collective-permute-start | bytes 1622024 | tf_op jit(solution)/shard_map/ppermute | solution.py:380
  44.0 2.3 %collective-permute-done.8.pair.near.refs_2_ = f32[512,512]{1,0:T(8,128)S(1)} collective-permute-done((f32[512,512]{1,0:T(8,128)S(1)}, f32[512,512]{1,0:T(8,128)S(1)}, u32[]{:S(2)}, u32[]{:S(2)}) %collective-permute-start.8) | collective-permute-done | bytes 1048608 | tf_op jit(solution)/shard_map/ppermute | solution.py:391
  46.2 1.6 %collective-permute-start.9 = (f32[512,512]{1,0:T(8,128)S(1)}, f32[512,512]{1,0:T(8,128)S(1)}, u32[]{:S(2)}, u32[]{:S(2)}) collective-permute-start(f32[512,512]{1,0:T(8,128)S(1)} %collective-permute-done.8.pair.near.refs_2_), channel_id=1, source_target_pairs={{0,1},{1,0},{2,3},{3,2},{4,5},{5,4},{6,7},{7,6},{8,9},{9,8},{10,11... | collective-permute-start | bytes 3145736 | tf_op jit(solution)/shard_map/ppermute | solution.py:362
  47.9 2.4 %collective-permute-done.13.refs_0_ = f32[264,512]{1,0:T(8,128)S(1)} collective-permute-done((f32[264,512]{1,0:T(8,128)S(1)}, f32[264,512]{1,0:T(8,128)S(1)}, u32[]{:S(2)}, u32[]{:S(2)}) %collective-permute-start.13) | collective-permute-done | bytes 540704 | tf_op jit(solution)/shard_map/ppermute | solution.py:380
  50.3 3.4 %collective-permute-start.14 = (f32[264,512]{1,0:T(8,128)S(1)}, f32[264,512]{1,0:T(8,128)S(1)}, u32[]{:S(2)}, u32[]{:S(2)}) collective-permute-start(f32[264,512]{1,0:T(8,128)S(1)} %gate.10.refs_3_), channel_id=1, source_target_pairs={{0,1},{1,0},{2,3},{3,2},{4,5},{5,4},{6,7},{7,6},{8,9},{9,8},{10,11... | collective-permute-start | bytes 1622024 | tf_op jit(solution)/shard_map/ppermute | solution.py:362
  53.7 2.7 %collective-permute-start.10 = (f32[256,512]{1,0:T(8,128)S(1)}, f32[256,512]{1,0:T(8,128)S(1)}, u32[]{:S(2)}, u32[]{:S(2)}) collective-permute-start(f32[256,512]{1,0:T(8,128)S(1)} %cut.2.refs_1_), channel_id=1, source_target_pairs={{0,8},{1,25},{2,10},{3,27},{4,12},{5,29},{6,14},{7,31},{8,16},{9,1... | collective-permute-start | bytes 1572872 | tf_op jit(solution)/shard_map/ppermute | solution.py:391
  56.4 6.0 %noise.1 = (f32[4,64,512]{2,1,0:T(8,128)S(1)}, f32[8,512]{1,0:T(8,128)S(1)}, f32[520,512]{1,0:T(8,128)S(1)}) custom-call(bf16[3,512,512]{2,1,0:T(8,128)(2,1)S(1)} %get-tuple-element.43.e_hi, bf16[3,512,512]{2,1,0:T(8,128)(2,1)S(1)} %get-tuple-element.44.e_lo, f32[528,512]{1,0:T(8,128)S(1)} %pair.1.refs_1_.refs_0_, ...), custom_call_target="tpu_custom_call" | custom-call | tf_op jit(solution)/shard_map/noise/pallas_call | solution.py:42
  62.4 2.2 %second.1.refs_1_.moved = f32[520,512]{1,0:T(8,128)S(1)} custom-call(f32[520,512]{1,0:T(8,128)S(1)} %get-tuple-element.45.cov, f32[512,512]{1,0:T(8,128)S(1)} %collective-permute-done.8.pair.near.refs_2_, f32[512,512]{1,0:T(8,128)S(1)} %collective-permute-done.9.other.refs_3_), custom_call_target="tpu_custom_call" | custom-call | tf_op jit(solution)/shard_map/second/pallas_call | solution.py:42
  64.6 0.1 collective-permute-start.15
  64.7 1.9 %collective-permute-done.15.refs_5_ = f32[256,512]{1,0:T(8,128)S(1)} collective-permute-done((f32[256,512]{1,0:T(8,128)S(1)}, f32[256,512]{1,0:T(8,128)S(1)}, u32[]{:S(2)}, u32[]{:S(2)}) %collective-permute-start.15) | collective-permute-done | bytes 524320 | tf_op jit(solution)/shard_map/ppermute | solution.py:362
  66.6 5.0 %prefix.1 = (f32[256,512]{1,0:T(8,128)S(1)}, f32[144,512]{1,0:T(8,128)S(1)}, f32[144,512]{1,0:T(8,128)S(1)}, f32[144,512]{1,0:T(8,128)S(1)}) custom-call(f32[520,512]{1,0:T(8,128)S(1)} %get-tuple-element.45.cov, f32[520,512]{1,0:T(8,128)S(1)} %second.1.refs_1_.moved, bf16[512,512]{1,0:T(8,128)(2,1)S(1)} %get-tuple-element.40.refs_0_, ...), custom_call_target="tpu_custom_call" | custom-call | tf_op jit(solution)/shard_map/prefix/pallas_call | solution.py:42
  71.5 2.5 %collective-permute-start.16 = (f32[256,512]{1,0:T(8,128)S(1)}, f32[256,512]{1,0:T(8,128)S(1)}, u32[]{:S(2)}, u32[]{:S(2)}) collective-permute-start(f32[256,512]{1,0:T(8,128)S(1)} %get-tuple-element.54), channel_id=1, source_target_pairs={{0,96},{8,104},{16,112},{24,120},{32,0},{40,8},{48,16},{56,24},{64... | collective-permute-start | bytes 1572872 | tf_op jit(solution)/shard_map/ppermute | solution.py:370
  74.1 0.1 collective-permute-start.17
  74.2 2.7 %collective-permute-start.18 = (f32[144,512]{1,0:T(8,128)S(1)}, f32[144,512]{1,0:T(8,128)S(1)}, u32[]{:S(2)}, u32[]{:S(2)}) collective-permute-start(f32[144,512]{1,0:T(8,128)S(1)} %get-tuple-element.56), channel_id=1, source_target_pairs={{0,16},{8,24},{16,0},{24,8},{32,48},{40,56},{48,32},{56,40},{64,80... | collective-permute-start | bytes 884744 | tf_op jit(solution)/shard_map/ppermute | solution.py:365
  76.9 1.1 collective-permute-start.19
  77.9 2.7 %tail.1 = (bf16[512,512]{1,0:T(8,128)(2,1)S(1)}, bf16[512,512]{1,0:T(8,128)(2,1)S(1)}) custom-call(bf16[512,512]{1,0:T(8,128)(2,1)S(1)} %get-tuple-element.40.refs_0_, bf16[512,512]{1,0:T(8,128)(2,1)S(1)} %get-tuple-element.41.refs_1_, f32[512,512]{1,0:T(8,128)S(1)} %collective-permute-done.8.pair.near.refs_2_, ...), custom_call_target="tpu_custom_call" | custom-call | tf_op jit(solution)/shard_map/tail/pallas_call | solution.py:42
  80.6 3.0 %collective-permute-done.17.third = f32[144,512]{1,0:T(8,128)S(1)} collective-permute-done((f32[144,512]{1,0:T(8,128)S(1)}, f32[144,512]{1,0:T(8,128)S(1)}, u32[]{:S(2)}, u32[]{:S(2)}) %collective-permute-start.17) | collective-permute-done | bytes 294944 | tf_op jit(solution)/shard_map/ppermute | solution.py:365
  83.6 1.6 %collective-permute-done.16.refs_1_.refs_0_ = f32[256,512]{1,0:T(8,128)S(1)} collective-permute-done((f32[256,512]{1,0:T(8,128)S(1)}, f32[256,512]{1,0:T(8,128)S(1)}, u32[]{:S(2)}, u32[]{:S(2)}) %collective-permute-start.16) | collective-permute-done | bytes 524320 | tf_op jit(solution)/shard_map/ppermute | solution.py:370
  85.3 4.3 %collective-permute-done.18.second = f32[144,512]{1,0:T(8,128)S(1)} collective-permute-done((f32[144,512]{1,0:T(8,128)S(1)}, f32[144,512]{1,0:T(8,128)S(1)}, u32[]{:S(2)}, u32[]{:S(2)}) %collective-permute-start.18) | collective-permute-done | bytes 294944 | tf_op jit(solution)/shard_map/ppermute | solution.py:365
  89.6 0.5 collective-permute-done.19.first
  90.1 0.1 sum.1
  90.2 1.6 %collective-permute-start.20 = (f32[256,512]{1,0:T(8,128)S(1)}, f32[256,512]{1,0:T(8,128)S(1)}, u32[]{:S(2)}, u32[]{:S(2)}) collective-permute-start(f32[256,512]{1,0:T(8,128)S(1)} %gate.13.refs_8_.refs_0_), channel_id=1, source_target_pairs={{0,1},{1,0},{2,3},{3,2},{4,5},{5,4},{6,7},{7,6},{8,9},{9,8},{10,11... | collective-permute-start | bytes 1572872 | tf_op jit(solution)/shard_map/ppermute | solution.py:362
  91.8 0.6 collective-permute-start.21
  92.4 0.2 collective-permute-start.22
  92.6 0.7 collective-permute-start.24
  93.3 0.1 collective-permute-done.20.refs_9_
  93.4 1.9 %outer.1 = (bf16[2,512,512]{2,1,0:T(8,128)(2,1)S(1)}, bf16[2,512,512]{2,1,0:T(8,128)(2,1)S(1)}, bf16[2,256,512]{2,1,0:T(8,128)(2,1)S(1)}, bf16[2,256,512]{2,1,0:...) custom-call(bf16[512,512]{1,0:T(8,128)(2,1)S(1)} %get-tuple-element.46.refs_2_.p_hi, ...), custom_call_target="tpu_custom_call" | custom-call | tf_op jit(solution)/shard_map/outer/pallas_call | solution.py:42
  95.3 2.0 %collective-permute-done.21.refs_1_.first.refs_8_ = f32[72,512]{1,0:T(8,128)S(1)} collective-permute-done((f32[72,512]{1,0:T(8,128)S(1)}, f32[72,512]{1,0:T(8,128)S(1)}, u32[]{:S(2)}, u32[]{:S(2)}) %collective-permute-start.21) | collective-permute-done | bytes 147488 | tf_op jit(solution)/shard_map/ppermute | solution.py:370
  97.2 1.8 %collective-permute-done.22.refs_2_.second.refs_9_ = f32[72,512]{1,0:T(8,128)S(1)} collective-permute-done((f32[72,512]{1,0:T(8,128)S(1)}, f32[72,512]{1,0:T(8,128)S(1)}, u32[]{:S(2)}, u32[]{:S(2)}) %collective-permute-start.22) | collective-permute-done | bytes 147488 | tf_op jit(solution)/shard_map/ppermute | solution.py:370
  99.0 3.8 %collective-permute-start.23 = (f32[256,512]{1,0:T(8,128)S(1)}, f32[256,512]{1,0:T(8,128)S(1)}, u32[]{:S(2)}, u32[]{:S(2)}) collective-permute-start(f32[256,512]{1,0:T(8,128)S(1)} %gate.14), channel_id=1, source_target_pairs={{0,96},{8,104},{16,112},{24,120},{32,0},{40,8},{48,16},{56,24},{64... | collective-permute-start | bytes 1572872 | tf_op jit(solution)/shard_map/ppermute | solution.py:370
  102.8 0.0 collective-permute-done.24.third.refs_10_
  102.8 0.1 blocks.1
  103.0 0.1 collective-permute-start.25
  103.1 1.5 %collective-permute-start.26 = (f32[256,256]{1,0:T(8,128)S(1)}, f32[256,256]{1,0:T(8,128)S(1)}, u32[]{:S(2)}, u32[]{:S(2)}) collective-permute-start(f32[256,256]{1,0:T(8,128)S(1)} %get-tuple-element.65), channel_id=1, source_target_pairs={{0,2},{1,3},{2,4},{3,5},{4,6},{5,7},{6,0},{7,1},{8,10},{9,11},{10,... | collective-permute-start | bytes 786440 | tf_op jit(solution)/shard_map/ppermute | solution.py:375
  104.5 7.2 %collective-permute-done.27.refs_3_.refs_18_ = f32[256,128]{1,0:T(8,128)S(1)} collective-permute-done((f32[256,128]{1,0:T(8,128)S(1)}, f32[256,128]{1,0:T(8,128)S(1)}, u32[]{:S(2)}, u32[]{:S(2)}) %collective-permute-start.27) | collective-permute-done | bytes 131104 | tf_op jit(solution)/shard_map/ppermute | solution.py:375
  111.7 2.3 %collective-permute-done.26.refs_2_.refs_16_ = f32[256,256]{1,0:T(8,128)S(1)} collective-permute-done((f32[256,256]{1,0:T(8,128)S(1)}, f32[256,256]{1,0:T(8,128)S(1)}, u32[]{:S(2)}, u32[]{:S(2)}) %collective-permute-start.26) | collective-permute-done | bytes 262176 | tf_op jit(solution)/shard_map/ppermute | solution.py:375
  114.1 2.1 %collective-permute-start.28 = (f32[256,512]{1,0:T(8,128)S(1)}, f32[256,512]{1,0:T(8,128)S(1)}, u32[]{:S(2)}, u32[]{:S(2)}) collective-permute-start(f32[256,512]{1,0:T(8,128)S(1)} %gate.15.mine), channel_id=1, source_target_pairs={{0,1},{1,0},{2,3},{3,2},{4,5},{5,4},{6,7},{7,6},{8,9},{9,8},{10,11... | collective-permute-start | bytes 1572872 | tf_op jit(solution)/shard_map/ppermute | solution.py:362
  116.2 0.1 collective-permute-start.29
  116.3 0.4 collective-permute-start.30
  116.7 0.1 collective-permute-start.31
  116.8 0.4 collective-permute-start.32
  117.2 0.5 collective-permute-done.28.other
  117.7 1.5 %outermost.1 = (bf16[512,512]{1,0:T(8,128)(2,1)S(1)}, bf16[512,512]{1,0:T(8,128)(2,1)S(1)}, bf16[256,512]{1,0:T(8,128)(2,1)S(1)}, bf16[256,512]{1,0:T(8,128)(2,1)S(1)}) custom-call(bf16[2,512,512]{2,1,0:T(8,128)(2,1)S(1)} %get-tuple-element.59.b_hi, bf16[2,512,512]{2,1,0:T(8,128)(2,1)S(1)} %get-tuple-element.60.b_lo, ...), custom_call_target="tpu_custom_call" | custom-call | tf_op jit(solution)/shard_map/outermost/pallas_call | solution.py:42
  119.3 0.3 collective-permute-done.32.refs_19_
  119.6 7.2 %final.1 = (f32[4,64,512]{2,1,0:T(8,128)}, f32[4,64]{1,0:T(4,128)}) custom-call(bf16[2,512,512]{2,1,0:T(8,128)(2,1)S(1)} %get-tuple-element.59.b_hi, bf16[2,512,512]{2,1,0:T(8,128)(2,1)S(1)} %get-tuple-element.60.b_lo, bf16[2,256,512]{2,1,0:T(8,128)(2,1)S(1)} %get-tuple-element.61.x_hi, bf16[2,256,512]{2,1,0:T(8,128)(2,1)S(1)} %get-tuple-element.62.x_lo, ...), custom_call_target="tpu_custom_call" | custom-call | tf_op jit(solution)/shard_map/final/pallas_call | solution.py:42
  (30 shorter events, 0.1 us)
Async XLA Ops:
  0.6 13.5 %collective-permute-start = (f32[256,512]{1,0:T(8,128)}, f32[256,512]{1,0:T(8,128)S(1)}, u32[]{:S(2)}, u32[]{:S(2)}) collective-permute-start(f32[256,512]{1,0:T(8,128)} %bitcast.3), channel_id=1, source_target_pairs={{0,2},{1,7},{2,4},{3,1},{4,6},{5,3},{6,0},{7,5},{8,10},{9,15},{10,... | collective-permute-start | bytes 1572872 | tf_op jit(solution)/shard_map/ppermute | solution.py:380
  5.3 1.0 copy-start
  6.3 0.7 copy-start.2
  7.1 11.4 %collective-permute-start.3 = (f32[264,512]{1,0:T(8,128)S(1)}, f32[264,512]{1,0:T(8,128)S(1)}, u32[]{:S(2)}, u32[]{:S(2)}) collective-permute-start(f32[264,512]{1,0:T(8,128)S(1)} %pack.1.refs_0_), channel_id=1, source_target_pairs={{0,1},{1,0},{2,3},{3,2},{4,5},{5,4},{6,7},{7,6},{8,9},{9,8},{10,11... | collective-permute-start | bytes 1622024 | tf_op jit(solution)/shard_map/ppermute | solution.py:362
  7.2 11.3 %collective-permute-start.1 = (f32[256,512]{1,0:T(8,128)}, f32[256,512]{1,0:T(8,128)S(1)}, u32[]{:S(2)}, u32[]{:S(2)}) collective-permute-start(f32[256,512]{1,0:T(8,128)} %bitcast.4), channel_id=1, source_target_pairs={{0,6},{1,3},{2,0},{3,5},{4,2},{5,7},{6,4},{7,1},{8,14},{9,11},{10,... | collective-permute-start | bytes 1572872 | tf_op jit(solution)/shard_map/ppermute | solution.py:380
  14.1 9.4 %collective-permute-start.2 = (f32[256,512]{1,0:T(8,128)S(1)}, f32[256,512]{1,0:T(8,128)S(1)}, u32[]{:S(2)}, u32[]{:S(2)}) collective-permute-start(f32[256,512]{1,0:T(8,128)S(1)} %collective-permute-done.refs_1_), channel_id=1, source_target_pairs={{0,2},{1,7},{2,4},{3,1},{4,6},{5,3},{6,0},{7,5},{8,10},{9,15},{10,... | collective-permute-start | bytes 1572872 | tf_op jit(solution)/shard_map/ppermute | solution.py:380
  17.5 10.9 %collective-permute-start.4 = (f32[256,512]{1,0:T(8,128)}, f32[256,512]{1,0:T(8,128)S(1)}, u32[]{:S(2)}, u32[]{:S(2)}) collective-permute-start(f32[256,512]{1,0:T(8,128)} %bitcast.5), channel_id=1, source_target_pairs={{0,1},{1,0},{2,3},{3,2},{4,5},{5,4},{6,7},{7,6},{8,9},{9,8},{10,11... | collective-permute-start | bytes 1572872 | tf_op jit(solution)/shard_map/ppermute | solution.py:362
  17.5 10.9 %collective-permute-start.5 = (f32[256,512]{1,0:T(8,128)S(1)}, f32[256,512]{1,0:T(8,128)S(1)}, u32[]{:S(2)}, u32[]{:S(2)}) collective-permute-start(f32[256,512]{1,0:T(8,128)S(1)} %collective-permute-done.refs_1_), channel_id=1, source_target_pairs={{0,1},{1,0},{2,3},{3,2},{4,5},{5,4},{6,7},{7,6},{8,9},{9,8},{10,11... | collective-permute-start | bytes 1572872 | tf_op jit(solution)/shard_map/ppermute | solution.py:362
  18.5 9.8 %collective-permute-start.6 = (f32[256,512]{1,0:T(8,128)S(1)}, f32[256,512]{1,0:T(8,128)S(1)}, u32[]{:S(2)}, u32[]{:S(2)}) collective-permute-start(f32[256,512]{1,0:T(8,128)S(1)} %collective-permute-done.1.refs_1_.refs_2_), channel_id=1, source_target_pairs={{0,1},{1,0},{2,3},{3,2},{4,5},{5,4},{6,7},{7,6},{8,9},{9,8},{10,11... | collective-permute-start | bytes 1572872 | tf_op jit(solution)/shard_map/ppermute | solution.py:362
  18.6 9.7 %copy-start.1 = (f32[4,64,512]{2,1,0:T(8,128)S(1)}, f32[4,64,512]{2,1,0:T(8,128)}, u32[]{:S(2)}) copy-start(f32[4,64,512]{2,1,0:T(8,128)} %param.3) | copy-start | bytes 1572868
  23.6 4.8 %collective-permute-start.7 = (f32[256,512]{1,0:T(8,128)S(1)}, f32[256,512]{1,0:T(8,128)S(1)}, u32[]{:S(2)}, u32[]{:S(2)}) collective-permute-start(f32[256,512]{1,0:T(8,128)S(1)} %gate.9.refs_3_), channel_id=1, source_target_pairs={{0,1},{1,0},{2,3},{3,2},{4,5},{5,4},{6,7},{7,6},{8,9},{9,8},{10,11... | collective-permute-start | bytes 1572872 | tf_op jit(solution)/shard_map/ppermute | solution.py:362
  26.6 14.3 %collective-permute-start.11 = (f32[528,512]{1,0:T(8,128)S(1)}, f32[528,512]{1,0:T(8,128)S(1)}, u32[]{:S(2)}, u32[]{:S(2)}) collective-permute-start(f32[528,512]{1,0:T(8,128)S(1)} %pair.1.refs_1_.refs_0_), channel_id=1, source_target_pairs={{0,2},{1,7},{2,4},{3,1},{4,6},{5,3},{6,0},{7,5},{8,10},{9,15},{10,... | collective-permute-start | bytes 3244040 | tf_op jit(solution)/shard_map/ppermute | solution.py:380
  31.7 14.5 %collective-permute-start.8 = (f32[512,512]{1,0:T(8,128)S(1)}, f32[512,512]{1,0:T(8,128)S(1)}, u32[]{:S(2)}, u32[]{:S(2)}) collective-permute-start(f32[512,512]{1,0:T(8,128)S(1)} %get-tuple-element.42), channel_id=1, source_target_pairs={{0,8},{1,25},{2,10},{3,27},{4,12},{5,29},{6,14},{7,31},{8,16},{9,1... | collective-permute-start | bytes 3145736 | tf_op jit(solution)/shard_map/ppermute | solution.py:391
  41.0 9.3 %collective-permute-start.13 = (f32[264,512]{1,0:T(8,128)S(1)}, f32[264,512]{1,0:T(8,128)S(1)}, u32[]{:S(2)}, u32[]{:S(2)}) collective-permute-start(f32[264,512]{1,0:T(8,128)S(1)} %cut.3), channel_id=1, source_target_pairs={{0,2},{1,7},{2,4},{3,1},{4,6},{5,3},{6,0},{7,5},{8,10},{9,15},{10,... | collective-permute-start | bytes 1622024 | tf_op jit(solution)/shard_map/ppermute | solution.py:380
  44.0 12.4 %collective-permute-start.12 = (f32[528,512]{1,0:T(8,128)S(1)}, f32[528,512]{1,0:T(8,128)S(1)}, u32[]{:S(2)}, u32[]{:S(2)}) collective-permute-start(f32[528,512]{1,0:T(8,128)S(1)} %collective-permute-done.11.pair.refs_1_), channel_id=1, source_target_pairs={{0,1},{1,0},{2,3},{3,2},{4,5},{5,4},{6,7},{7,6},{8,9},{9,8},{10,11... | collective-permute-start | bytes 3244040 | tf_op jit(solution)/shard_map/ppermute | solution.py:362
  46.2 16.2 %collective-permute-start.9 = (f32[512,512]{1,0:T(8,128)S(1)}, f32[512,512]{1,0:T(8,128)S(1)}, u32[]{:S(2)}, u32[]{:S(2)}) collective-permute-start(f32[512,512]{1,0:T(8,128)S(1)} %collective-permute-done.8.pair.near.refs_2_), channel_id=1, source_target_pairs={{0,1},{1,0},{2,3},{3,2},{4,5},{5,4},{6,7},{7,6},{8,9},{9,8},{10,11... | collective-permute-start | bytes 3145736 | tf_op jit(solution)/shard_map/ppermute | solution.py:362
  50.3 6.1 %collective-permute-start.14 = (f32[264,512]{1,0:T(8,128)S(1)}, f32[264,512]{1,0:T(8,128)S(1)}, u32[]{:S(2)}, u32[]{:S(2)}) collective-permute-start(f32[264,512]{1,0:T(8,128)S(1)} %gate.10.refs_3_), channel_id=1, source_target_pairs={{0,1},{1,0},{2,3},{3,2},{4,5},{5,4},{6,7},{7,6},{8,9},{9,8},{10,11... | collective-permute-start | bytes 1622024 | tf_op jit(solution)/shard_map/ppermute | solution.py:362
  53.7 10.9 %collective-permute-start.10 = (f32[256,512]{1,0:T(8,128)S(1)}, f32[256,512]{1,0:T(8,128)S(1)}, u32[]{:S(2)}, u32[]{:S(2)}) collective-permute-start(f32[256,512]{1,0:T(8,128)S(1)} %cut.2.refs_1_), channel_id=1, source_target_pairs={{0,8},{1,25},{2,10},{3,27},{4,12},{5,29},{6,14},{7,31},{8,16},{9,1... | collective-permute-start | bytes 1572872 | tf_op jit(solution)/shard_map/ppermute | solution.py:391
  64.6 2.0 %collective-permute-start.15 = (f32[256,512]{1,0:T(8,128)S(1)}, f32[256,512]{1,0:T(8,128)S(1)}, u32[]{:S(2)}, u32[]{:S(2)}) collective-permute-start(f32[256,512]{1,0:T(8,128)S(1)} %gate.11.refs_4_), channel_id=1, source_target_pairs={{0,1},{1,0},{2,3},{3,2},{4,5},{5,4},{6,7},{7,6},{8,9},{9,8},{10,11... | collective-permute-start | bytes 1572872 | tf_op jit(solution)/shard_map/ppermute | solution.py:362
  71.5 13.7 %collective-permute-start.16 = (f32[256,512]{1,0:T(8,128)S(1)}, f32[256,512]{1,0:T(8,128)S(1)}, u32[]{:S(2)}, u32[]{:S(2)}) collective-permute-start(f32[256,512]{1,0:T(8,128)S(1)} %get-tuple-element.54), channel_id=1, source_target_pairs={{0,96},{8,104},{16,112},{24,120},{32,0},{40,8},{48,16},{56,24},{64... | collective-permute-start | bytes 1572872 | tf_op jit(solution)/shard_map/ppermute | solution.py:370
  74.1 9.5 %collective-permute-start.17 = (f32[144,512]{1,0:T(8,128)S(1)}, f32[144,512]{1,0:T(8,128)S(1)}, u32[]{:S(2)}, u32[]{:S(2)}) collective-permute-start(f32[144,512]{1,0:T(8,128)S(1)} %get-tuple-element.55.refs_0_), channel_id=1, source_target_pairs={{0,8},{8,16},{16,24},{24,0},{32,40},{40,48},{48,56},{56,32},{64,72... | collective-permute-start | bytes 884744 | tf_op jit(solution)/shard_map/ppermute | solution.py:365
  74.2 15.4 %collective-permute-start.18 = (f32[144,512]{1,0:T(8,128)S(1)}, f32[144,512]{1,0:T(8,128)S(1)}, u32[]{:S(2)}, u32[]{:S(2)}) collective-permute-start(f32[144,512]{1,0:T(8,128)S(1)} %get-tuple-element.56), channel_id=1, source_target_pairs={{0,16},{8,24},{16,0},{24,8},{32,48},{40,56},{48,32},{56,40},{64,80... | collective-permute-start | bytes 884744 | tf_op jit(solution)/shard_map/ppermute | solution.py:365
  76.9 13.3 %collective-permute-start.19 = (f32[144,512]{1,0:T(8,128)S(1)}, f32[144,512]{1,0:T(8,128)S(1)}, u32[]{:S(2)}, u32[]{:S(2)}) collective-permute-start(f32[144,512]{1,0:T(8,128)S(1)} %get-tuple-element.57), channel_id=1, source_target_pairs={{0,24},{8,0},{16,8},{24,16},{32,56},{40,32},{48,40},{56,48},{64,88... | collective-permute-start | bytes 884744 | tf_op jit(solution)/shard_map/ppermute | solution.py:365
  90.2 3.2 %collective-permute-start.20 = (f32[256,512]{1,0:T(8,128)S(1)}, f32[256,512]{1,0:T(8,128)S(1)}, u32[]{:S(2)}, u32[]{:S(2)}) collective-permute-start(f32[256,512]{1,0:T(8,128)S(1)} %gate.13.refs_8_.refs_0_), channel_id=1, source_target_pairs={{0,1},{1,0},{2,3},{3,2},{4,5},{5,4},{6,7},{7,6},{8,9},{9,8},{10,11... | collective-permute-start | bytes 1572872 | tf_op jit(solution)/shard_map/ppermute | solution.py:362
  91.8 5.4 %collective-permute-start.21 = (f32[72,512]{1,0:T(8,128)S(1)}, f32[72,512]{1,0:T(8,128)S(1)}, u32[]{:S(2)}, u32[]{:S(2)}) collective-permute-start(f32[72,512]{1,0:T(8,128)S(1)} %get-tuple-element.58.refs_1_), channel_id=1, source_target_pairs={{0,96},{8,104},{16,112},{24,120},{32,0},{40,8},{48,16},{56,24},{64... | collective-permute-start | bytes 442376 | tf_op jit(solution)/shard_map/ppermute | solution.py:370
  92.4 6.6 %collective-permute-start.22 = (f32[72,512]{1,0:T(8,128)S(1)}, f32[72,512]{1,0:T(8,128)S(1)}, u32[]{:S(2)}, u32[]{:S(2)}) collective-permute-start(f32[72,512]{1,0:T(8,128)S(1)} %get-tuple-element.58.refs_1_), channel_id=1, source_target_pairs={{0,64},{8,72},{16,80},{24,88},{32,96},{40,104},{48,112},{56,120},{... | collective-permute-start | bytes 442376 | tf_op jit(solution)/shard_map/ppermute | solution.py:370
  92.6 10.2 %collective-permute-start.24 = (f32[72,512]{1,0:T(8,128)S(1)}, f32[72,512]{1,0:T(8,128)S(1)}, u32[]{:S(2)}, u32[]{:S(2)}) collective-permute-start(f32[72,512]{1,0:T(8,128)S(1)} %get-tuple-element.58.refs_1_), channel_id=1, source_target_pairs={{0,32},{8,40},{16,48},{24,56},{32,64},{40,72},{48,80},{56,88},{64,... | collective-permute-start | bytes 442376 | tf_op jit(solution)/shard_map/ppermute | solution.py:370
  99.0 15.1 %collective-permute-start.23 = (f32[256,512]{1,0:T(8,128)S(1)}, f32[256,512]{1,0:T(8,128)S(1)}, u32[]{:S(2)}, u32[]{:S(2)}) collective-permute-start(f32[256,512]{1,0:T(8,128)S(1)} %gate.14), channel_id=1, source_target_pairs={{0,96},{8,104},{16,112},{24,120},{32,0},{40,8},{48,16},{56,24},{64... | collective-permute-start | bytes 1572872 | tf_op jit(solution)/shard_map/ppermute | solution.py:370
  103.0 11.1 %collective-permute-start.25 = (f32[256,384]{1,0:T(8,128)S(1)}, f32[256,384]{1,0:T(8,128)S(1)}, u32[]{:S(2)}, u32[]{:S(2)}) collective-permute-start(f32[256,384]{1,0:T(8,128)S(1)} %get-tuple-element.64), channel_id=1, source_target_pairs={{0,6},{1,7},{2,0},{3,1},{4,2},{5,3},{6,4},{7,5},{8,14},{9,15},{10,... | collective-permute-start | bytes 1179656 | tf_op jit(solution)/shard_map/ppermute | solution.py:375
  103.1 11.0 %collective-permute-start.26 = (f32[256,256]{1,0:T(8,128)S(1)}, f32[256,256]{1,0:T(8,128)S(1)}, u32[]{:S(2)}, u32[]{:S(2)}) collective-permute-start(f32[256,256]{1,0:T(8,128)S(1)} %get-tuple-element.65), channel_id=1, source_target_pairs={{0,2},{1,3},{2,4},{3,5},{4,6},{5,7},{6,0},{7,1},{8,10},{9,11},{10,... | collective-permute-start | bytes 786440 | tf_op jit(solution)/shard_map/ppermute | solution.py:375
  104.5 7.2 %collective-permute-start.27 = (f32[256,128]{1,0:T(8,128)S(1)}, f32[256,128]{1,0:T(8,128)S(1)}, u32[]{:S(2)}, u32[]{:S(2)}) collective-permute-start(f32[256,128]{1,0:T(8,128)S(1)} %get-tuple-element.66), channel_id=1, source_target_pairs={{0,4},{1,5},{2,6},{3,7},{4,0},{5,1},{6,2},{7,3},{8,12},{9,13},{10,... | collective-permute-start | bytes 393224 | tf_op jit(solution)/shard_map/ppermute | solution.py:375
  114.1 3.6 %collective-permute-start.28 = (f32[256,512]{1,0:T(8,128)S(1)}, f32[256,512]{1,0:T(8,128)S(1)}, u32[]{:S(2)}, u32[]{:S(2)}) collective-permute-start(f32[256,512]{1,0:T(8,128)S(1)} %gate.15.mine), channel_id=1, source_target_pairs={{0,1},{1,0},{2,3},{3,2},{4,5},{5,4},{6,7},{7,6},{8,9},{9,8},{10,11... | collective-permute-start | bytes 1572872 | tf_op jit(solution)/shard_map/ppermute | solution.py:362
  116.2 3.4 %collective-permute-start.29 = (f32[256,512]{1,0:T(8,128)S(1)}, f32[256,512]{1,0:T(8,128)S(1)}, u32[]{:S(2)}, u32[]{:S(2)}) collective-permute-start(f32[256,512]{1,0:T(8,128)S(1)} %get-tuple-element.75.refs_12_), channel_id=1, source_target_pairs={{0,1},{1,0},{2,3},{3,2},{4,5},{5,4},{6,7},{7,6},{8,9},{9,8},{10,11... | collective-permute-start | bytes 1572872 | tf_op jit(solution)/shard_map/ppermute | solution.py:362
  116.3 3.3 %collective-permute-start.30 = (f32[256,384]{1,0:T(8,128)S(1)}, f32[256,384]{1,0:T(8,128)S(1)}, u32[]{:S(2)}, u32[]{:S(2)}) collective-permute-start(f32[256,384]{1,0:T(8,128)S(1)} %collective-permute-done.25.refs_1_.refs_14_), channel_id=1, source_target_pairs={{0,1},{1,0},{2,3},{3,2},{4,5},{5,4},{6,7},{7,6},{8,9},{9,8},{10,11... | collective-permute-start | bytes 1179656 | tf_op jit(solution)/shard_map/ppermute | solution.py:362
  116.7 2.9 %collective-permute-start.31 = (f32[256,256]{1,0:T(8,128)S(1)}, f32[256,256]{1,0:T(8,128)S(1)}, u32[]{:S(2)}, u32[]{:S(2)}) collective-permute-start(f32[256,256]{1,0:T(8,128)S(1)} %collective-permute-done.26.refs_2_.refs_16_), channel_id=1, source_target_pairs={{0,1},{1,0},{2,3},{3,2},{4,5},{5,4},{6,7},{7,6},{8,9},{9,8},{10,11... | collective-permute-start | bytes 786440 | tf_op jit(solution)/shard_map/ppermute | solution.py:362
  116.8 2.8 %collective-permute-start.32 = (f32[256,128]{1,0:T(8,128)S(1)}, f32[256,128]{1,0:T(8,128)S(1)}, u32[]{:S(2)}, u32[]{:S(2)}) collective-permute-start(f32[256,128]{1,0:T(8,128)S(1)} %collective-permute-done.27.refs_3_.refs_18_), channel_id=1, source_target_pairs={{0,1},{1,0},{2,3},{3,2},{4,5},{5,4},{6,7},{7,6},{8,9},{9,8},{10,11... | collective-permute-start | bytes 393224 | tf_op jit(solution)/shard_map/ppermute | solution.py:362
